TPU v7x, 512 devices: a whole 4x8x8 slice. The times are simulated.
512 devices in a mesh: clip: 16 (over y_hi, z), seq: 32 (over y_lo, x, core).
Axes of the slice: x: 4, y: 8 (y_hi: 2, y_lo: 4; y = y_hi * 4 + y_lo), z: 8, core: 2. Of those that a mesh axis runs over, the one named last changes fastest.
Arguments:
- video_query: bfloat16 [131072, 1536], P(('clip', 'seq')), may hold values from -7 to 7
- audio_key: bfloat16 [65536, 1536], P(('clip', 'seq')), may hold values from -7 to 7
- audio_value: bfloat16 [65536, 1536], P(('clip', 'seq')), may hold values from -6 to 6
- null_kv: bfloat16 [2, 1536], replicated, may hold values from -4 to 4
- audio_keep: int32 [65536], P('clip'), may hold values 0 or 1
- clip_lengths: int32 [16, 4], P('clip'), may hold values from 1 to 2048, as said below
- out_grad: bfloat16 [131072, 1536], P(('clip', 'seq')), may hold values from -6 to 6
Outputs:
- attended: bfloat16 [131072, 1536], P(('clip', 'seq'))
- query_grad: bfloat16 [131072, 1536], P(('clip', 'seq'))
- key_grad: bfloat16 [65536, 1536], P(('clip', 'seq'))
- value_grad: bfloat16 [65536, 1536], P(('clip', 'seq'))
- null_grad: float32 [2, 1536], replicated
Inputs may be any that keep to these rules, and one draw needn't show every extreme that they name: `clip_lengths`: each row holds 3 clip lengths in packing order and then the padding at the group's end; a row sums to 4096, its largest entry is 2048, and the padding is 1 to 256 tokens.
All inputs are finite; a program needn't handle non-finite values. No bound on the sum of `audio_keep` on one device may be relied on, other than what follows from the above.
Results may differ from a plain program's by a relative error of at most 0.035.
Values may be sent and summed in bfloat16 or wider, within the bound.
No kernel may reach another device: no remote copies, remote signals or barrier semaphores. Data moves between devices by JAX's collectives and lax.ppermute only.
A program may use at most 64 MiB of HBM per device.

v0:
```python
import jax
import jax.numpy as jnp
from jax import lax
from jax.sharding import PartitionSpec as P

HEADS = 12
HEAD = 128


def padded(cells, sides, width):
    for axis, dim in sides:
        count = lax.axis_size(axis)
        ends = count - 1
        head = lax.slice_in_dim(cells, 0, width, axis=dim)
        tail = lax.slice_in_dim(cells, cells.shape[dim] - width, cells.shape[dim], axis=dim)
        cells = jnp.concatenate(
            [
                lax.ppermute(tail, axis, [(i, (i + 1) % count) for i in range(ends)]),
                cells,
                lax.ppermute(head, axis, [((i + 1) % count, i) for i in range(ends)]),
            ],
            axis=dim,
        )
    return cells


def shifted(block, axis, distance):
    devices = range(lax.axis_size(axis))
    route = [(i - distance, i) for i in devices if i - distance in devices]
    return lax.ppermute(block, axis, route)


def segment_of(positions, bounds):
    return jnp.sum((positions[:, None] >= bounds[None, :-1]).astype(jnp.int32), axis=1)


def allowed_pairs(query_pos, key_pos, bounds, keep_rows, total_audio, pad_segment, window):
    key_clip = jnp.clip(key_pos, 0, total_audio - 1)
    key_seg = segment_of(key_clip, bounds)
    query_seg = segment_of(jnp.clip(query_pos // 2, 0, total_audio - 1), bounds)
    key_inside = (
        (key_pos >= 0) & (key_pos < total_audio) & (keep_rows == 1) & (key_seg < pad_segment)
    )
    query_inside = (query_pos >= 0) & (query_pos < 2 * total_audio) & (query_seg < pad_segment)
    nearby = jnp.abs(query_pos[:, None] - 2 * key_pos[None, :]) <= 2 * window
    return (
        key_inside[None, :]
        & query_inside[:, None]
        & (key_seg[None, :] == query_seg[:, None])
        & nearby
    )


def score_block(queries, key_rows, null_key):
    row_count = queries.shape[0]
    factor = HEAD ** (-0.5)
    query_heads = queries.reshape(row_count, HEADS, HEAD)
    key_heads = key_rows.reshape(key_rows.shape[0], HEADS, HEAD)
    scores = (
        jnp.einsum("ihd,jhd->hij", query_heads, key_heads, preferred_element_type=jnp.float32)
        * factor
    )
    null_score = (
        jnp.einsum(
            "ihd,hd->hi",
            query_heads,
            null_key.reshape(HEADS, HEAD),
            preferred_element_type=jnp.float32,
        )
        * factor
    )
    return (scores, null_score)


def forward_block(queries, key_rows, value_rows, allowed, row_valid, null_kv):
    row_count = queries.shape[0]
    scores, null_score = score_block(queries, key_rows, null_kv[0])
    masked = jnp.where(allowed[None], scores, -jnp.inf)
    row_top = jnp.maximum(jnp.max(masked, axis=2), null_score)
    exponent = jnp.where(allowed[None], jnp.exp(scores - row_top[:, :, None]), 0.0)
    null_exponent = jnp.exp(null_score - row_top)
    row_total = jnp.sum(exponent, axis=2) + null_exponent
    weights = (exponent / row_total[:, :, None]).astype(jnp.bfloat16)
    null_prob = (null_exponent / row_total).astype(jnp.bfloat16)
    value_heads = value_rows.reshape(value_rows.shape[0], HEADS, HEAD)
    mixed = jnp.einsum("hij,jhd->ihd", weights, value_heads, preferred_element_type=jnp.float32)
    null_value = null_kv[1].reshape(HEADS, HEAD).astype(jnp.float32)
    mixed = mixed + null_prob.astype(jnp.float32).T[:, :, None] * null_value[None]
    attended = (
        (mixed * row_valid[:, None, None]).reshape(row_count, HEADS * HEAD).astype(jnp.bfloat16)
    )
    return (attended, weights, null_prob, row_top, row_total)


def backward_block(queries, grad_rows, key_rows, value_rows, weights, null_prob, null_kv):
    row_count = queries.shape[0]
    factor = HEAD ** (-0.5)
    query_heads = queries.reshape(row_count, HEADS, HEAD)
    grad_heads = grad_rows.reshape(row_count, HEADS, HEAD)
    key_heads = key_rows.reshape(key_rows.shape[0], HEADS, HEAD)
    value_heads = value_rows.reshape(value_rows.shape[0], HEADS, HEAD)
    prob_grad = jnp.einsum(
        "ihd,jhd->hij", grad_heads, value_heads, preferred_element_type=jnp.float32
    )
    null_prob_grad = jnp.einsum(
        "ihd,hd->hi",
        grad_heads,
        null_kv[1].reshape(HEADS, HEAD),
        preferred_element_type=jnp.float32,
    )
    null_float = null_prob.astype(jnp.float32)
    row_delta = (
        jnp.sum(weights.astype(jnp.float32) * prob_grad, axis=2) + null_float * null_prob_grad
    )
    score_grad = (
        weights.astype(jnp.float32) * (prob_grad - row_delta[:, :, None]) * factor
    ).astype(jnp.bfloat16)
    null_score_grad = (null_float * (null_prob_grad - row_delta) * factor).astype(jnp.bfloat16)
    query_grad = jnp.einsum(
        "hij,jhd->ihd", score_grad, key_heads, preferred_element_type=jnp.float32
    )
    null_key = null_kv[0].reshape(HEADS, HEAD).astype(jnp.float32)
    query_grad = query_grad + null_score_grad.astype(jnp.float32).T[:, :, None] * null_key[None]
    query_grad = query_grad.reshape(row_count, HEADS * HEAD).astype(jnp.bfloat16)
    null_grad = jnp.stack(
        [
            jnp.einsum(
                "hi,ihd->hd", null_score_grad, query_heads, preferred_element_type=jnp.float32
            ),
            jnp.einsum("hi,ihd->hd", null_prob, grad_heads, preferred_element_type=jnp.float32),
        ]
    ).reshape(2, HEADS * HEAD)
    return (query_grad, score_grad, row_delta, null_grad)


def key_terms(score_grad, weights, queries, grad_rows):
    row_count = queries.shape[0]
    query_heads = queries.reshape(row_count, HEADS, HEAD)
    grad_heads = grad_rows.reshape(row_count, HEADS, HEAD)
    key_grad = jnp.einsum(
        "hij,ihd->jhd", score_grad, query_heads, preferred_element_type=jnp.float32
    )
    value_grad = jnp.einsum("hij,ihd->jhd", weights, grad_heads, preferred_element_type=jnp.float32)
    return (key_grad.reshape(-1, HEADS * HEAD), value_grad.reshape(-1, HEADS * HEAD))


def body(video_query, audio_key, audio_value, null_kv, audio_keep, clip_lengths, out_grad):
    audio_rows = audio_key.shape[0]
    video_rows = video_query.shape[0]
    shards = lax.axis_size("seq")
    seq_index = lax.axis_index("seq")
    total_audio = audio_rows * shards
    bounds = jnp.cumsum(clip_lengths[0])
    pad_segment = clip_lengths.shape[1] - 1
    query_pos = seq_index * video_rows + jnp.arange(video_rows, dtype=jnp.int32)
    key_pos = seq_index * audio_rows - audio_rows + jnp.arange(3 * audio_rows, dtype=jnp.int32)
    keep_padded = jnp.pad(audio_keep, (audio_rows, audio_rows))
    keep_rows = lax.dynamic_slice_in_dim(keep_padded, seq_index * audio_rows, 3 * audio_rows)
    allowed = allowed_pairs(
        query_pos, key_pos, bounds, keep_rows, total_audio, pad_segment, audio_rows
    )
    row_valid = (segment_of(query_pos // 2, bounds) < pad_segment).astype(jnp.float32)
    stacked = jnp.stack([audio_key, audio_value])
    key_rims = padded(stacked, (("seq", 1),), audio_rows)
    rim_keys = key_rims[0]
    rim_values = key_rims[1]
    attended, weights, null_prob, row_top, row_total = forward_block(
        video_query, rim_keys, rim_values, allowed, row_valid, null_kv
    )
    grad_rows = out_grad * row_valid[:, None].astype(jnp.bfloat16)
    query_grad, score_grad, row_delta, null_part = backward_block(
        video_query, grad_rows, rim_keys, rim_values, weights, null_prob, null_kv
    )
    key_all, value_all = key_terms(score_grad, weights, video_query, grad_rows)
    backs = jnp.stack([key_all, value_all])
    from_lower = shifted(backs[:, 2 * audio_rows :], "seq", 1)
    from_upper = shifted(backs[:, :audio_rows], "seq", -1)
    summed = backs[:, audio_rows : 2 * audio_rows] + from_lower + from_upper
    key_grad = summed[0]
    value_grad = summed[1]
    null_grad = lax.psum(null_part, ("clip", "seq"))
    return (
        attended,
        query_grad,
        key_grad.astype(jnp.bfloat16),
        value_grad.astype(jnp.bfloat16),
        null_grad,
    )


def solution(mesh):
    placed = (
        P(("clip", "seq"), None),
        P(("clip", "seq"), None),
        P(("clip", "seq"), None),
        P(),
        P("clip"),
        P("clip", None),
        P(("clip", "seq"), None),
    )
    return jax.shard_map(
        body,
        mesh=mesh,
        in_specs=placed,
        out_specs=(
            P(("clip", "seq"), None),
            P(("clip", "seq"), None),
            P(("clip", "seq"), None),
            P(("clip", "seq"), None),
            P(),
        ),
        check_vma=False,
    )
```

profile of v0, /device:TPU:1, one launch (start us, length us, event | category | flops | bytes accessed | tf_op | source)
XLA Modules:
  0.0 170.0 jit_solution(7044517727369723659)
XLA Ops:
  0.6 0.0 copy-start.10
  0.7 1.3 copy.48
  2.0 0.0 copy-start.9
  2.0 1.2 copy.47
  3.2 1.0 pad_maximum_fusion.2
  4.1 8.8 %collective-permute-start.1 = (bf16[2,128,1536]{1,2,0:T(8,128)(2,1)}, bf16[2,128,1536]{1,2,0:T(8,128)(2,1)S(1)}, u32[]{:S(2)}, u32[]{:S(2)}) collective-permute-start(bf16[2,128,1536]{1,2,0:T(8,128)(2,1)} %pad_maximum_fusion.2), channel_id=1, source_target_pairs={{1,0},{2,1},{3,2},{4,3},{5,4},{6,5},{7,6},{8,7},{9,8},{10,9},{11,1... | collective-permute-start | bytes 2359304 | tf_op jit(solution)/shard_map/ppermute | solution.py:20
  12.9 1.9 %collective-permute-start = (bf16[2,128,1536]{1,2,0:T(8,128)(2,1)}, bf16[2,128,1536]{1,2,0:T(8,128)(2,1)}, u32[]{:S(2)}, u32[]{:S(2)}) collective-permute-start(bf16[2,128,1536]{1,2,0:T(8,128)(2,1)} %pad_maximum_fusion.2), channel_id=1, source_target_pairs={{0,1},{1,2},{2,3},{3,4},{4,5},{5,6},{6,7},{7,8},{8,9},{9,10},{10,1... | collective-permute-start | bytes 2359304 | tf_op jit(solution)/shard_map/ppermute | solution.py:18
  14.9 0.2 reduce-window.4
  15.1 0.1 convert_reduce_fusion
  15.2 0.1 convert_reduce_fusion.1
  15.3 0.3 copy.49
  15.6 0.0 copy-done.8
  15.6 0.2 fusion.41
  15.8 0.1 fusion.52
  15.9 0.2 fusion.15
  16.2 1.4 copy.53
  17.6 0.1 broadcast_multiply_fusion
  17.7 0.2 fusion.39
  17.9 0.6 collective-permute-done.1
  18.5 5.6 %collective-permute-done = bf16[2,128,1536]{1,2,0:T(8,128)(2,1)} collective-permute-done((bf16[2,128,1536]{1,2,0:T(8,128)(2,1)}, bf16[2,128,1536]{1,2,0:T(8,128)(2,1)}, u32[]{:S(2)}, u32[]{:S(2)}) %collective-permute-start) | collective-permute-done | bytes 786464 | tf_op jit(solution)/shard_map/ppermute | solution.py:18
  24.1 1.4 pad_maximum_fusion
  25.5 0.2 fusion.55
  25.8 0.0 copy-start.2
  25.8 0.0 copy-start.5
  25.8 1.0 fusion.3
  26.8 0.0 copy-done.2
  26.8 1.0 fusion.6
  27.8 1.8 %fusion = (f32[12,256]{1,0:T(8,128)S(1)}, bf16[12,256,384]{1,2,0:T(8,128)(2,1)S(1)}, f32[12,256,384]{1,2,0:T(8,128)S(1)}) fusion(f32[12,256]{1,0:T(8,128)S(1)} %fusion.38, f32[12,256]{1,0:T(8,128)S(1)} %fusion.28, f32[12,384,256]{2,1,0:T(8,128)S(1)} %get-tuple-element.39, pred[256,384]{0,1:T(8,128)(4,1)S(1)} %fusion.15, ...), kind=kOutput, calls=%fused_computation.6 | convolution fusion | flops 311424000 | bytes 13897728 | tf_op jit(solution)/shard_map/ihd,jhd->hij/dot_general | solution.py:102
  29.6 0.0 copy-start.3
  29.7 2.2 %fusion.57 = f32[12,128,384]{2,1,0:T(8,128)} fusion(bf16[256,12,128]{0,2,1:T(8,128)(2,1)S(1)} %bitcast.184, bf16[12,256,384]{1,2,0:T(8,128)(2,1)S(1)} %get-tuple-element.29), kind=kOutput, calls=%fused_computation.105 | convolution fusion | flops 301989888 | bytes 5505024 | tf_op jit(solution)/shard_map/hij,ihd->jhd/dot_general | solution.py:143
  32.0 0.8 fusion.2
  32.8 2.2 %fusion.56 = f32[12,384,128]{1,2,0:T(8,128)} fusion(bf16[12,256,384]{1,2,0:T(8,128)(2,1)S(1)} %fusion.2, bf16[256,12,128]{0,2,1:T(8,128)(2,1)S(1)} %bitcast.180), kind=kOutput, calls=%fused_computation.104 | convolution fusion | flops 301989888 | bytes 5505024 | tf_op jit(solution)/shard_map/hij,ihd->jhd/dot_general | solution.py:140
  35.0 2.0 %copy.61 = f32[1,384,1536]{2,1,0:T(8,128)S(1)} copy(f32[1,384,1536]{1,2,0:T(8,128)} %bitcast.189) | data formatting | bytes 4718592 | tf_op jit(solution)/shard_map/stack;reshape | solution.py:175
  37.1 3.1 %copy.62 = f32[1,384,1536]{2,1,0:T(8,128)} copy(f32[1,384,1536]{1,2,0:T(8,128)} %bitcast.188) | data formatting | bytes 4718592 | tf_op jit(solution)/shard_map/stack;reshape | solution.py:175
  40.2 3.5 %fusion.7 = (f32[2,128,1536]{2,1,0:T(8,128)}, f32[2,128,1536]{2,1,0:T(8,128)}) fusion(f32[1,384,1536]{2,1,0:T(8,128)S(1)} %copy.61, f32[1,384,1536]{2,1,0:T(8,128)} %copy.62), kind=kLoop, calls=%fused_computation.17 | loop fusion | flops 786432 | bytes 7864320 | tf_op jit(solution)/shard_map/stack | solution.py:175
  43.7 1.9 %collective-permute-start.3 = (f32[2,128,1536]{2,1,0:T(8,128)}, f32[2,128,1536]{2,1,0:T(8,128)}, u32[]{:S(2)}, u32[]{:S(2)}) collective-permute-start(f32[2,128,1536]{2,1,0:T(8,128)} %get-tuple-element.31), channel_id=1, source_target_pairs={{1,0},{2,1},{3,2},{4,3},{5,4},{6,5},{7,6},{8,7},{9,8},{10,9},{11,1... | collective-permute-start | bytes 4718600 | tf_op jit(solution)/shard_map/ppermute | solution.py:30
  45.6 4.4 %collective-permute-start.2 = (f32[2,128,1536]{2,1,0:T(8,128)}, f32[2,128,1536]{2,1,0:T(8,128)}, u32[]{:S(2)}, u32[]{:S(2)}) collective-permute-start(f32[2,128,1536]{2,1,0:T(8,128)} %get-tuple-element.30), channel_id=1, source_target_pairs={{0,1},{1,2},{2,3},{3,4},{4,5},{5,6},{6,7},{7,8},{8,9},{9,10},{10,1... | collective-permute-start | bytes 4718600 | tf_op jit(solution)/shard_map/ppermute | solution.py:30
  50.1 1.5 fusion.14
  51.6 2.3 %copy.63 = bf16[256,1536]{1,0:T(8,128)(2,1)} copy(bf16[256,1536]{0,1:T(8,128)(2,1)} %bitcast.197) | data formatting | bytes 1572864
  53.9 3.5 %fusion.12 = bf16[256,12,128]{0,2,1:T(8,128)(2,1)} fusion(bf16[384,12,128]{0,2,1:T(8,128)(2,1)} %bitcast.187, bf16[12,256,384]{1,2,0:T(8,128)(2,1)} %copy-done, f32[12,128]{1,0:T(8,128)S(1)} %get-tuple-element.45, f32[256,12]{0,1:T(8,128)S(1)} %get-tuple-element.26), kind=kOutput, calls=%fused_computation.24 | convolution fusion | flops 303169536 | bytes 4343808 | tf_op jit(solution)/shard_map/hij,jhd->ihd/dot_general | solution.py:119
  57.4 2.3 %copy.64 = bf16[256,1536]{1,0:T(8,128)(2,1)} copy(bf16[256,1536]{0,1:T(8,128)(2,1)} %bitcast.194) | data formatting | bytes 1572864
  59.7 1.4 fusion.31
  61.2 0.3 fusion.33
  61.5 105.1 %psum.7 = f32[2,1536]{1,0:T(2,128)} all-reduce(f32[2,1536]{1,0:T(2,128)S(1)} %pad_maximum_fusion.3), channel_id=1, replica_groups=mesh['clip'=16,'seq'=32] {'clip','seq'}, use_global_device_ids=true, to_apply=%region_7.8 | all-reduce | flops 3072 | bytes 24576 | tf_op jit(solution)/shard_map/psum | solution.py:181
  166.6 0.0 collective-permute-done.3
  166.6 0.0 collective-permute-done.2
  166.6 2.4 %fusion.11 = bf16[2,128,1536]{2,1,0:T(8,128)(2,1)S(1)} fusion(f32[2,128,1536]{2,1,0:T(8,128)} %collective-permute-done.3, f32[2,128,1536]{2,1,0:T(8,128)} %collective-permute-done.2, f32[1,384,1536]{2,1,0:T(8,128)S(1)} %copy.61, f32[1,384,1536]{2,1,0:T(8,128)} %copy.62), kind=kLoop, calls=%fused_computation.21 | loop fusion | flops 1572864 | bytes 8650752 | tf_op jit(solution)/shard_map/convert.1
  169.0 0.9 slice_bitcast_fusion
  (33 shorter events, 0.3 us)
Async XLA Ops:
  0.6 14.3 %copy-start.10 = (s32[1,4]{1,0:T(1,128)S(1)}, s32[1,4]{1,0:T(1,128)}, u32[]{:S(2)}) copy-start(s32[1,4]{1,0:T(1,128)} %param.12) | copy-start | bytes 52
  0.6 14.7 %copy-start.7 = (bf16[256,1536]{1,0:T(8,128)(2,1)S(1)}, bf16[256,1536]{1,0:T(8,128)(2,1)}, u32[]{:S(2)}) copy-start(bf16[256,1536]{1,0:T(8,128)(2,1)} %param.7) | copy-start | bytes 2359300
  0.7 14.9 %copy-start.8 = (bf16[2,1536]{1,0:T(2,128)(2,1)S(1)}, bf16[2,1536]{1,0:T(2,128)(2,1)}, u32[]{:S(2)}) copy-start(bf16[2,1536]{1,0:T(2,128)(2,1)} %param.10) | copy-start | bytes 18436
  2.0 13.9 %copy-start.9 = (s32[4096]{0:T(1024)S(1)}, s32[4096]{0:T(1024)}, u32[]{:S(2)}) copy-start(s32[4096]{0:T(1024)} %param.11) | copy-start | bytes 49156
  4.1 14.4 %collective-permute-start.1 = (bf16[2,128,1536]{1,2,0:T(8,128)(2,1)}, bf16[2,128,1536]{1,2,0:T(8,128)(2,1)S(1)}, u32[]{:S(2)}, u32[]{:S(2)}) collective-permute-start(bf16[2,128,1536]{1,2,0:T(8,128)(2,1)} %pad_maximum_fusion.2), channel_id=1, source_target_pairs={{1,0},{2,1},{3,2},{4,3},{5,4},{6,5},{7,6},{8,7},{9,8},{10,9},{11,1... | collective-permute-start | bytes 2359304 | tf_op jit(solution)/shard_map/ppermute | solution.py:20
  12.9 11.2 %collective-permute-start = (bf16[2,128,1536]{1,2,0:T(8,128)(2,1)}, bf16[2,128,1536]{1,2,0:T(8,128)(2,1)}, u32[]{:S(2)}, u32[]{:S(2)}) collective-permute-start(bf16[2,128,1536]{1,2,0:T(8,128)(2,1)} %pad_maximum_fusion.2), channel_id=1, source_target_pairs={{0,1},{1,2},{2,3},{3,4},{4,5},{5,6},{6,7},{7,8},{8,9},{9,10},{10,1... | collective-permute-start | bytes 2359304 | tf_op jit(solution)/shard_map/ppermute | solution.py:18
  17.7 12.0 %copy-start.1 = (bf16[256,1536]{0,1:T(8,128)(2,1)}, bf16[256,1536]{0,1:T(8,128)(2,1)S(1)}, u32[]{:S(2)}) copy-start(bf16[256,1536]{0,1:T(8,128)(2,1)S(1)} %broadcast_multiply_fusion) | copy-start | bytes 2359300
  25.8 1.0 copy-start.2
  25.8 2.0 %copy-start.5 = (bf16[1,384,1536]{1,2,0:T(8,128)(2,1)}, bf16[1,384,1536]{1,2,0:T(8,128)(2,1)S(1)}, u32[]{:S(2)}) copy-start(bf16[1,384,1536]{1,2,0:T(8,128)(2,1)S(1)} %get-tuple-element.33) | copy-start | bytes 3538948
  29.6 2.3 %copy-start.3 = (bf16[12,256,384]{1,2,0:T(8,128)(2,1)}, bf16[12,256,384]{1,2,0:T(8,128)(2,1)S(1)}, u32[]{:S(2)}) copy-start(bf16[12,256,384]{1,2,0:T(8,128)(2,1)S(1)} %get-tuple-element.29) | copy-start | bytes 7077892
  32.8 2.2 %copy-start = (bf16[12,256,384]{1,2,0:T(8,128)(2,1)}, bf16[12,256,384]{1,2,0:T(8,128)(2,1)S(1)}, u32[]{:S(2)}) copy-start(bf16[12,256,384]{1,2,0:T(8,128)(2,1)S(1)} %fusion.2) | copy-start | bytes 7077892
  40.2 9.9 %copy-start.4 = (bf16[12,256,384]{1,2,0:T(8,128)(2,1)S(1)}, bf16[12,256,384]{1,2,0:T(8,128)(2,1)}, u32[]{:S(2)}) copy-start(bf16[12,256,384]{1,2,0:T(8,128)(2,1)} %copy-done.3) | copy-start | bytes 7077892
  40.2 9.9 %copy-start.6 = (bf16[1,384,1536]{1,2,0:T(8,128)(2,1)S(1)}, bf16[1,384,1536]{1,2,0:T(8,128)(2,1)}, u32[]{:S(2)}) copy-start(bf16[1,384,1536]{1,2,0:T(8,128)(2,1)} %copy-done.5) | copy-start | bytes 3538948
  43.7 122.9 %collective-permute-start.3 = (f32[2,128,1536]{2,1,0:T(8,128)}, f32[2,128,1536]{2,1,0:T(8,128)}, u32[]{:S(2)}, u32[]{:S(2)}) collective-permute-start(f32[2,128,1536]{2,1,0:T(8,128)} %get-tuple-element.31), channel_id=1, source_target_pairs={{1,0},{2,1},{3,2},{4,3},{5,4},{6,5},{7,6},{8,7},{9,8},{10,9},{11,1... | collective-permute-start | bytes 4718600 | tf_op jit(solution)/shard_map/ppermute | solution.py:30
  45.6 121.0 %collective-permute-start.2 = (f32[2,128,1536]{2,1,0:T(8,128)}, f32[2,128,1536]{2,1,0:T(8,128)}, u32[]{:S(2)}, u32[]{:S(2)}) collective-permute-start(f32[2,128,1536]{2,1,0:T(8,128)} %get-tuple-element.30), channel_id=1, source_target_pairs={{0,1},{1,2},{2,3},{3,4},{4,5},{5,6},{6,7},{7,8},{8,9},{9,10},{10,1... | collective-permute-start | bytes 4718600 | tf_op jit(solution)/shard_map/ppermute | solution.py:30
where the time goes:
time: 171 us; the launch traced here: 170 us
  blocking collectives  105 us (61%)
  starting transfers between devices  17 us (10%)
  local copies, waits for them, and re-layouts  15.2 us (9%)
  matrix products  14.4 us (8%)
  other arithmetic  11 us (6%)
  waiting for transfers between devices  6.2 us (4%)
    psum x1, blocking collectives, body(): null_grad = lax.psum(null_part, ('clip', 'seq'))  105 us
    unnamed x30, local copies, waits for them, and re-layouts  8.84 us
    ppermute x1, starting transfers between devices, padded(): lax.ppermute(head, axis, [((i + 1) % count, i) for i in range(ends)])  8.77 us
    ppermute x2, starting transfers between devices, shifted(): return lax.ppermute(block, axis, route)  6.31 us
    ppermute x1, waiting for transfers between devices, padded(): lax.ppermute(tail, axis, [(i, (i + 1) % count) for i in range(ends)])  5.57 us
    another operation x2, local copies, waits for them, and re-layouts, body(): backs = jnp.stack([key_all, value_all])  5.17 us
    dot_general x1, matrix products, backward_block(): jnp.einsum('hij,jhd->ihd', score_grad, key_heads, preferred_element_type=...  3.54 us
    another operation x1, other arithmetic, body(): backs = jnp.stack([key_all, value_all])  3.53 us
  transfers between devices with their start and end apart: 4, of which 2 were waited for; matrix products, arithmetic and copies ran while one was open for 8% of the time, Pallas kernels for 0%

commit v1 on v0

v1 whole, which is shorter than its diff:
```python
import numpy as np

import jax
import jax.numpy as jnp
from jax import lax
from jax.experimental import pallas as pl
from jax.experimental.pallas import tpu as pltpu
from jax.sharding import Mesh
from jax.sharding import PartitionSpec as P

HEADS = 12
HEAD = 128
NULL_ROWS = 16
MASKED = -1e30
FACTOR = HEAD**-0.5
LOG2E = 1.4426950408889634
CLIP_PARTS = (("yh", 2), ("z", 8))
SEQ_PARTS = (("yl", 4), ("x", 4), ("core", 2))
CLIP = tuple(name for name, _ in CLIP_PARTS)
SEQ = tuple(name for name, _ in SEQ_PARTS)
VMEM_LIMIT = 60 * 1024 * 1024
PER_STEP = 2
STEPS = HEADS // PER_STEP
WIDE = PER_STEP * HEAD


def swap_chip(block):
    count = lax.axis_size(SEQ)
    return lax.ppermute(block, SEQ, [(i, i ^ 1) for i in range(count)])


def swap_link(block):
    last = lax.axis_size(SEQ) - 1
    pairs = [(i, i + 1) for i in range(1, last, 2)]
    return lax.ppermute(block, SEQ, pairs + [(b, a) for a, b in pairs])


def segment_of(positions, bounds):
    return jnp.sum((positions[:, None] >= bounds[None, :-1]).astype(jnp.int32), axis=1)


def allowed_pairs(query_pos, key_pos, bounds, keep_rows, total_audio, pad_segment, window):
    key_clip = jnp.clip(key_pos, 0, total_audio - 1)
    key_seg = segment_of(key_clip, bounds)
    query_seg = segment_of(query_pos // 2, bounds)
    key_inside = (
        (key_pos >= 0) & (key_pos < total_audio) & (keep_rows == 1) & (key_seg < pad_segment)
    )
    nearby = jnp.abs(query_pos[None, :] - 2 * key_pos[:, None]) <= 2 * window
    return key_inside[:, None] & (key_seg[:, None] == query_seg[None, :]) & nearby


def dot(a, b, lhs_dim, rhs_dim):
    return lax.dot_general(
        a, b, (((lhs_dim,), (rhs_dim,)), ((), ())), preferred_element_type=jnp.float32
    )


def stack_kernel(key_ref, value_ref, out_ref, sems):
    rows = key_ref.shape[0]
    copies = [
        pltpu.make_async_copy(ref, out_ref.at[pl.ds(i * rows, rows)], sems.at[i])
        for i, ref in enumerate((key_ref, value_ref))
    ]
    for copy in copies:
        copy.start()
    for copy in copies:
        copy.wait()


def stack_call(keys, values):
    rows, width = keys.shape
    return pl.pallas_call(
        stack_kernel,
        in_specs=[pl.BlockSpec(memory_space=pl.ANY)] * 2,
        out_specs=pl.BlockSpec(memory_space=pltpu.VMEM),
        out_shape=jax.ShapeDtypeStruct((2 * rows, width), keys.dtype),
        scratch_shapes=[pltpu.SemaphoreType.DMA((2,))],
        compiler_params=pltpu.CompilerParams(vmem_limit_bytes=VMEM_LIMIT),
        name="stack",
    )(keys, values)


def columns(step):
    return pl.ds(pl.multiple_of(step * WIDE, WIDE), WIDE)


def wide_copies(refs, held, sems, step):
    return [
        pltpu.make_async_copy(ref.at[:, columns(step)], held.at[step, i], sems.at[step, i])
        for i, ref in enumerate(refs)
    ]


def start(copies):
    for copy in copies:
        copy.start()


def wait(copies):
    for copy in copies:
        copy.wait()


def gathered(blocks, null_ref, cols, index):
    rows = blocks.shape[1] // 2
    return jnp.concatenate(
        [blocks[i, index * rows : (index + 1) * rows, cols] for i in range(3)] + [null_ref[index]],
        axis=0,
    )


def heads_kernel(
    q_hbm, g_hbm, far_hbm, own_hbm, near_hbm, null_hbm, bias_hbm, valid_hbm,
    out_hbm, dq_hbm, far_grad_hbm, own_grad_hbm, near_grad_hbm, null_grad_ref,
    held, null_ref, bias_ref, valid_ref, results, ends, middle, null_sum,
    in_sems, rest_sems, out_sems,
):
    refs = (q_hbm, g_hbm, far_hbm, own_hbm, near_hbm)
    rows = middle.shape[2]
    rest = [
        pltpu.make_async_copy(src, dst, rest_sems.at[i])
        for i, (src, dst) in enumerate(
            ((bias_hbm, bias_ref), (valid_hbm, valid_ref), (null_hbm, null_ref))
        )
    ]
    start(wide_copies(refs, held, in_sems, 0))
    start(rest)
    for step in range(1, STEPS):
        start(wide_copies(refs, held, in_sems, step))
    wait(rest)

    def out_copies(step):
        pairs = [
            (results.at[step, 0], out_hbm.at[:, columns(step)]),
            (results.at[step, 1], dq_hbm.at[:, columns(step)]),
            (ends.at[step, 0], far_grad_hbm.at[:, :, columns(step)]),
            (middle.at[step], own_grad_hbm.at[:, :, columns(step)]),
            (ends.at[step, 1], near_grad_hbm.at[:, :, columns(step)]),
        ]
        return [
            pltpu.make_async_copy(src, dst, out_sems.at[step, i])
            for i, (src, dst) in enumerate(pairs)
        ]

    def one_step(step, carry):
        wait(wide_copies(refs, held, in_sems, step))
        for part in range(PER_STEP):
            head = step * PER_STEP + part
            cols = slice(part * HEAD, (part + 1) * HEAD)
            q = held[step, 0, :, cols]
            g = held[step, 1, :, cols]
            keys = gathered(held.at[step, 2:], null_ref.at[head], cols, 0)
            values = gathered(held.at[step, 2:], null_ref.at[head], cols, 1)
            scores = dot(keys, q, 1, 1) + bias_ref[...]
            top = jnp.max(scores, axis=0, keepdims=True)
            exponent = jnp.exp2((scores - top) * (FACTOR * LOG2E))
            total = jnp.sum(exponent, axis=0, keepdims=True)
            exponent = exponent.astype(jnp.bfloat16)
            share = valid_ref[...] / total
            g_flip = g.T.astype(jnp.float32)
            out_flip = dot(values, exponent, 0, 0) * share
            delta = jnp.sum(out_flip * g_flip, axis=0, keepdims=True)
            results[step, 0, :, cols] = out_flip.astype(jnp.bfloat16).T
            prob_grad = dot(values, g, 1, 1)
            score_grad = ((prob_grad - delta) * (share * FACTOR)).astype(jnp.bfloat16) * exponent
            results[step, 1, :, cols] = dot(keys, score_grad, 0, 0).astype(jnp.bfloat16).T
            key_term = dot(score_grad, q, 1, 0)
            value_term = dot(exponent, (g_flip * share).astype(jnp.bfloat16), 1, 1)
            for index, term in enumerate((key_term, value_term)):
                ends[step, 0, index, :, cols] = term[:rows].astype(jnp.bfloat16)
                middle[step, index, :, cols] = term[rows : 2 * rows]
                ends[step, 1, index, :, cols] = term[2 * rows : 3 * rows].astype(jnp.bfloat16)
                null_sum[pl.ds(index * HEADS + head, 1), :] = term[3 * rows : 3 * rows + 1]
        start(out_copies(step))
        return carry

    lax.fori_loop(0, STEPS, one_step, 0)
    null_grad_ref[...] = jnp.broadcast_to(
        null_sum[...].astype(jnp.bfloat16)[None], null_grad_ref.shape
    )
    for step in range(STEPS):
        wait(out_copies(step))


def heads_call(q, g, far, own, near, null_rows, bias, valid, peers):
    video_rows, width = q.shape
    audio_rows = video_rows // 2
    args = (q, g, far, own, near, null_rows, bias, valid)
    anywhere = pl.BlockSpec(memory_space=pl.ANY)
    wide = jax.ShapeDtypeStruct((video_rows, width), jnp.bfloat16)
    terms = [
        jax.ShapeDtypeStruct((2, audio_rows, width), dtype)
        for dtype in (jnp.bfloat16, jnp.float32, jnp.bfloat16)
    ]
    return pl.pallas_call(
        heads_kernel,
        in_specs=[anywhere] * len(args),
        out_specs=[anywhere] * 5 + [pl.BlockSpec(memory_space=pltpu.VMEM)],
        out_shape=[wide, wide, *terms, jax.ShapeDtypeStruct((peers, 2 * HEADS, HEAD), jnp.bfloat16)],
        scratch_shapes=[
            pltpu.VMEM((STEPS, 5, video_rows, WIDE), jnp.bfloat16),
            pltpu.VMEM(null_rows.shape, jnp.bfloat16),
            pltpu.VMEM(bias.shape, jnp.float32),
            pltpu.VMEM(valid.shape, jnp.float32),
            pltpu.VMEM((STEPS, 2, video_rows, WIDE), jnp.bfloat16),
            pltpu.VMEM((STEPS, 2, 2, audio_rows, WIDE), jnp.bfloat16),
            pltpu.VMEM((STEPS, 2, audio_rows, WIDE), jnp.float32),
            pltpu.VMEM((2 * HEADS, HEAD), jnp.float32),
            pltpu.SemaphoreType.DMA((STEPS, 5)),
            pltpu.SemaphoreType.DMA((3,)),
            pltpu.SemaphoreType.DMA((STEPS, 5)),
        ],
        compiler_params=pltpu.CompilerParams(vmem_limit_bytes=VMEM_LIMIT),
        cost_estimate=pl.CostEstimate(
            flops=12 * bias.size * width, bytes_accessed=9_000_000, transcendentals=bias.size * HEADS
        ),
        name="heads",
    )(*args)


def sum_peers(parts):
    return jnp.sum(parts.astype(jnp.float32), axis=0)


def body(video_query, audio_key, audio_value, null_kv, audio_keep, clip_lengths, out_grad):
    audio_rows = audio_key.shape[0]
    video_rows = video_query.shape[0]
    shards = lax.axis_size(SEQ)
    seq_index = lax.axis_index(SEQ)
    total_audio = audio_rows * shards

    stacked = stack_call(audio_key, audio_value)
    far = swap_link(stacked)

    bounds = jnp.cumsum(clip_lengths[0])
    pad_segment = clip_lengths.shape[1] - 1
    query_pos = seq_index * video_rows + jnp.arange(video_rows, dtype=jnp.int32)
    side = 1 - 2 * (seq_index % 2)
    starts = [(seq_index + move) * audio_rows for move in (-side, 0, side)]
    own_pos = jnp.arange(audio_rows, dtype=jnp.int32)
    key_pos = jnp.concatenate([start + own_pos for start in starts])
    keep_padded = jnp.pad(audio_keep, (audio_rows, audio_rows))
    keep_rows = jnp.concatenate(
        [lax.dynamic_slice_in_dim(keep_padded, start + audio_rows, audio_rows) for start in starts]
    )
    allowed = allowed_pairs(
        query_pos, key_pos, bounds, keep_rows, total_audio, pad_segment, audio_rows
    )
    null_allowed = jnp.arange(NULL_ROWS) == 0
    bias = jnp.where(
        jnp.concatenate([allowed, jnp.broadcast_to(null_allowed[:, None], (NULL_ROWS, video_rows))]),
        0.0,
        MASKED,
    ).astype(jnp.float32)
    valid = (segment_of(query_pos // 2, bounds) < pad_segment).astype(jnp.float32)[None]
    null_heads = null_kv.reshape(2, HEADS, 1, HEAD).swapaxes(0, 1)
    null_rows = jnp.pad(null_heads, ((0, 0), (0, 0), (0, NULL_ROWS - 1), (0, 0)))

    stacked, valid = lax.optimization_barrier((stacked, valid))
    near = swap_chip(stacked)

    wide_axes, deep_axes = ("yh", "yl", "x"), ("z", "core")
    attended, query_grad, far_grad, own_grad, near_grad, null_copies = heads_call(
        video_query, out_grad, far, stacked, near, null_rows, bias, valid, lax.axis_size(wide_axes)
    )
    far_back = swap_link(far_grad)
    first = lax.all_to_all(null_copies, wide_axes, 0, 0)
    first, near_grad = lax.optimization_barrier((first, near_grad))
    partial = sum_peers(first).astype(jnp.bfloat16)
    copies = jnp.broadcast_to(partial[None], (lax.axis_size(deep_axes), *partial.shape))
    second = lax.all_to_all(copies, deep_axes, 0, 0)
    near_back = swap_chip(near_grad)
    grads = [
        (own_grad[i] + far_back[i].astype(jnp.float32) + near_back[i].astype(jnp.float32)).astype(
            jnp.bfloat16
        )
        for i in range(2)
    ]
    second, *grads = lax.optimization_barrier((second, *grads))
    null_grad = sum_peers(second).reshape(null_kv.shape)
    return (attended, query_grad, grads[0], grads[1], null_grad)


def solution(mesh):
    parts = CLIP_PARTS + SEQ_PARTS
    fine = Mesh(
        np.asarray(mesh.devices).reshape([size for _, size in parts]), [name for name, _ in parts]
    )
    rows = P(CLIP + SEQ, None)
    return jax.shard_map(
        body,
        mesh=fine,
        in_specs=(rows, rows, rows, P(), P(CLIP), P(CLIP, None), rows),
        out_specs=(rows, rows, rows, rows, P()),
        check_vma=False,
    )
```

time: 171 us -> 78.2 us (0.46)
  blocking collectives: 105 us -> 0 us
  starting transfers between devices: 17 us -> 36.1 us
  Pallas kernels: 0 us -> 16.1 us
  matrix products: 14.4 us -> 0 us
  local copies, waits for them, and re-layouts: 15.2 us -> 2.87 us
  waiting for transfers between devices: 6.2 us -> 17 us
  other arithmetic: 11 us -> 4.78 us
    psum x1 -> x0, blocking collectives: 105 us -> none  [body(): null_grad = lax.psum(null_part, ('clip', 'seq'))]
    all_to_all x0 -> x2, starting transfers between devices: none -> 22.3 us  [the longest x1 11.5 us: body(): first = lax.all_to_all(null_copies, wide_axes, 0, 0)]
    pallas_call x0 -> x2, Pallas kernels: none -> 16.1 us  [the longest x1 14.1 us: heads_call(): pl.pallas_call(heads_kernel, in_specs=[anywhere] * len(args), out_specs=[...]
    all_to_all x0 -> x2, waiting for transfers between devices: none -> 15.1 us  [the longest x1 9.2 us: body(): first = lax.all_to_all(null_copies, wide_axes, 0, 0)]
    dot_general x10 -> x0, matrix products: 14.4 us -> none  [the longest x1 3.54 us: backward_block(): jnp.einsum('hij,jhd->ihd', score_grad, key_heads, preferred_element_type=...]
    unnamed x30 -> x10, local copies, waits for them, and re-layouts: 8.84 us -> 0.91 us
    another operation x5 -> x1, other arithmetic: 7.08 us -> 0.18 us  [the longest x1 3.53 us: body(): backs = jnp.stack([key_all, value_all])]
    another operation x2 -> x0, local copies, waits for them, and re-layouts: 5.17 us -> none  [body(): backs = jnp.stack([key_all, value_all])]
  transfers between devices with their start and end apart: 4 -> 6, of which waited for: 2 -> 3; matrix products, arithmetic and copies ran while one was open for 8% -> 8% of each run, Pallas kernels for 0% -> 0%
where the time goes in v1:
time: 78.2 us; the launch traced here: 77.8 us
  starting transfers between devices  36.1 us (46%)
  waiting for transfers between devices  17 us (22%)
  Pallas kernels  16.1 us (21%)
  other arithmetic  4.78 us (6%)
  local copies, waits for them, and re-layouts  2.87 us (4%)
  between operations  0.85 us (1%)
    pallas_call x1, Pallas kernels, heads_call(): pl.pallas_call(heads_kernel, in_specs=[anywhere] * len(args), out_specs=[...  14.1 us
    all_to_all x1, starting transfers between devices, body(): first = lax.all_to_all(null_copies, wide_axes, 0, 0)  11.5 us
    all_to_all x1, starting transfers between devices, body(): second = lax.all_to_all(copies, deep_axes, 0, 0)  10.8 us
    all_to_all x1, waiting for transfers between devices, body(): first = lax.all_to_all(null_copies, wide_axes, 0, 0)  9.2 us
    ppermute x2, starting transfers between devices, swap_link(): return lax.ppermute(block, SEQ, pairs + [(b, a) for a, b in pairs])  6.93 us
    ppermute x2, starting transfers between devices, swap_chip(): return lax.ppermute(block, SEQ, [(i, i ^ 1) for i in range(count)])  6.88 us
    all_to_all x1, waiting for transfers between devices, body(): second = lax.all_to_all(copies, deep_axes, 0, 0)  5.94 us
    convert_element_type x1, other arithmetic, body(): (own_grad[i] + far_back[i].astype(jnp.float32) + near_back[i].astype(jnp....  2.53 us
  transfers between devices with their start and end apart: 6, of which 3 were waited for; matrix products, arithmetic and copies ran while one was open for 8% of the time, Pallas kernels for 0%

profile of v1, /device:TPU:1, one launch (start us, length us, event | category | flops | bytes accessed | tf_op | source)
XLA Modules:
  0.0 77.8 jit_solution(4188465753486178682)
XLA Ops:
  0.6 0.0 copy-start.4
  0.6 0.0 copy-start.1
  0.7 0.0 copy-start
  0.7 2.0 %stack.1.own_hbm = bf16[256,1536]{1,0:T(8,128)(2,1)} custom-call(bf16[128,1536]{1,0:T(8,128)(2,1)} %key_ref.1, bf16[128,1536]{1,0:T(8,128)(2,1)} %value_ref.1), custom_call_target="tpu_custom_call" | custom-call | tf_op jit(solution)/shard_map/stack/pallas_call | solution.py:73
  2.7 4.5 %collective-permute-start = (bf16[256,1536]{1,0:T(8,128)(2,1)}, bf16[256,1536]{1,0:T(8,128)(2,1)S(1)}, u32[]{:S(2)}, u32[]{:S(2)}) collective-permute-start(bf16[256,1536]{1,0:T(8,128)(2,1)} %stack.1.own_hbm), channel_id=1, source_target_pairs={{1,2},{3,4},{5,6},{7,8},{9,10},{11,12},{13,14},{15,16},{17,18},{19... | collective-permute-start | bytes 2359304 | tf_op jit(solution)/shard_map/ppermute | solution.py:35
  7.2 0.0 copy-done.4
  7.2 0.2 reduce-window.4
  7.4 0.1 convert_reduce_fusion.2
  7.5 0.6 compare_convert_fusion
  8.1 5.0 %collective-permute-start.1 = (bf16[256,1536]{1,0:T(8,128)(2,1)}, bf16[256,1536]{1,0:T(8,128)(2,1)S(1)}, u32[]{:S(2)}, u32[]{:S(2)}) collective-permute-start(bf16[256,1536]{1,0:T(8,128)(2,1)} %stack.1.own_hbm), channel_id=1, source_target_pairs={{0,1},{1,0},{2,3},{3,2},{4,5},{5,4},{6,7},{7,6},{8,9},{9,8},{10,11... | collective-permute-start | bytes 2359304 | tf_op jit(solution)/shard_map/ppermute | solution.py:29
  13.1 0.0 copy-done.1
  13.2 0.7 pad.8.null_hbm
  13.8 0.0 copy-done
  13.9 0.1 pad_dynamic-slice_fusion.2
  14.0 0.1 convert_reduce_fusion.1
  14.1 0.2 fusion.2
  14.3 0.9 %add_select_fusion.bias_hbm = f32[400,256]{1,0:T(8,128)} fusion(pred[384,256]{1,0:T(8,128)(4,1)S(1)} %fusion.2, pred[400]{0:T(512)(128)(4,1)S(1)} %pad.11.clone), kind=kLoop, calls=%fused_computation.2 | loop fusion | flops 204800 | bytes 508304 | tf_op jit(solution)/shard_map/jit(_where)/select_n | solution.py:251
  15.2 0.0 collective-permute-done.1.near_hbm
  15.2 0.0 copy-start.3
  15.2 1.9 %collective-permute-done.far_hbm = bf16[256,1536]{1,0:T(8,128)(2,1)S(1)} collective-permute-done((bf16[256,1536]{1,0:T(8,128)(2,1)}, bf16[256,1536]{1,0:T(8,128)(2,1)S(1)}, u32[]{:S(2)}, u32[]{:S(2)}) %collective-permute-start) | collective-permute-done | bytes 786464 | tf_op jit(solution)/shard_map/ppermute | solution.py:35
  17.1 0.0 copy-done.3
  17.1 0.0 copy-start.2
  17.1 0.9 %copy-done.2 = bf16[256,1536]{1,0:T(8,128)(2,1)} copy-done((bf16[256,1536]{1,0:T(8,128)(2,1)}, bf16[256,1536]{1,0:T(8,128)(2,1)S(1)}, u32[]{:S(2)}) %copy-start.2) | copy-done | bytes 786456
  18.0 14.1 %heads.1 = (bf16[256,1536]{1,0:T(8,128)(2,1)}, bf16[256,1536]{1,0:T(8,128)(2,1)}, bf16[2,128,1536]{2,1,0:T(8,128)(2,1)}, f32[2,128,1536]{2,1,0:T(8,128)}, bf16[2...) custom-call(bf16[256,1536]{1,0:T(8,128)(2,1)} %q_hbm.1, bf16[256,1536]{1,0:T(8,128)(2,1)} %g_hbm.1, ...), custom_call_target="tpu_custom_call" | custom-call | flops 1887436800 | bytes 9000000 | tf_op jit(solution)/shard_map/heads/pallas_call | solution.py:196
  32.1 11.5 %all-to-all-start = ((bf16[32,24,128]{2,1,0:T(8,128)(2,1)}), bf16[32,24,128]{2,1,0:T(8,128)(2,1)S(1)}, u32[]{:S(2)}, u32[]{:S(2)}) async-start(bf16[32,24,128]{2,1,0:T(8,128)(2,1)} %get-tuple-element.22), calls=%async_computation | async-start | bytes 393216 | tf_op jit(solution)/shard_map/all_to_all | solution.py:268
  43.6 2.4 %collective-permute-start.2 = (bf16[2,128,1536]{2,1,0:T(8,128)(2,1)}, bf16[2,128,1536]{2,1,0:T(8,128)(2,1)S(1)}, u32[]{:S(2)}, u32[]{:S(2)}) collective-permute-start(bf16[2,128,1536]{2,1,0:T(8,128)(2,1)} %get-tuple-element.26), channel_id=1, source_target_pairs={{1,2},{3,4},{5,6},{7,8},{9,10},{11,12},{13,14},{15,16},{17,18},{19... | collective-permute-start | bytes 2359304 | tf_op jit(solution)/shard_map/ppermute | solution.py:35
  46.0 9.2 %all-to-all-done = bf16[32,24,128]{2,1,0:T(8,128)(2,1)S(1)} async-done(((bf16[32,24,128]{2,1,0:T(8,128)(2,1)}), bf16[32,24,128]{2,1,0:T(8,128)(2,1)S(1)}, u32[]{:S(2)}, u32[]{:S(2)}) %all-to-all-start) | async-done | bytes 196640 | tf_op jit(solution)/shard_map/all_to_all | solution.py:268
  55.2 1.9 %collective-permute-start.3 = (bf16[2,128,1536]{2,1,0:T(8,128)(2,1)}, bf16[2,128,1536]{2,1,0:T(8,128)(2,1)S(1)}, u32[]{:S(2)}, u32[]{:S(2)}) collective-permute-start(bf16[2,128,1536]{2,1,0:T(8,128)(2,1)} %get-tuple-element.27), channel_id=1, source_target_pairs={{0,1},{1,0},{2,3},{3,2},{4,5},{5,4},{6,7},{7,6},{8,9},{9,8},{10,11... | collective-permute-start | bytes 2359304 | tf_op jit(solution)/shard_map/ppermute | solution.py:29
  57.2 0.6 broadcast_in_dim.13
  57.8 10.8 %all-to-all-start.1 = ((bf16[16,24,128]{2,1,0:T(8,128)(2,1)}), bf16[16,24,128]{2,1,0:T(8,128)(2,1)S(1)}, u32[]{:S(2)}, u32[]{:S(2)}) async-start(bf16[16,24,128]{2,1,0:T(8,128)(2,1)} %broadcast_in_dim.13), calls=%async_computation.1 | async-start | bytes 196608 | tf_op jit(solution)/shard_map/all_to_all | solution.py:272
  68.6 0.0 collective-permute-done.2
  68.6 0.0 collective-permute-done.3
  68.7 2.5 %fusion.1 = (bf16[128,1536]{1,0:T(8,128)(2,1)}, bf16[128,1536]{1,0:T(8,128)(2,1)}) fusion(f32[2,128,1536]{2,1,0:T(8,128)} %get-tuple-element.25, bf16[2,128,1536]{2,1,0:T(8,128)(2,1)S(1)} %collective-permute-done.3, bf16[2,128,1536]{2,1,0:T(8,128)(2,1)S(1)} %collective-permute-done.2), kind=kLoop, calls=%fused_computation.4 | loop fusion | flops 1966080 | bytes 3932160 | tf_op jit(solution)/shard_map/convert_element_type | solution.py:275
  71.2 5.9 %all-to-all-done.1 = bf16[16,24,128]{2,1,0:T(8,128)(2,1)S(1)} async-done(((bf16[16,24,128]{2,1,0:T(8,128)(2,1)}), bf16[16,24,128]{2,1,0:T(8,128)(2,1)S(1)}, u32[]{:S(2)}, u32[]{:S(2)}) %all-to-all-start.1) | async-done | bytes 98336 | tf_op jit(solution)/shard_map/all_to_all | solution.py:272
  77.2 0.6 reshape.173
  (11 shorter events, 0.1 us)
Async XLA Ops:
  0.6 6.6 %copy-start.4 = (s32[1,4]{1,0:T(1,128)S(1)}, s32[1,4]{1,0:T(1,128)}, u32[]{:S(2)}) copy-start(s32[1,4]{1,0:T(1,128)} %param.12) | copy-start | bytes 52
  0.6 12.5 %copy-start.1 = (bf16[2,1536]{1,0:T(2,128)(2,1)S(1)}, bf16[2,1536]{1,0:T(2,128)(2,1)}, u32[]{:S(2)}) copy-start(bf16[2,1536]{1,0:T(2,128)(2,1)} %param.10) | copy-start | bytes 18436
  0.7 13.2 %copy-start = (s32[4096]{0:T(1024)S(1)}, s32[4096]{0:T(1024)}, u32[]{:S(2)}) copy-start(s32[4096]{0:T(1024)} %param.11) | copy-start | bytes 49156
  2.7 14.4 %collective-permute-start = (bf16[256,1536]{1,0:T(8,128)(2,1)}, bf16[256,1536]{1,0:T(8,128)(2,1)S(1)}, u32[]{:S(2)}, u32[]{:S(2)}) collective-permute-start(bf16[256,1536]{1,0:T(8,128)(2,1)} %stack.1.own_hbm), channel_id=1, source_target_pairs={{1,2},{3,4},{5,6},{7,8},{9,10},{11,12},{13,14},{15,16},{17,18},{19... | collective-permute-start | bytes 2359304 | tf_op jit(solution)/shard_map/ppermute | solution.py:35
  8.1 7.1 %collective-permute-start.1 = (bf16[256,1536]{1,0:T(8,128)(2,1)}, bf16[256,1536]{1,0:T(8,128)(2,1)S(1)}, u32[]{:S(2)}, u32[]{:S(2)}) collective-permute-start(bf16[256,1536]{1,0:T(8,128)(2,1)} %stack.1.own_hbm), channel_id=1, source_target_pairs={{0,1},{1,0},{2,3},{3,2},{4,5},{5,4},{6,7},{7,6},{8,9},{9,8},{10,11... | collective-permute-start | bytes 2359304 | tf_op jit(solution)/shard_map/ppermute | solution.py:29
  15.2 1.9 %copy-start.3 = (bf16[256,1536]{1,0:T(8,128)(2,1)}, bf16[256,1536]{1,0:T(8,128)(2,1)S(1)}, u32[]{:S(2)}) copy-start(bf16[256,1536]{1,0:T(8,128)(2,1)S(1)} %collective-permute-done.1.near_hbm) | copy-start | bytes 2359300
  17.1 0.9 %copy-start.2 = (bf16[256,1536]{1,0:T(8,128)(2,1)}, bf16[256,1536]{1,0:T(8,128)(2,1)S(1)}, u32[]{:S(2)}) copy-start(bf16[256,1536]{1,0:T(8,128)(2,1)S(1)} %collective-permute-done.far_hbm) | copy-start | bytes 2359300
  32.1 23.1 %all-to-all-start = ((bf16[32,24,128]{2,1,0:T(8,128)(2,1)}), bf16[32,24,128]{2,1,0:T(8,128)(2,1)S(1)}, u32[]{:S(2)}, u32[]{:S(2)}) async-start(bf16[32,24,128]{2,1,0:T(8,128)(2,1)} %get-tuple-element.22), calls=%async_computation | async-start | bytes 393216 | tf_op jit(solution)/shard_map/all_to_all | solution.py:268
  43.6 25.1 %collective-permute-start.2 = (bf16[2,128,1536]{2,1,0:T(8,128)(2,1)}, bf16[2,128,1536]{2,1,0:T(8,128)(2,1)S(1)}, u32[]{:S(2)}, u32[]{:S(2)}) collective-permute-start(bf16[2,128,1536]{2,1,0:T(8,128)(2,1)} %get-tuple-element.26), channel_id=1, source_target_pairs={{1,2},{3,4},{5,6},{7,8},{9,10},{11,12},{13,14},{15,16},{17,18},{19... | collective-permute-start | bytes 2359304 | tf_op jit(solution)/shard_map/ppermute | solution.py:35
  55.2 13.4 %collective-permute-start.3 = (bf16[2,128,1536]{2,1,0:T(8,128)(2,1)}, bf16[2,128,1536]{2,1,0:T(8,128)(2,1)S(1)}, u32[]{:S(2)}, u32[]{:S(2)}) collective-permute-start(bf16[2,128,1536]{2,1,0:T(8,128)(2,1)} %get-tuple-element.27), channel_id=1, source_target_pairs={{0,1},{1,0},{2,3},{3,2},{4,5},{5,4},{6,7},{7,6},{8,9},{9,8},{10,11... | collective-permute-start | bytes 2359304 | tf_op jit(solution)/shard_map/ppermute | solution.py:29
  57.8 19.3 %all-to-all-start.1 = ((bf16[16,24,128]{2,1,0:T(8,128)(2,1)}), bf16[16,24,128]{2,1,0:T(8,128)(2,1)S(1)}, u32[]{:S(2)}, u32[]{:S(2)}) async-start(bf16[16,24,128]{2,1,0:T(8,128)(2,1)} %broadcast_in_dim.13), calls=%async_computation.1 | async-start | bytes 196608 | tf_op jit(solution)/shard_map/all_to_all | solution.py:272

commit v2 on v1

v2 whole, which is shorter than its diff:
```python
import numpy as np

import jax
import jax.numpy as jnp
from jax import lax
from jax.experimental import pallas as pl
from jax.experimental.pallas import tpu as pltpu
from jax.sharding import Mesh
from jax.sharding import PartitionSpec as P

HEADS = 12
HEAD = 128
NULL_ROWS = 16
MASKED = -1e30
FACTOR = HEAD**-0.5
LOG2E = 1.4426950408889634
CLIP_PARTS = (("yh", 2), ("z", 8))
SEQ_PARTS = (("yl", 4), ("x", 4), ("core", 2))
CLIP = tuple(name for name, _ in CLIP_PARTS)
SEQ = tuple(name for name, _ in SEQ_PARTS)
VMEM_LIMIT = 60 * 1024 * 1024
PER_STEP = 4
STEPS = HEADS // PER_STEP
WIDE = PER_STEP * HEAD


def swap_chip(block):
    count = lax.axis_size(SEQ)
    return lax.ppermute(block, SEQ, [(i, i ^ 1) for i in range(count)])


def swap_link(block):
    last = lax.axis_size(SEQ) - 1
    pairs = [(i, i + 1) for i in range(1, last, 2)]
    return lax.ppermute(block, SEQ, pairs + [(b, a) for a, b in pairs])


def segment_of(positions, bounds):
    return jnp.sum((positions[:, None] >= bounds[None, :-1]).astype(jnp.int32), axis=1)


def allowed_pairs(query_pos, key_pos, bounds, keep_rows, total_audio, pad_segment, window):
    key_clip = jnp.clip(key_pos, 0, total_audio - 1)
    key_seg = segment_of(key_clip, bounds)
    query_seg = segment_of(query_pos // 2, bounds)
    key_inside = (
        (key_pos >= 0) & (key_pos < total_audio) & (keep_rows == 1) & (key_seg < pad_segment)
    )
    nearby = jnp.abs(query_pos[None, :] - 2 * key_pos[:, None]) <= 2 * window
    return key_inside[:, None] & (key_seg[:, None] == query_seg[None, :]) & nearby


def dot(a, b, lhs_dim, rhs_dim):
    return lax.dot_general(
        a, b, (((lhs_dim,), (rhs_dim,)), ((), ())), preferred_element_type=jnp.float32
    )


def start(copies):
    for copy in copies:
        copy.start()


def wait(copies):
    for copy in copies:
        copy.wait()


def stack_kernel(key_ref, value_ref, out_ref, held, in_sems, out_sems):
    rows = held.shape[1]
    pieces = [pl.ds(i * rows, rows) for i in range(key_ref.shape[0] // rows)]
    sources = [ref.at[piece] for ref in (key_ref, value_ref) for piece in pieces]
    arrive = [
        pltpu.make_async_copy(src, held.at[i], in_sems.at[i]) for i, src in enumerate(sources)
    ]
    leave = [
        pltpu.make_async_copy(held.at[i], out_ref.at[pl.ds(i * rows, rows)], out_sems.at[i])
        for i in range(len(sources))
    ]
    start(arrive)
    for first, second in zip(arrive, leave):
        first.wait()
        second.start()
    wait(leave)


def stack_call(keys, values):
    rows, width = keys.shape
    return pl.pallas_call(
        stack_kernel,
        in_specs=[pl.BlockSpec(memory_space=pl.ANY)] * 2,
        out_specs=pl.BlockSpec(memory_space=pl.ANY),
        out_shape=jax.ShapeDtypeStruct((2 * rows, width), keys.dtype),
        scratch_shapes=[
            pltpu.VMEM((4, rows // 2, width), keys.dtype),
            pltpu.SemaphoreType.DMA((4,)),
            pltpu.SemaphoreType.DMA((4,)),
        ],
        compiler_params=pltpu.CompilerParams(vmem_limit_bytes=VMEM_LIMIT),
        name="stack",
    )(keys, values)


def gathered(refs, null_ref, cols, index):
    rows = refs[0].shape[0] // 2
    return jnp.concatenate(
        [ref[index * rows : (index + 1) * rows, cols] for ref in refs] + [null_ref[index]], axis=0
    )


def heads_kernel(
    q_ref, g_ref, far_ref, own_ref, near_ref, null_ref, bias_ref, valid_ref,
    out_ref, dq_ref, far_grad_ref, own_grad_ref, near_grad_ref, null_grad_ref, null_sum,
):
    step = pl.program_id(0)
    rows = own_ref.shape[0] // 2
    refs = (far_ref, own_ref, near_ref)
    parts = range(PER_STEP)
    cols = [slice(i * HEAD, (i + 1) * HEAD) for i in parts]
    keys = [gathered(refs, null_ref.at[i], cols[i], 0) for i in parts]
    values = [gathered(refs, null_ref.at[i], cols[i], 1) for i in parts]
    scores = [dot(keys[i], q_ref[:, cols[i]], 1, 1) + bias_ref[...] for i in parts]
    tops = [jnp.max(x, axis=0, keepdims=True) for x in scores]
    exact = [jnp.exp2((x - top) * (FACTOR * LOG2E)) for x, top in zip(scores, tops)]
    shares = [valid_ref[...] / jnp.sum(x, axis=0, keepdims=True) for x in exact]
    exponents = [x.astype(jnp.bfloat16) for x in exact]
    flips = [g_ref[:, cols[i]].T.astype(jnp.float32) for i in parts]
    mixed = [dot(values[i], exponents[i], 0, 0) * shares[i] for i in parts]
    deltas = [jnp.sum(x * flip, axis=0, keepdims=True) for x, flip in zip(mixed, flips)]
    prob_grads = [dot(values[i], g_ref[:, cols[i]], 1, 1) for i in parts]
    score_grads = [
        ((x - delta) * (share * FACTOR)).astype(jnp.bfloat16) * exponent
        for x, delta, share, exponent in zip(prob_grads, deltas, shares, exponents)
    ]
    for i in parts:
        out_ref[:, cols[i]] = mixed[i].astype(jnp.bfloat16).T
        dq_ref[:, cols[i]] = dot(keys[i], score_grads[i], 0, 0).astype(jnp.bfloat16).T
        terms = (
            dot(score_grads[i], q_ref[:, cols[i]], 1, 0),
            dot(exponents[i], (flips[i] * shares[i]).astype(jnp.bfloat16), 1, 1),
        )
        for index, term in enumerate(terms):
            far_grad_ref[index, :, cols[i]] = term[:rows].astype(jnp.bfloat16)
            own_grad_ref[index, :, cols[i]] = term[rows : 2 * rows]
            near_grad_ref[index, :, cols[i]] = term[2 * rows : 3 * rows].astype(jnp.bfloat16)
            null_sum[pl.ds(index * HEADS + step * PER_STEP + i, 1), :] = term[3 * rows : 3 * rows + 1]

    @pl.when(step == STEPS - 1)
    def _():
        null_grad_ref[...] = jnp.broadcast_to(
            null_sum[...].astype(jnp.bfloat16)[None], null_grad_ref.shape
        )


def block(*lead):
    return pl.BlockSpec((*lead, WIDE), lambda i: (0,) * len(lead) + (i,))


def whole(shape):
    return pl.BlockSpec(shape, lambda i: (0,) * len(shape))


def heads_call(q, g, far, own, near, null_rows, bias, valid, peers):
    video_rows, width = q.shape
    audio_rows = video_rows // 2
    wide = jax.ShapeDtypeStruct((video_rows, width), jnp.bfloat16)
    terms = [
        jax.ShapeDtypeStruct((2, audio_rows, width), dtype)
        for dtype in (jnp.bfloat16, jnp.float32, jnp.bfloat16)
    ]
    null_shape = (peers, 2 * HEADS, HEAD)
    return pl.pallas_call(
        heads_kernel,
        grid=(STEPS,),
        in_specs=[block(video_rows)] * 5
        + [
            pl.BlockSpec((PER_STEP, *null_rows.shape[1:]), lambda i: (i, 0, 0, 0)),
            whole(bias.shape),
            whole(valid.shape),
        ],
        out_specs=[block(video_rows)] * 2 + [block(2, audio_rows)] * 3 + [whole(null_shape)],
        out_shape=[wide, wide, *terms, jax.ShapeDtypeStruct(null_shape, jnp.bfloat16)],
        scratch_shapes=[pltpu.VMEM((2 * HEADS, HEAD), jnp.float32)],
        compiler_params=pltpu.CompilerParams(vmem_limit_bytes=VMEM_LIMIT),
        cost_estimate=pl.CostEstimate(
            flops=12 * bias.size * width, bytes_accessed=9_000_000, transcendentals=bias.size * HEADS
        ),
        name="heads",
    )(q, g, far, own, near, null_rows, bias, valid)


def sum_peers(parts):
    return jnp.sum(parts.astype(jnp.float32), axis=0)


def body(video_query, audio_key, audio_value, null_kv, audio_keep, clip_lengths, out_grad):
    audio_rows = audio_key.shape[0]
    video_rows = video_query.shape[0]
    shards = lax.axis_size(SEQ)
    seq_index = lax.axis_index(SEQ)
    total_audio = audio_rows * shards

    stacked = stack_call(audio_key, audio_value)
    far = swap_link(stacked)

    bounds = jnp.cumsum(clip_lengths[0])
    pad_segment = clip_lengths.shape[1] - 1
    query_pos = seq_index * video_rows + jnp.arange(video_rows, dtype=jnp.int32)
    side = 1 - 2 * (seq_index % 2)
    starts = [(seq_index + move) * audio_rows for move in (-side, 0, side)]
    own_pos = jnp.arange(audio_rows, dtype=jnp.int32)
    key_pos = jnp.concatenate([start + own_pos for start in starts])
    keep_padded = jnp.pad(audio_keep, (audio_rows, audio_rows))
    keep_rows = jnp.concatenate(
        [lax.dynamic_slice_in_dim(keep_padded, start + audio_rows, audio_rows) for start in starts]
    )
    allowed = allowed_pairs(
        query_pos, key_pos, bounds, keep_rows, total_audio, pad_segment, audio_rows
    )
    null_allowed = jnp.arange(NULL_ROWS) == 0
    bias = jnp.where(
        jnp.concatenate([allowed, jnp.broadcast_to(null_allowed[:, None], (NULL_ROWS, video_rows))]),
        0.0,
        MASKED,
    ).astype(jnp.float32)
    valid = (segment_of(query_pos // 2, bounds) < pad_segment).astype(jnp.float32)[None]
    null_heads = null_kv.reshape(2, HEADS, 1, HEAD).swapaxes(0, 1)
    null_rows = jnp.pad(null_heads, ((0, 0), (0, 0), (0, NULL_ROWS - 1), (0, 0)))

    stacked, valid = lax.optimization_barrier((stacked, valid))
    near = swap_chip(stacked)

    wide_axes, deep_axes = ("yh", "yl", "x"), ("z", "core")
    attended, query_grad, far_grad, own_grad, near_grad, null_copies = heads_call(
        video_query, out_grad, far, stacked, near, null_rows, bias, valid, lax.axis_size(wide_axes)
    )
    far_back = swap_link(far_grad)
    first = lax.all_to_all(null_copies, wide_axes, 0, 0)
    partial = sum_peers(first).astype(jnp.bfloat16)
    copies = jnp.broadcast_to(partial[None], (lax.axis_size(deep_axes), *partial.shape))
    copies, near_grad = lax.optimization_barrier((copies, near_grad))
    second = lax.all_to_all(copies, deep_axes, 0, 0)
    near_back = swap_chip(near_grad)
    grads = [
        (own_grad[i] + far_back[i].astype(jnp.float32) + near_back[i].astype(jnp.float32)).astype(
            jnp.bfloat16
        )
        for i in range(2)
    ]
    second, *grads = lax.optimization_barrier((second, *grads))
    null_grad = sum_peers(second).reshape(null_kv.shape)
    return (attended, query_grad, grads[0], grads[1], null_grad)


def solution(mesh):
    parts = CLIP_PARTS + SEQ_PARTS
    fine = Mesh(
        np.asarray(mesh.devices).reshape([size for _, size in parts]), [name for name, _ in parts]
    )
    rows = P(CLIP + SEQ, None)
    return jax.shard_map(
        body,
        mesh=fine,
        in_specs=(rows, rows, rows, P(), P(CLIP), P(CLIP, None), rows),
        out_specs=(rows, rows, rows, rows, P()),
        check_vma=False,
    )
```

time: 78.2 us -> 72.3 us (0.925)
  Pallas kernels: 16.1 us -> 10.2 us
    pallas_call x1, Pallas kernels: 14.1 us -> 8.19 us  [heads_call(): pl.pallas_call(heads_kernel, grid=(STEPS,), in_specs=[block(video_rows)]...]
  transfers between devices with their start and end apart: 6 -> 6, of which waited for: 3 -> 3; matrix products, arithmetic and copies ran while one was open for 8% -> 9% of each run, Pallas kernels for 0% -> 0%
where the time goes in v2:
time: 72.3 us; the launch traced here: 71.8 us
  starting transfers between devices  36.1 us (50%)
  waiting for transfers between devices  17 us (24%)
  Pallas kernels  10.2 us (14%)
  other arithmetic  4.77 us (7%)
  local copies, waits for them, and re-layouts  2.87 us (4%)
  between operations  0.85 us (1%)
    all_to_all x1, starting transfers between devices, body(): first = lax.all_to_all(null_copies, wide_axes, 0, 0)  11.5 us
    all_to_all x1, starting transfers between devices, body(): second = lax.all_to_all(copies, deep_axes, 0, 0)  10.8 us
    all_to_all x1, waiting for transfers between devices, body(): first = lax.all_to_all(null_copies, wide_axes, 0, 0)  9.2 us
    pallas_call x1, Pallas kernels, heads_call(): pl.pallas_call(heads_kernel, grid=(STEPS,), in_specs=[block(video_rows)]...  8.19 us
    ppermute x2, starting transfers between devices, swap_link(): return lax.ppermute(block, SEQ, pairs + [(b, a) for a, b in pairs])  6.93 us
    ppermute x2, starting transfers between devices, swap_chip(): return lax.ppermute(block, SEQ, [(i, i ^ 1) for i in range(count)])  6.88 us
    all_to_all x1, waiting for transfers between devices, body(): second = lax.all_to_all(copies, deep_axes, 0, 0)  5.94 us
    convert_element_type x1, other arithmetic, body(): (own_grad[i] + far_back[i].astype(jnp.float32) + near_back[i].astype(jnp....  2.53 us
  transfers between devices with their start and end apart: 6, of which 3 were waited for; matrix products, arithmetic and copies ran while one was open for 9% of the time, Pallas kernels for 0%

profile of v2, /device:TPU:1, one launch (start us, length us, event | category | flops | bytes accessed | tf_op | source)
XLA Modules:
  0.0 71.8 jit_solution(1513898960062197574)
XLA Ops:
  0.6 0.0 copy-start.4
  0.6 0.0 copy-start.1
  0.7 0.0 copy-start
  0.7 2.0 %stack.1.own_ref = bf16[256,1536]{1,0:T(8,128)(2,1)} custom-call(bf16[128,1536]{1,0:T(8,128)(2,1)} %key_ref.1, bf16[128,1536]{1,0:T(8,128)(2,1)} %value_ref.1), custom_call_target="tpu_custom_call" | custom-call | tf_op jit(solution)/shard_map/stack/pallas_call | solution.py:89
  2.6 4.5 %collective-permute-start = (bf16[256,1536]{1,0:T(8,128)(2,1)}, bf16[256,1536]{1,0:T(8,128)(2,1)S(1)}, u32[]{:S(2)}, u32[]{:S(2)}) collective-permute-start(bf16[256,1536]{1,0:T(8,128)(2,1)} %stack.1.own_ref), channel_id=1, source_target_pairs={{1,2},{3,4},{5,6},{7,8},{9,10},{11,12},{13,14},{15,16},{17,18},{19... | collective-permute-start | bytes 2359304 | tf_op jit(solution)/shard_map/ppermute | solution.py:35
  7.2 0.0 copy-done.4
  7.2 0.2 reduce-window.4
  7.4 0.1 convert_reduce_fusion.2
  7.5 0.6 compare_convert_fusion
  8.0 5.0 %collective-permute-start.1 = (bf16[256,1536]{1,0:T(8,128)(2,1)}, bf16[256,1536]{1,0:T(8,128)(2,1)S(1)}, u32[]{:S(2)}, u32[]{:S(2)}) collective-permute-start(bf16[256,1536]{1,0:T(8,128)(2,1)} %stack.1.own_ref), channel_id=1, source_target_pairs={{0,1},{1,0},{2,3},{3,2},{4,5},{5,4},{6,7},{7,6},{8,9},{9,8},{10,11... | collective-permute-start | bytes 2359304 | tf_op jit(solution)/shard_map/ppermute | solution.py:29
  13.1 0.0 copy-done.1
  13.1 0.7 pad.8.null_ref
  13.8 0.0 copy-done
  13.8 0.1 pad_dynamic-slice_fusion.2
  13.9 0.1 convert_reduce_fusion.1
  14.0 0.2 fusion.2
  14.2 0.9 %add_select_fusion.bias_ref = f32[400,256]{1,0:T(8,128)} fusion(pred[384,256]{1,0:T(8,128)(4,1)S(1)} %fusion.2, pred[400]{0:T(512)(128)(4,1)S(1)} %pad.11.clone), kind=kLoop, calls=%fused_computation.2 | loop fusion | flops 204800 | bytes 508304 | tf_op jit(solution)/shard_map/jit(_where)/select_n | solution.py:221
  15.1 0.0 collective-permute-done.1.near_ref
  15.1 0.0 copy-start.3
  15.1 1.9 %collective-permute-done.far_ref = bf16[256,1536]{1,0:T(8,128)(2,1)S(1)} collective-permute-done((bf16[256,1536]{1,0:T(8,128)(2,1)}, bf16[256,1536]{1,0:T(8,128)(2,1)S(1)}, u32[]{:S(2)}, u32[]{:S(2)}) %collective-permute-start) | collective-permute-done | bytes 786464 | tf_op jit(solution)/shard_map/ppermute | solution.py:35
  17.0 0.0 copy-done.3
  17.0 0.0 copy-start.2
  17.0 0.9 %copy-done.2 = bf16[256,1536]{1,0:T(8,128)(2,1)} copy-done((bf16[256,1536]{1,0:T(8,128)(2,1)}, bf16[256,1536]{1,0:T(8,128)(2,1)S(1)}, u32[]{:S(2)}) %copy-start.2) | copy-done | bytes 786456
  17.9 8.2 %heads.1 = (bf16[256,1536]{1,0:T(8,128)(2,1)}, bf16[256,1536]{1,0:T(8,128)(2,1)}, bf16[2,128,1536]{2,1,0:T(8,128)(2,1)}, f32[2,128,1536]{2,1,0:T(8,128)}, bf16[2...) custom-call(bf16[256,1536]{1,0:T(8,128)(2,1)} %q_ref.1, bf16[256,1536]{1,0:T(8,128)(2,1)} %g_ref.1, ...), custom_call_target="tpu_custom_call" | custom-call | flops 1887436800 | bytes 9000000 | tf_op jit(solution)/shard_map/heads/pallas_call | solution.py:172
  26.1 11.5 %all-to-all-start = ((bf16[32,24,128]{2,1,0:T(8,128)(2,1)}), bf16[32,24,128]{2,1,0:T(8,128)(2,1)S(1)}, u32[]{:S(2)}, u32[]{:S(2)}) async-start(bf16[32,24,128]{2,1,0:T(8,128)(2,1)} %get-tuple-element.22), calls=%async_computation | async-start | bytes 393216 | tf_op jit(solution)/shard_map/all_to_all | solution.py:238
  37.6 2.4 %collective-permute-start.2 = (bf16[2,128,1536]{2,1,0:T(8,128)(2,1)}, bf16[2,128,1536]{2,1,0:T(8,128)(2,1)S(1)}, u32[]{:S(2)}, u32[]{:S(2)}) collective-permute-start(bf16[2,128,1536]{2,1,0:T(8,128)(2,1)} %get-tuple-element.26), channel_id=1, source_target_pairs={{1,2},{3,4},{5,6},{7,8},{9,10},{11,12},{13,14},{15,16},{17,18},{19... | collective-permute-start | bytes 2359304 | tf_op jit(solution)/shard_map/ppermute | solution.py:35
  40.1 9.2 %all-to-all-done = bf16[32,24,128]{2,1,0:T(8,128)(2,1)S(1)} async-done(((bf16[32,24,128]{2,1,0:T(8,128)(2,1)}), bf16[32,24,128]{2,1,0:T(8,128)(2,1)S(1)}, u32[]{:S(2)}, u32[]{:S(2)}) %all-to-all-start) | async-done | bytes 196640 | tf_op jit(solution)/shard_map/all_to_all | solution.py:238
  49.3 0.7 broadcast_in_dim.13
  49.9 1.9 %collective-permute-start.3 = (bf16[2,128,1536]{2,1,0:T(8,128)(2,1)}, bf16[2,128,1536]{2,1,0:T(8,128)(2,1)S(1)}, u32[]{:S(2)}, u32[]{:S(2)}) collective-permute-start(bf16[2,128,1536]{2,1,0:T(8,128)(2,1)} %get-tuple-element.27), channel_id=1, source_target_pairs={{0,1},{1,0},{2,3},{3,2},{4,5},{5,4},{6,7},{7,6},{8,9},{9,8},{10,11... | collective-permute-start | bytes 2359304 | tf_op jit(solution)/shard_map/ppermute | solution.py:29
  51.9 10.8 %all-to-all-start.1 = ((bf16[16,24,128]{2,1,0:T(8,128)(2,1)}), bf16[16,24,128]{2,1,0:T(8,128)(2,1)S(1)}, u32[]{:S(2)}, u32[]{:S(2)}) async-start(bf16[16,24,128]{2,1,0:T(8,128)(2,1)} %broadcast_in_dim.13), calls=%async_computation.1 | async-start | bytes 196608 | tf_op jit(solution)/shard_map/all_to_all | solution.py:242
  62.7 0.0 collective-permute-done.2
  62.7 0.0 collective-permute-done.3
  62.7 2.5 %fusion.1 = (bf16[128,1536]{1,0:T(8,128)(2,1)}, bf16[128,1536]{1,0:T(8,128)(2,1)}) fusion(f32[2,128,1536]{2,1,0:T(8,128)} %get-tuple-element.25, bf16[2,128,1536]{2,1,0:T(8,128)(2,1)S(1)} %collective-permute-done.3, bf16[2,128,1536]{2,1,0:T(8,128)(2,1)S(1)} %collective-permute-done.2), kind=kLoop, calls=%fused_computation.4 | loop fusion | flops 1966080 | bytes 3932160 | tf_op jit(solution)/shard_map/convert_element_type | solution.py:245
  65.2 5.9 %all-to-all-done.1 = bf16[16,24,128]{2,1,0:T(8,128)(2,1)S(1)} async-done(((bf16[16,24,128]{2,1,0:T(8,128)(2,1)}), bf16[16,24,128]{2,1,0:T(8,128)(2,1)S(1)}, u32[]{:S(2)}, u32[]{:S(2)}) %all-to-all-start.1) | async-done | bytes 98336 | tf_op jit(solution)/shard_map/all_to_all | solution.py:242
  71.2 0.6 reshape.173
  (11 shorter events, 0.1 us)
Async XLA Ops:
  0.6 6.5 %copy-start.4 = (s32[1,4]{1,0:T(1,128)S(1)}, s32[1,4]{1,0:T(1,128)}, u32[]{:S(2)}) copy-start(s32[1,4]{1,0:T(1,128)} %param.12) | copy-start | bytes 52
  0.6 12.4 %copy-start.1 = (bf16[2,1536]{1,0:T(2,128)(2,1)S(1)}, bf16[2,1536]{1,0:T(2,128)(2,1)}, u32[]{:S(2)}) copy-start(bf16[2,1536]{1,0:T(2,128)(2,1)} %param.10) | copy-start | bytes 18436
  0.7 13.1 %copy-start = (s32[4096]{0:T(1024)S(1)}, s32[4096]{0:T(1024)}, u32[]{:S(2)}) copy-start(s32[4096]{0:T(1024)} %param.11) | copy-start | bytes 49156
  2.6 14.4 %collective-permute-start = (bf16[256,1536]{1,0:T(8,128)(2,1)}, bf16[256,1536]{1,0:T(8,128)(2,1)S(1)}, u32[]{:S(2)}, u32[]{:S(2)}) collective-permute-start(bf16[256,1536]{1,0:T(8,128)(2,1)} %stack.1.own_ref), channel_id=1, source_target_pairs={{1,2},{3,4},{5,6},{7,8},{9,10},{11,12},{13,14},{15,16},{17,18},{19... | collective-permute-start | bytes 2359304 | tf_op jit(solution)/shard_map/ppermute | solution.py:35
  8.0 7.1 %collective-permute-start.1 = (bf16[256,1536]{1,0:T(8,128)(2,1)}, bf16[256,1536]{1,0:T(8,128)(2,1)S(1)}, u32[]{:S(2)}, u32[]{:S(2)}) collective-permute-start(bf16[256,1536]{1,0:T(8,128)(2,1)} %stack.1.own_ref), channel_id=1, source_target_pairs={{0,1},{1,0},{2,3},{3,2},{4,5},{5,4},{6,7},{7,6},{8,9},{9,8},{10,11... | collective-permute-start | bytes 2359304 | tf_op jit(solution)/shard_map/ppermute | solution.py:29
  15.1 1.9 %copy-start.3 = (bf16[256,1536]{1,0:T(8,128)(2,1)}, bf16[256,1536]{1,0:T(8,128)(2,1)S(1)}, u32[]{:S(2)}) copy-start(bf16[256,1536]{1,0:T(8,128)(2,1)S(1)} %collective-permute-done.1.near_ref) | copy-start | bytes 2359300
  17.0 0.9 %copy-start.2 = (bf16[256,1536]{1,0:T(8,128)(2,1)}, bf16[256,1536]{1,0:T(8,128)(2,1)S(1)}, u32[]{:S(2)}) copy-start(bf16[256,1536]{1,0:T(8,128)(2,1)S(1)} %collective-permute-done.far_ref) | copy-start | bytes 2359300
  26.1 23.1 %all-to-all-start = ((bf16[32,24,128]{2,1,0:T(8,128)(2,1)}), bf16[32,24,128]{2,1,0:T(8,128)(2,1)S(1)}, u32[]{:S(2)}, u32[]{:S(2)}) async-start(bf16[32,24,128]{2,1,0:T(8,128)(2,1)} %get-tuple-element.22), calls=%async_computation | async-start | bytes 393216 | tf_op jit(solution)/shard_map/all_to_all | solution.py:238
  37.6 25.1 %collective-permute-start.2 = (bf16[2,128,1536]{2,1,0:T(8,128)(2,1)}, bf16[2,128,1536]{2,1,0:T(8,128)(2,1)S(1)}, u32[]{:S(2)}, u32[]{:S(2)}) collective-permute-start(bf16[2,128,1536]{2,1,0:T(8,128)(2,1)} %get-tuple-element.26), channel_id=1, source_target_pairs={{1,2},{3,4},{5,6},{7,8},{9,10},{11,12},{13,14},{15,16},{17,18},{19... | collective-permute-start | bytes 2359304 | tf_op jit(solution)/shard_map/ppermute | solution.py:35
  49.9 12.8 %collective-permute-start.3 = (bf16[2,128,1536]{2,1,0:T(8,128)(2,1)}, bf16[2,128,1536]{2,1,0:T(8,128)(2,1)S(1)}, u32[]{:S(2)}, u32[]{:S(2)}) collective-permute-start(bf16[2,128,1536]{2,1,0:T(8,128)(2,1)} %get-tuple-element.27), channel_id=1, source_target_pairs={{0,1},{1,0},{2,3},{3,2},{4,5},{5,4},{6,7},{7,6},{8,9},{9,8},{10,11... | collective-permute-start | bytes 2359304 | tf_op jit(solution)/shard_map/ppermute | solution.py:29
  51.9 19.3 %all-to-all-start.1 = ((bf16[16,24,128]{2,1,0:T(8,128)(2,1)}), bf16[16,24,128]{2,1,0:T(8,128)(2,1)S(1)}, u32[]{:S(2)}, u32[]{:S(2)}) async-start(bf16[16,24,128]{2,1,0:T(8,128)(2,1)} %broadcast_in_dim.13), calls=%async_computation.1 | async-start | bytes 196608 | tf_op jit(solution)/shard_map/all_to_all | solution.py:242

commit v3 on v2

--- a/solution.py
+++ b/solution.py
@@ -19,6 +19,8 @@
 CLIP = tuple(name for name, _ in CLIP_PARTS)
 SEQ = tuple(name for name, _ in SEQ_PARTS)
 VMEM_LIMIT = 60 * 1024 * 1024
+HEADS_LIMIT = 56 * 1024 * 1024
+ADD_LIMIT = 8 * 1024 * 1024
 PER_STEP = 4
 STEPS = HEADS // PER_STEP
 WIDE = PER_STEP * HEAD
@@ -99,6 +101,26 @@
         compiler_params=pltpu.CompilerParams(vmem_limit_bytes=VMEM_LIMIT),
         name="stack",
     )(keys, values)
+
+
+def prepare_kernel(q_hbm, g_hbm, own_hbm, q_ref, g_ref, own_ref, sems):
+    pairs = ((q_hbm, q_ref), (g_hbm, g_ref), (own_hbm, own_ref))
+    copies = [pltpu.make_async_copy(a, b, sems.at[i]) for i, (a, b) in enumerate(pairs)]
+    start(copies)
+    wait(copies)
+
+
+def prepare_call(q, g, own):
+    arrays = (q, g, own)
+    return pl.pallas_call(
+        prepare_kernel,
+        in_specs=[pl.BlockSpec(memory_space=pl.ANY)] * 3,
+        out_specs=[pl.BlockSpec(memory_space=pltpu.VMEM)] * 3,
+        out_shape=[jax.ShapeDtypeStruct(x.shape, x.dtype) for x in arrays],
+        scratch_shapes=[pltpu.SemaphoreType.DMA((3,))],
+        compiler_params=pltpu.CompilerParams(vmem_limit_bytes=HEADS_LIMIT),
+        name="prepare",
+    )(*arrays)
 
 
 def gathered(refs, null_ref, cols, index):
@@ -141,7 +163,7 @@
         )
         for index, term in enumerate(terms):
             far_grad_ref[index, :, cols[i]] = term[:rows].astype(jnp.bfloat16)
-            own_grad_ref[index, :, cols[i]] = term[rows : 2 * rows]
+            own_grad_ref[index, :, cols[i]] = term[rows : 2 * rows].astype(jnp.bfloat16)
             near_grad_ref[index, :, cols[i]] = term[2 * rows : 3 * rows].astype(jnp.bfloat16)
             null_sum[pl.ds(index * HEADS + step * PER_STEP + i, 1), :] = term[3 * rows : 3 * rows + 1]
 
@@ -164,10 +186,7 @@
     video_rows, width = q.shape
     audio_rows = video_rows // 2
     wide = jax.ShapeDtypeStruct((video_rows, width), jnp.bfloat16)
-    terms = [
-        jax.ShapeDtypeStruct((2, audio_rows, width), dtype)
-        for dtype in (jnp.bfloat16, jnp.float32, jnp.bfloat16)
-    ]
+    terms = [jax.ShapeDtypeStruct((2, audio_rows, width), jnp.bfloat16)] * 3
     null_shape = (peers, 2 * HEADS, HEAD)
     return pl.pallas_call(
         heads_kernel,
@@ -181,12 +200,39 @@
         out_specs=[block(video_rows)] * 2 + [block(2, audio_rows)] * 3 + [whole(null_shape)],
         out_shape=[wide, wide, *terms, jax.ShapeDtypeStruct(null_shape, jnp.bfloat16)],
         scratch_shapes=[pltpu.VMEM((2 * HEADS, HEAD), jnp.float32)],
-        compiler_params=pltpu.CompilerParams(vmem_limit_bytes=VMEM_LIMIT),
+        compiler_params=pltpu.CompilerParams(vmem_limit_bytes=HEADS_LIMIT),
         cost_estimate=pl.CostEstimate(
             flops=12 * bias.size * width, bytes_accessed=9_000_000, transcendentals=bias.size * HEADS
         ),
         name="heads",
     )(q, g, far, own, near, null_rows, bias, valid)
+
+
+def add_kernel(a_ref, b_ref, *out_refs):
+    total = a_ref[...].astype(jnp.float32) + b_ref[...].astype(jnp.float32)
+    if len(out_refs) == 1:
+        out_refs[0][...] = total.astype(jnp.bfloat16)
+    else:
+        for i, ref in enumerate(out_refs):
+            ref[...] = total[i].astype(jnp.bfloat16)
+
+
+def add_call(a, b, split, work, name):
+    _, rows, width = a.shape
+    steps = 3
+    both = pl.BlockSpec((2, rows, width // steps), lambda i: (0, 0, i))
+    one = pl.BlockSpec((rows, width // steps), lambda i: (0, i))
+    single = jax.ShapeDtypeStruct((rows, width), jnp.bfloat16)
+    return pl.pallas_call(
+        add_kernel,
+        grid=(steps,),
+        in_specs=[both, both],
+        out_specs=[one, one] if split else both,
+        out_shape=[single, single] if split else jax.ShapeDtypeStruct(a.shape, jnp.bfloat16),
+        compiler_params=pltpu.CompilerParams(vmem_limit_bytes=ADD_LIMIT),
+        cost_estimate=pl.CostEstimate(flops=a.size, bytes_accessed=work, transcendentals=0),
+        name=name,
+    )(a, b)
 
 
 def sum_peers(parts):
@@ -231,8 +277,9 @@
     near = swap_chip(stacked)
 
     wide_axes, deep_axes = ("yh", "yl", "x"), ("z", "core")
+    q_held, g_held, own = prepare_call(video_query, out_grad, stacked)
     attended, query_grad, far_grad, own_grad, near_grad, null_copies = heads_call(
-        video_query, out_grad, far, stacked, near, null_rows, bias, valid, lax.axis_size(wide_axes)
+        q_held, g_held, far, own, near, null_rows, bias, valid, lax.axis_size(wide_axes)
     )
     far_back = swap_link(far_grad)
     first = lax.all_to_all(null_copies, wide_axes, 0, 0)
@@ -241,12 +288,8 @@
     copies, near_grad = lax.optimization_barrier((copies, near_grad))
     second = lax.all_to_all(copies, deep_axes, 0, 0)
     near_back = swap_chip(near_grad)
-    grads = [
-        (own_grad[i] + far_back[i].astype(jnp.float32) + near_back[i].astype(jnp.float32)).astype(
-            jnp.bfloat16
-        )
-        for i in range(2)
-    ]
+    part = add_call(own_grad, far_back, False, 40_000_000, "add_far")
+    grads = add_call(part, near_back, True, 2_400_000, "add_near")
     second, *grads = lax.optimization_barrier((second, *grads))
     null_grad = sum_peers(second).reshape(null_kv.shape)
     return (attended, query_grad, grads[0], grads[1], null_grad)

time: 72.3 us -> 72.3 us (level)
  Pallas kernels: 10.2 us -> 15.1 us
  other arithmetic: 4.77 us -> 2.23 us
  starting transfers between devices: 36.1 us -> 33.6 us
  local copies, waits for them, and re-layouts: 2.87 us -> 4.41 us
  waiting for transfers between devices: 17 us -> 15.7 us
    pallas_call x0 -> x3, Pallas kernels: none -> 5.03 us  [the longest x1 3.05 us: prepare_call(): pl.pallas_call(prepare_kernel, in_specs=[pl.BlockSpec(memory_space=pl.ANY...]
    all_to_all x1, starting transfers between devices: 11.5 us -> 8.92 us  [body(): first = lax.all_to_all(null_copies, wide_axes, 0, 0)]
    convert_element_type x1 -> x0, other arithmetic: 2.53 us -> none  [body(): (own_grad[i] + far_back[i].astype(jnp.float32) + near_back[i].astype(jnp....]
    ppermute x2, waiting for transfers between devices: 1.88 us -> 0.01 us  [swap_link(): return lax.ppermute(block, SEQ, pairs + [(b, a) for a, b in pairs])]
    unnamed x10 -> x12, local copies, waits for them, and re-layouts: 0.91 us -> 2.44 us
  transfers between devices with their start and end apart: 6 -> 6, of which waited for: 3 -> 2; matrix products, arithmetic and copies ran while one was open for 9% -> 5% of each run, Pallas kernels for 0% -> 7%
where the time goes in v3:
time: 72.3 us; the launch traced here: 71.8 us
  starting transfers between devices  33.6 us (46%)
  waiting for transfers between devices  15.7 us (22%)
  Pallas kernels  15.1 us (21%)
  local copies, waits for them, and re-layouts  4.41 us (6%)
  other arithmetic  2.23 us (3%)
  between operations  0.86 us (1%)
    all_to_all x1, starting transfers between devices, body(): second = lax.all_to_all(copies, deep_axes, 0, 0)  10.8 us
    all_to_all x1, waiting for transfers between devices, body(): first = lax.all_to_all(null_copies, wide_axes, 0, 0)  9.2 us
    all_to_all x1, starting transfers between devices, body(): first = lax.all_to_all(null_copies, wide_axes, 0, 0)  8.92 us
    pallas_call x1, Pallas kernels, heads_call(): pl.pallas_call(heads_kernel, grid=(STEPS,), in_specs=[block(video_rows)]...  8.1 us
    ppermute x2, starting transfers between devices, swap_link(): return lax.ppermute(block, SEQ, pairs + [(b, a) for a, b in pairs])  6.91 us
    ppermute x2, starting transfers between devices, swap_chip(): return lax.ppermute(block, SEQ, [(i, i ^ 1) for i in range(count)])  6.88 us
    all_to_all x1, waiting for transfers between devices, body(): second = lax.all_to_all(copies, deep_axes, 0, 0)  6.47 us
    pallas_call x1, Pallas kernels, prepare_call(): pl.pallas_call(prepare_kernel, in_specs=[pl.BlockSpec(memory_space=pl.ANY...  3.05 us
  transfers between devices with their start and end apart: 6, of which 2 were waited for; matrix products, arithmetic and copies ran while one was open for 5% of the time, Pallas kernels for 7%

profile of v3, /device:TPU:1, one launch (start us, length us, event | category | flops | bytes accessed | tf_op | source)
XLA Modules:
  0.0 71.8 jit_solution(18301440456893713178)
XLA Ops:
  0.6 2.0 %stack.1.own_hbm = bf16[256,1536]{1,0:T(8,128)(2,1)} custom-call(bf16[128,1536]{1,0:T(8,128)(2,1)} %key_ref.1, bf16[128,1536]{1,0:T(8,128)(2,1)} %value_ref.1), custom_call_target="tpu_custom_call" | custom-call | tf_op jit(solution)/shard_map/stack/pallas_call | solution.py:91
  2.6 4.5 %collective-permute-start = (bf16[256,1536]{1,0:T(8,128)(2,1)}, bf16[256,1536]{1,0:T(8,128)(2,1)S(1)}, u32[]{:S(2)}, u32[]{:S(2)}) collective-permute-start(bf16[256,1536]{1,0:T(8,128)(2,1)} %stack.1.own_hbm), channel_id=1, source_target_pairs={{1,2},{3,4},{5,6},{7,8},{9,10},{11,12},{13,14},{15,16},{17,18},{19... | collective-permute-start | bytes 2359304 | tf_op jit(solution)/shard_map/ppermute | solution.py:37
  7.1 0.0 copy-start.5
  7.1 0.6 copy-done.5
  7.8 0.2 reduce-window.4
  8.0 0.1 convert_reduce_fusion.2
  8.1 0.6 compare_convert_fusion
  8.6 5.0 %collective-permute-start.1 = (bf16[256,1536]{1,0:T(8,128)(2,1)}, bf16[256,1536]{1,0:T(8,128)(2,1)S(1)}, u32[]{:S(2)}, u32[]{:S(2)}) collective-permute-start(bf16[256,1536]{1,0:T(8,128)(2,1)} %stack.1.own_hbm), channel_id=1, source_target_pairs={{0,1},{1,0},{2,3},{3,2},{4,5},{5,4},{6,7},{7,6},{8,9},{9,8},{10,11... | collective-permute-start | bytes 2359304 | tf_op jit(solution)/shard_map/ppermute | solution.py:31
  13.6 0.0 copy-start.2
  13.7 0.6 copy-done.2
  14.4 0.7 pad.8.null_ref
  15.1 0.0 copy-start.1
  15.1 3.0 %prepare.1 = (bf16[256,1536]{1,0:T(8,128)(2,1)}, bf16[256,1536]{1,0:T(8,128)(2,1)}, bf16[256,1536]{1,0:T(8,128)(2,1)}) custom-call(bf16[256,1536]{1,0:T(8,128)(2,1)} %q_hbm.1, bf16[256,1536]{1,0:T(8,128)(2,1)} %g_hbm.1, bf16[256,1536]{1,0:T(8,128)(2,1)} %stack.1.own_hbm), custom_call_target="tpu_custom_call" | custom-call | tf_op jit(solution)/shard_map/prepare/pallas_call | solution.py:115
  18.1 0.0 copy-done.1
  18.1 0.1 pad_dynamic-slice_fusion.2
  18.2 0.1 convert_reduce_fusion.1
  18.3 0.2 fusion
  18.6 0.9 %add_select_fusion.bias_ref = f32[400,256]{1,0:T(8,128)} fusion(pred[384,256]{1,0:T(8,128)(4,1)S(1)} %fusion, pred[400]{0:T(512)(128)(4,1)S(1)} %pad.11.clone), kind=kLoop, calls=%fused_computation | loop fusion | flops 204800 | bytes 508304 | tf_op jit(solution)/shard_map/jit(_where)/select_n | solution.py:267
  19.5 0.0 collective-permute-done.1.near_ref
  19.5 0.0 copy-start.4
  19.5 0.0 collective-permute-done.far_ref
  19.5 0.0 copy-start.3
  19.5 0.9 %copy-done.4 = bf16[256,1536]{1,0:T(8,128)(2,1)} copy-done((bf16[256,1536]{1,0:T(8,128)(2,1)}, bf16[256,1536]{1,0:T(8,128)(2,1)S(1)}, u32[]{:S(2)}) %copy-start.4) | copy-done | bytes 786456
  20.3 0.3 copy-done.3
  20.6 8.1 %heads.1 = (bf16[256,1536]{1,0:T(8,128)(2,1)}, bf16[256,1536]{1,0:T(8,128)(2,1)}, bf16[2,128,1536]{2,1,0:T(8,128)(2,1)}, bf16[2,128,1536]{2,1,0:T(8,128)(2,1)}, ...) custom-call(bf16[256,1536]{1,0:T(8,128)(2,1)} %get-tuple-element.24.q_ref, ...), custom_call_target="tpu_custom_call" | custom-call | flops 1887436800 | bytes 9000000 | tf_op jit(solution)/shard_map/heads/pallas_call | solution.py:191
  28.7 0.0 copy-start
  28.7 8.9 %all-to-all-start = ((bf16[32,24,128]{2,1,0:T(8,128)(2,1)}), bf16[32,24,128]{2,1,0:T(8,128)(2,1)S(1)}, u32[]{:S(2)}, u32[]{:S(2)}) async-start(bf16[32,24,128]{2,1,0:T(8,128)(2,1)} %get-tuple-element.30), calls=%async_computation | async-start | bytes 393216 | tf_op jit(solution)/shard_map/all_to_all | solution.py:285
  37.7 2.4 %collective-permute-start.2 = (bf16[2,128,1536]{2,1,0:T(8,128)(2,1)}, bf16[2,128,1536]{2,1,0:T(8,128)(2,1)S(1)}, u32[]{:S(2)}, u32[]{:S(2)}) collective-permute-start(bf16[2,128,1536]{2,1,0:T(8,128)(2,1)} %get-tuple-element.34), channel_id=1, source_target_pairs={{1,2},{3,4},{5,6},{7,8},{9,10},{11,12},{13,14},{15,16},{17,18},{19... | collective-permute-start | bytes 2359304 | tf_op jit(solution)/shard_map/ppermute | solution.py:37
  40.1 9.2 %all-to-all-done = bf16[32,24,128]{2,1,0:T(8,128)(2,1)S(1)} async-done(((bf16[32,24,128]{2,1,0:T(8,128)(2,1)}), bf16[32,24,128]{2,1,0:T(8,128)(2,1)S(1)}, u32[]{:S(2)}, u32[]{:S(2)}) %all-to-all-start) | async-done | bytes 196640 | tf_op jit(solution)/shard_map/all_to_all | solution.py:285
  49.3 0.7 broadcast_in_dim.13
  50.0 1.9 %collective-permute-start.3 = (bf16[2,128,1536]{2,1,0:T(8,128)(2,1)}, bf16[2,128,1536]{2,1,0:T(8,128)(2,1)S(1)}, u32[]{:S(2)}, u32[]{:S(2)}) collective-permute-start(bf16[2,128,1536]{2,1,0:T(8,128)(2,1)} %get-tuple-element.35), channel_id=1, source_target_pairs={{0,1},{1,0},{2,3},{3,2},{4,5},{5,4},{6,7},{7,6},{8,9},{9,8},{10,11... | collective-permute-start | bytes 2359304 | tf_op jit(solution)/shard_map/ppermute | solution.py:31
  51.9 10.8 %all-to-all-start.1 = ((bf16[16,24,128]{2,1,0:T(8,128)(2,1)}), bf16[16,24,128]{2,1,0:T(8,128)(2,1)S(1)}, u32[]{:S(2)}, u32[]{:S(2)}) async-start(bf16[16,24,128]{2,1,0:T(8,128)(2,1)} %broadcast_in_dim.13), calls=%async_computation.1 | async-start | bytes 196608 | tf_op jit(solution)/shard_map/all_to_all | solution.py:289
  62.7 0.0 collective-permute-done.2.b_ref
  62.7 0.0 copy-done
  62.7 0.4 add_far.1.a_ref
  63.2 0.0 collective-permute-done.3.b_ref
  63.2 1.6 %add_near.1 = (bf16[128,1536]{1,0:T(8,128)(2,1)}, bf16[128,1536]{1,0:T(8,128)(2,1)}) custom-call(bf16[2,128,1536]{2,1,0:T(8,128)(2,1)S(1)} %add_far.1.a_ref, bf16[2,128,1536]{2,1,0:T(8,128)(2,1)S(1)} %collective-permute-done.3.b_ref), custom_call_target="tpu_custom_call" | custom-call | flops 393216 | bytes 2400000 | tf_op jit(solution)/shard_map/add_near/pallas_call | solution.py:226
  64.7 6.5 %all-to-all-done.1 = bf16[16,24,128]{2,1,0:T(8,128)(2,1)S(1)} async-done(((bf16[16,24,128]{2,1,0:T(8,128)(2,1)}), bf16[16,24,128]{2,1,0:T(8,128)(2,1)S(1)}, u32[]{:S(2)}, u32[]{:S(2)}) %all-to-all-start.1) | async-done | bytes 98336 | tf_op jit(solution)/shard_map/all_to_all | solution.py:289
  71.2 0.6 reshape.163
  (11 shorter events, 0.1 us)
Async XLA Ops:
  2.6 16.9 %collective-permute-start = (bf16[256,1536]{1,0:T(8,128)(2,1)}, bf16[256,1536]{1,0:T(8,128)(2,1)S(1)}, u32[]{:S(2)}, u32[]{:S(2)}) collective-permute-start(bf16[256,1536]{1,0:T(8,128)(2,1)} %stack.1.own_hbm), channel_id=1, source_target_pairs={{1,2},{3,4},{5,6},{7,8},{9,10},{11,12},{13,14},{15,16},{17,18},{19... | collective-permute-start | bytes 2359304 | tf_op jit(solution)/shard_map/ppermute | solution.py:37
  7.1 0.7 copy-start.5
  8.6 10.8 %collective-permute-start.1 = (bf16[256,1536]{1,0:T(8,128)(2,1)}, bf16[256,1536]{1,0:T(8,128)(2,1)S(1)}, u32[]{:S(2)}, u32[]{:S(2)}) collective-permute-start(bf16[256,1536]{1,0:T(8,128)(2,1)} %stack.1.own_hbm), channel_id=1, source_target_pairs={{0,1},{1,0},{2,3},{3,2},{4,5},{5,4},{6,7},{7,6},{8,9},{9,8},{10,11... | collective-permute-start | bytes 2359304 | tf_op jit(solution)/shard_map/ppermute | solution.py:31
  13.6 0.7 copy-start.2
  15.1 3.1 %copy-start.1 = (s32[4096]{0:T(1024)S(1)}, s32[4096]{0:T(1024)}, u32[]{:S(2)}) copy-start(s32[4096]{0:T(1024)} %param.11) | copy-start | bytes 49156
  19.5 0.9 %copy-start.4 = (bf16[256,1536]{1,0:T(8,128)(2,1)}, bf16[256,1536]{1,0:T(8,128)(2,1)S(1)}, u32[]{:S(2)}) copy-start(bf16[256,1536]{1,0:T(8,128)(2,1)S(1)} %collective-permute-done.1.near_ref) | copy-start | bytes 2359300
  19.5 1.1 %copy-start.3 = (bf16[256,1536]{1,0:T(8,128)(2,1)}, bf16[256,1536]{1,0:T(8,128)(2,1)S(1)}, u32[]{:S(2)}) copy-start(bf16[256,1536]{1,0:T(8,128)(2,1)S(1)} %collective-permute-done.far_ref) | copy-start | bytes 2359300
  28.7 34.0 %copy-start = (bf16[2,128,1536]{2,1,0:T(8,128)(2,1)S(1)}, bf16[2,128,1536]{2,1,0:T(8,128)(2,1)}, u32[]{:S(2)}) copy-start(bf16[2,128,1536]{2,1,0:T(8,128)(2,1)} %get-tuple-element.33.a_ref) | copy-start | bytes 2359300
  28.7 20.5 %all-to-all-start = ((bf16[32,24,128]{2,1,0:T(8,128)(2,1)}), bf16[32,24,128]{2,1,0:T(8,128)(2,1)S(1)}, u32[]{:S(2)}, u32[]{:S(2)}) async-start(bf16[32,24,128]{2,1,0:T(8,128)(2,1)} %get-tuple-element.30), calls=%async_computation | async-start | bytes 393216 | tf_op jit(solution)/shard_map/all_to_all | solution.py:285
  37.7 25.1 %collective-permute-start.2 = (bf16[2,128,1536]{2,1,0:T(8,128)(2,1)}, bf16[2,128,1536]{2,1,0:T(8,128)(2,1)S(1)}, u32[]{:S(2)}, u32[]{:S(2)}) collective-permute-start(bf16[2,128,1536]{2,1,0:T(8,128)(2,1)} %get-tuple-element.34), channel_id=1, source_target_pairs={{1,2},{3,4},{5,6},{7,8},{9,10},{11,12},{13,14},{15,16},{17,18},{19... | collective-permute-start | bytes 2359304 | tf_op jit(solution)/shard_map/ppermute | solution.py:37
  50.0 13.2 %collective-permute-start.3 = (bf16[2,128,1536]{2,1,0:T(8,128)(2,1)}, bf16[2,128,1536]{2,1,0:T(8,128)(2,1)S(1)}, u32[]{:S(2)}, u32[]{:S(2)}) collective-permute-start(bf16[2,128,1536]{2,1,0:T(8,128)(2,1)} %get-tuple-element.35), channel_id=1, source_target_pairs={{0,1},{1,0},{2,3},{3,2},{4,5},{5,4},{6,7},{7,6},{8,9},{9,8},{10,11... | collective-permute-start | bytes 2359304 | tf_op jit(solution)/shard_map/ppermute | solution.py:31
  51.9 19.3 %all-to-all-start.1 = ((bf16[16,24,128]{2,1,0:T(8,128)(2,1)}), bf16[16,24,128]{2,1,0:T(8,128)(2,1)S(1)}, u32[]{:S(2)}, u32[]{:S(2)}) async-start(bf16[16,24,128]{2,1,0:T(8,128)(2,1)} %broadcast_in_dim.13), calls=%async_computation.1 | async-start | bytes 196608 | tf_op jit(solution)/shard_map/all_to_all | solution.py:289

commit v4 on v3

--- a/solution.py
+++ b/solution.py
@@ -19,9 +19,9 @@
 CLIP = tuple(name for name, _ in CLIP_PARTS)
 SEQ = tuple(name for name, _ in SEQ_PARTS)
 VMEM_LIMIT = 60 * 1024 * 1024
-HEADS_LIMIT = 56 * 1024 * 1024
+HEADS_LIMIT = 48 * 1024 * 1024
 ADD_LIMIT = 8 * 1024 * 1024
-PER_STEP = 4
+PER_STEP = 6
 STEPS = HEADS // PER_STEP
 WIDE = PER_STEP * HEAD
 
@@ -286,8 +286,8 @@
     partial = sum_peers(first).astype(jnp.bfloat16)
     copies = jnp.broadcast_to(partial[None], (lax.axis_size(deep_axes), *partial.shape))
     copies, near_grad = lax.optimization_barrier((copies, near_grad))
+    near_back = swap_chip(near_grad)
     second = lax.all_to_all(copies, deep_axes, 0, 0)
-    near_back = swap_chip(near_grad)
     part = add_call(own_grad, far_back, False, 40_000_000, "add_far")
     grads = add_call(part, near_back, True, 2_400_000, "add_near")
     second, *grads = lax.optimization_barrier((second, *grads))

time: 72.3 us -> 70.4 us (0.974)
  Pallas kernels: 15.1 us -> 11.3 us
  starting transfers between devices: 33.6 us -> 35.9 us
  other arithmetic: 2.23 us -> 0.9 us
    pallas_call x1, Pallas kernels: 3.05 us -> 0.19 us  [prepare_call(): pl.pallas_call(prepare_kernel, in_specs=[pl.BlockSpec(memory_space=pl.ANY...]
    all_to_all x1, starting transfers between devices: 8.92 us -> 11.3 us  [body(): first = lax.all_to_all(null_copies, wide_axes, 0, 0)]
    pallas_call x1, Pallas kernels: 8.1 us -> 7.02 us  [heads_call(): pl.pallas_call(heads_kernel, grid=(STEPS,), in_specs=[block(video_rows)]...]
    select_n x1, other arithmetic: 0.88 us -> 0.12 us  [body(): jnp.where(jnp.concatenate([allowed, jnp.broadcast_to(null_allowed[:, None...]
    unnamed x12 -> x14, local copies, waits for them, and re-layouts: 2.44 us -> 3.18 us
  transfers between devices with their start and end apart: 6 -> 6, of which waited for: 2 -> 3; matrix products, arithmetic and copies ran while one was open for 5% -> 2% of each run, Pallas kernels for 7% -> 3%
where the time goes in v4:
time: 70.4 us; the launch traced here: 69.9 us
  starting transfers between devices  35.9 us (51%)
  waiting for transfers between devices  16.4 us (23%)
  Pallas kernels  11.3 us (16%)
  local copies, waits for them, and re-layouts  4.51 us (6%)
  other arithmetic  0.9 us (1%)
  between operations  0.9 us (1%)
    all_to_all x1, starting transfers between devices, body(): first = lax.all_to_all(null_copies, wide_axes, 0, 0)  11.3 us
    all_to_all x1, starting transfers between devices, body(): second = lax.all_to_all(copies, deep_axes, 0, 0)  10.8 us
    all_to_all x1, waiting for transfers between devices, body(): first = lax.all_to_all(null_copies, wide_axes, 0, 0)  9.2 us
    pallas_call x1, Pallas kernels, heads_call(): pl.pallas_call(heads_kernel, grid=(STEPS,), in_specs=[block(video_rows)]...  7.02 us
    ppermute x2, starting transfers between devices, swap_link(): return lax.ppermute(block, SEQ, pairs + [(b, a) for a, b in pairs])  6.96 us
    ppermute x2, starting transfers between devices, swap_chip(): return lax.ppermute(block, SEQ, [(i, i ^ 1) for i in range(count)])  6.89 us
    all_to_all x1, waiting for transfers between devices, body(): second = lax.all_to_all(copies, deep_axes, 0, 0)  6.48 us
    unnamed x14, local copies, waits for them, and re-layouts  3.18 us
  transfers between devices with their start and end apart: 6, of which 3 were waited for; matrix products, arithmetic and copies ran while one was open for 2% of the time, Pallas kernels for 3%

profile of v4, /device:TPU:1, one launch (start us, length us, event | category | flops | bytes accessed | tf_op | source)
XLA Modules:
  0.0 69.9 jit_solution(7440693386529790663)
XLA Ops:
  0.6 0.0 copy-start.2
  0.6 0.0 copy-start.1
  0.7 2.1 %stack.1.own_hbm = bf16[256,1536]{1,0:T(8,128)(2,1)} custom-call(bf16[128,1536]{1,0:T(8,128)(2,1)} %key_ref.1, bf16[128,1536]{1,0:T(8,128)(2,1)} %value_ref.1), custom_call_target="tpu_custom_call" | custom-call | tf_op jit(solution)/shard_map/stack/pallas_call | solution.py:91
  2.7 4.5 %collective-permute-start = (bf16[256,1536]{1,0:T(8,128)(2,1)}, bf16[256,1536]{1,0:T(8,128)(2,1)S(1)}, u32[]{:S(2)}, u32[]{:S(2)}) collective-permute-start(bf16[256,1536]{1,0:T(8,128)(2,1)} %stack.1.own_hbm), channel_id=1, source_target_pairs={{1,2},{3,4},{5,6},{7,8},{9,10},{11,12},{13,14},{15,16},{17,18},{19... | collective-permute-start | bytes 2359304 | tf_op jit(solution)/shard_map/ppermute | solution.py:37
  7.3 0.0 copy-start.6
  7.3 0.6 copy-done.6
  7.9 0.2 reduce-window.4
  8.1 0.1 convert_reduce_fusion.2
  8.2 5.0 %collective-permute-start.1 = (bf16[256,1536]{1,0:T(8,128)(2,1)}, bf16[256,1536]{1,0:T(8,128)(2,1)S(1)}, u32[]{:S(2)}, u32[]{:S(2)}) collective-permute-start(bf16[256,1536]{1,0:T(8,128)(2,1)} %stack.1.own_hbm), channel_id=1, source_target_pairs={{0,1},{1,0},{2,3},{3,2},{4,5},{5,4},{6,7},{7,6},{8,9},{9,8},{10,11... | collective-permute-start | bytes 2359304 | tf_op jit(solution)/shard_map/ppermute | solution.py:31
  13.2 0.0 copy-start.4
  13.3 0.6 copy-done.4
  14.0 0.0 copy-done.2
  14.0 0.0 copy-done.1
  14.0 0.0 copy-start
  14.0 1.1 %copy-done = bf16[256,1536]{1,0:T(8,128)(2,1)S(1)} copy-done((bf16[256,1536]{1,0:T(8,128)(2,1)S(1)}, bf16[256,1536]{1,0:T(8,128)(2,1)}, u32[]{:S(2)}) %copy-start) | copy-done | bytes 786456
  15.1 0.0 copy-start.3
  15.1 0.2 prepare.1
  15.3 0.5 copy-done.3
  15.9 0.1 pad_dynamic-slice_fusion.2
  16.0 0.1 convert_reduce_fusion.1
  16.1 0.2 fusion
  16.3 0.1 add_select_fusion.bias_ref
  16.4 0.0 collective-permute-done.1.near_ref
  16.4 0.0 copy-start.5
  16.4 0.7 collective-permute-done.far_ref
  17.1 0.2 copy-done.5
  17.3 7.0 %heads.1 = (bf16[256,1536]{1,0:T(8,128)(2,1)}, bf16[256,1536]{1,0:T(8,128)(2,1)}, bf16[2,128,1536]{2,1,0:T(8,128)(2,1)}, bf16[2,128,1536]{2,1,0:T(8,128)(2,1)S(1...) custom-call(bf16[256,1536]{1,0:T(8,128)(2,1)S(1)} %get-tuple-element.24.q_ref, ...), custom_call_target="tpu_custom_call" | custom-call | flops 1887436800 | bytes 9000000 | tf_op jit(solution)/shard_map/heads/pallas_call | solution.py:191
  24.4 11.3 %all-to-all-start = ((bf16[32,24,128]{2,1,0:T(8,128)(2,1)}), bf16[32,24,128]{2,1,0:T(8,128)(2,1)S(1)}, u32[]{:S(2)}, u32[]{:S(2)}) async-start(bf16[32,24,128]{2,1,0:T(8,128)(2,1)} %get-tuple-element.30), calls=%async_computation | async-start | bytes 393216 | tf_op jit(solution)/shard_map/all_to_all | solution.py:285
  35.6 2.4 %collective-permute-start.2 = (bf16[2,128,1536]{2,1,0:T(8,128)(2,1)}, bf16[2,128,1536]{2,1,0:T(8,128)(2,1)S(1)}, u32[]{:S(2)}, u32[]{:S(2)}) collective-permute-start(bf16[2,128,1536]{2,1,0:T(8,128)(2,1)} %get-tuple-element.34), channel_id=1, source_target_pairs={{1,2},{3,4},{5,6},{7,8},{9,10},{11,12},{13,14},{15,16},{17,18},{19... | collective-permute-start | bytes 2359304 | tf_op jit(solution)/shard_map/ppermute | solution.py:37
  38.1 9.2 %all-to-all-done = bf16[32,24,128]{2,1,0:T(8,128)(2,1)S(1)} async-done(((bf16[32,24,128]{2,1,0:T(8,128)(2,1)}), bf16[32,24,128]{2,1,0:T(8,128)(2,1)S(1)}, u32[]{:S(2)}, u32[]{:S(2)}) %all-to-all-start) | async-done | bytes 196640 | tf_op jit(solution)/shard_map/all_to_all | solution.py:285
  47.3 0.7 broadcast_in_dim.13
  48.0 1.9 %collective-permute-start.3 = (bf16[2,128,1536]{2,1,0:T(8,128)(2,1)S(1)}, bf16[2,128,1536]{2,1,0:T(8,128)(2,1)S(1)}, u32[]{:S(2)}, u32[]{:S(2)}) collective-permute-start(bf16[2,128,1536]{2,1,0:T(8,128)(2,1)S(1)} %get-tuple-element.35), channel_id=1, source_target_pairs={{0,1},{1,0},{2,3},{3,2},{4,5},{5,4},{6,7},{7,6},{8,9},{9,8},{10,11... | collective-permute-start | bytes 2359304 | tf_op jit(solution)/shard_map/ppermute | solution.py:31
  49.9 10.8 %all-to-all-start.1 = ((bf16[16,24,128]{2,1,0:T(8,128)(2,1)}), bf16[16,24,128]{2,1,0:T(8,128)(2,1)S(1)}, u32[]{:S(2)}, u32[]{:S(2)}) async-start(bf16[16,24,128]{2,1,0:T(8,128)(2,1)} %broadcast_in_dim.13), calls=%async_computation.1 | async-start | bytes 196608 | tf_op jit(solution)/shard_map/all_to_all | solution.py:290
  60.7 0.0 collective-permute-done.2.b_ref
  60.7 0.4 add_far.1.a_ref
  61.2 0.0 collective-permute-done.3.b_ref
  61.2 1.6 %add_near.1 = (bf16[128,1536]{1,0:T(8,128)(2,1)}, bf16[128,1536]{1,0:T(8,128)(2,1)}) custom-call(bf16[2,128,1536]{2,1,0:T(8,128)(2,1)S(1)} %add_far.1.a_ref, bf16[2,128,1536]{2,1,0:T(8,128)(2,1)S(1)} %collective-permute-done.3.b_ref), custom_call_target="tpu_custom_call" | custom-call | flops 393216 | bytes 2400000 | tf_op jit(solution)/shard_map/add_near/pallas_call | solution.py:226
  62.7 6.5 %all-to-all-done.1 = bf16[16,24,128]{2,1,0:T(8,128)(2,1)S(1)} async-done(((bf16[16,24,128]{2,1,0:T(8,128)(2,1)}), bf16[16,24,128]{2,1,0:T(8,128)(2,1)S(1)}, u32[]{:S(2)}, u32[]{:S(2)}) %all-to-all-start.1) | async-done | bytes 98336 | tf_op jit(solution)/shard_map/all_to_all | solution.py:290
  69.3 0.6 reshape.163
  (13 shorter events, 0.2 us)
Async XLA Ops:
  0.6 13.4 %copy-start.2 = (bf16[256,1536]{1,0:T(8,128)(2,1)S(1)}, bf16[256,1536]{1,0:T(8,128)(2,1)}, u32[]{:S(2)}) copy-start(bf16[256,1536]{1,0:T(8,128)(2,1)} %g_hbm.1) | copy-start | bytes 2359300
  0.6 13.4 %copy-start.1 = (bf16[256,1536]{1,0:T(8,128)(2,1)S(1)}, bf16[256,1536]{1,0:T(8,128)(2,1)}, u32[]{:S(2)}) copy-start(bf16[256,1536]{1,0:T(8,128)(2,1)} %q_hbm.1) | copy-start | bytes 2359300
  2.7 14.4 %collective-permute-start = (bf16[256,1536]{1,0:T(8,128)(2,1)}, bf16[256,1536]{1,0:T(8,128)(2,1)S(1)}, u32[]{:S(2)}, u32[]{:S(2)}) collective-permute-start(bf16[256,1536]{1,0:T(8,128)(2,1)} %stack.1.own_hbm), channel_id=1, source_target_pairs={{1,2},{3,4},{5,6},{7,8},{9,10},{11,12},{13,14},{15,16},{17,18},{19... | collective-permute-start | bytes 2359304 | tf_op jit(solution)/shard_map/ppermute | solution.py:37
  7.3 0.7 copy-start.6
  8.2 8.2 %collective-permute-start.1 = (bf16[256,1536]{1,0:T(8,128)(2,1)}, bf16[256,1536]{1,0:T(8,128)(2,1)S(1)}, u32[]{:S(2)}, u32[]{:S(2)}) collective-permute-start(bf16[256,1536]{1,0:T(8,128)(2,1)} %stack.1.own_hbm), channel_id=1, source_target_pairs={{0,1},{1,0},{2,3},{3,2},{4,5},{5,4},{6,7},{7,6},{8,9},{9,8},{10,11... | collective-permute-start | bytes 2359304 | tf_op jit(solution)/shard_map/ppermute | solution.py:31
  13.2 0.7 copy-start.4
  14.0 1.1 %copy-start = (bf16[256,1536]{1,0:T(8,128)(2,1)S(1)}, bf16[256,1536]{1,0:T(8,128)(2,1)}, u32[]{:S(2)}) copy-start(bf16[256,1536]{1,0:T(8,128)(2,1)} %stack.1.own_hbm) | copy-start | bytes 2359300
  15.1 0.7 %copy-start.3 = (s32[4096]{0:T(1024)S(1)}, s32[4096]{0:T(1024)}, u32[]{:S(2)}) copy-start(s32[4096]{0:T(1024)} %param.11) | copy-start | bytes 49156
  16.4 0.9 %copy-start.5 = (bf16[256,1536]{1,0:T(8,128)(2,1)}, bf16[256,1536]{1,0:T(8,128)(2,1)S(1)}, u32[]{:S(2)}) copy-start(bf16[256,1536]{1,0:T(8,128)(2,1)S(1)} %collective-permute-done.1.near_ref) | copy-start | bytes 2359300
  24.4 22.9 %all-to-all-start = ((bf16[32,24,128]{2,1,0:T(8,128)(2,1)}), bf16[32,24,128]{2,1,0:T(8,128)(2,1)S(1)}, u32[]{:S(2)}, u32[]{:S(2)}) async-start(bf16[32,24,128]{2,1,0:T(8,128)(2,1)} %get-tuple-element.30), calls=%async_computation | async-start | bytes 393216 | tf_op jit(solution)/shard_map/all_to_all | solution.py:285
  35.6 25.1 %collective-permute-start.2 = (bf16[2,128,1536]{2,1,0:T(8,128)(2,1)}, bf16[2,128,1536]{2,1,0:T(8,128)(2,1)S(1)}, u32[]{:S(2)}, u32[]{:S(2)}) collective-permute-start(bf16[2,128,1536]{2,1,0:T(8,128)(2,1)} %get-tuple-element.34), channel_id=1, source_target_pairs={{1,2},{3,4},{5,6},{7,8},{9,10},{11,12},{13,14},{15,16},{17,18},{19... | collective-permute-start | bytes 2359304 | tf_op jit(solution)/shard_map/ppermute | solution.py:37
  48.0 13.2 %collective-permute-start.3 = (bf16[2,128,1536]{2,1,0:T(8,128)(2,1)S(1)}, bf16[2,128,1536]{2,1,0:T(8,128)(2,1)S(1)}, u32[]{:S(2)}, u32[]{:S(2)}) collective-permute-start(bf16[2,128,1536]{2,1,0:T(8,128)(2,1)S(1)} %get-tuple-element.35), channel_id=1, source_target_pairs={{0,1},{1,0},{2,3},{3,2},{4,5},{5,4},{6,7},{7,6},{8,9},{9,8},{10,11... | collective-permute-start | bytes 2359304 | tf_op jit(solution)/shard_map/ppermute | solution.py:31
  49.9 19.3 %all-to-all-start.1 = ((bf16[16,24,128]{2,1,0:T(8,128)(2,1)}), bf16[16,24,128]{2,1,0:T(8,128)(2,1)S(1)}, u32[]{:S(2)}, u32[]{:S(2)}) async-start(bf16[16,24,128]{2,1,0:T(8,128)(2,1)} %broadcast_in_dim.13), calls=%async_computation.1 | async-start | bytes 196608 | tf_op jit(solution)/shard_map/all_to_all | solution.py:290

commit v5 on v4

--- a/solution.py
+++ b/solution.py
@@ -19,7 +19,8 @@
 CLIP = tuple(name for name, _ in CLIP_PARTS)
 SEQ = tuple(name for name, _ in SEQ_PARTS)
 VMEM_LIMIT = 60 * 1024 * 1024
-HEADS_LIMIT = 48 * 1024 * 1024
+HEADS_LIMIT = 36 * 1024 * 1024
+PREPARE_LIMIT = 24 * 1024 * 1024
 ADD_LIMIT = 8 * 1024 * 1024
 PER_STEP = 6
 STEPS = HEADS // PER_STEP
@@ -103,22 +104,31 @@
     )(keys, values)
 
 
-def prepare_kernel(q_hbm, g_hbm, own_hbm, q_ref, g_ref, own_ref, sems):
-    pairs = ((q_hbm, q_ref), (g_hbm, g_ref), (own_hbm, own_ref))
+def prepare_kernel(
+    q_hbm, g_hbm, own_hbm, near_hbm, q_ref, g_ref, own_ref, near_ref,
+    g_flip, own_flip, near_flip, sems,
+):
+    pairs = ((g_hbm, g_ref), (own_hbm, own_ref), (near_hbm, near_ref), (q_hbm, q_ref))
     copies = [pltpu.make_async_copy(a, b, sems.at[i]) for i, (a, b) in enumerate(pairs)]
     start(copies)
     wait(copies)
-
-
-def prepare_call(q, g, own):
-    arrays = (q, g, own)
+    for head in range(HEADS):
+        span = slice(head * HEAD, (head + 1) * HEAD)
+        for ref, flip in ((g_ref, g_flip), (own_ref, own_flip), (near_ref, near_flip)):
+            flip[span, :] = ref[:, span].T
+
+
+def prepare_call(q, g, own, near):
+    arrays = (q, g, own, near)
+    inside = pl.BlockSpec(memory_space=pltpu.VMEM)
+    flips = [jax.ShapeDtypeStruct(x.shape[::-1], x.dtype) for x in (g, own, near)]
     return pl.pallas_call(
         prepare_kernel,
-        in_specs=[pl.BlockSpec(memory_space=pl.ANY)] * 3,
-        out_specs=[pl.BlockSpec(memory_space=pltpu.VMEM)] * 3,
-        out_shape=[jax.ShapeDtypeStruct(x.shape, x.dtype) for x in arrays],
-        scratch_shapes=[pltpu.SemaphoreType.DMA((3,))],
-        compiler_params=pltpu.CompilerParams(vmem_limit_bytes=HEADS_LIMIT),
+        in_specs=[pl.BlockSpec(memory_space=pl.ANY)] * 4,
+        out_specs=[inside] * 7,
+        out_shape=[jax.ShapeDtypeStruct(x.shape, x.dtype) for x in arrays] + flips,
+        scratch_shapes=[pltpu.SemaphoreType.DMA((4,))],
+        compiler_params=pltpu.CompilerParams(vmem_limit_bytes=PREPARE_LIMIT),
         name="prepare",
     )(*arrays)
 
@@ -130,8 +140,16 @@
     )
 
 
+def flipped(far_ref, own_flip, near_flip, null_flip, cols, index):
+    rows = far_ref.shape[0] // 2
+    span = slice(index * rows, (index + 1) * rows)
+    far = far_ref[span, cols].T
+    return jnp.concatenate([far, own_flip[cols, span], near_flip[cols, span], null_flip[index]], axis=1)
+
+
 def heads_kernel(
-    q_ref, g_ref, far_ref, own_ref, near_ref, null_ref, bias_ref, valid_ref,
+    q_ref, g_ref, far_ref, own_ref, near_ref, g_flip, own_flip, near_flip,
+    null_ref, null_flip, bias_ref, valid_ref,
     out_ref, dq_ref, far_grad_ref, own_grad_ref, near_grad_ref, null_grad_ref, null_sum,
 ):
     step = pl.program_id(0)
@@ -146,8 +164,12 @@
     exact = [jnp.exp2((x - top) * (FACTOR * LOG2E)) for x, top in zip(scores, tops)]
     shares = [valid_ref[...] / jnp.sum(x, axis=0, keepdims=True) for x in exact]
     exponents = [x.astype(jnp.bfloat16) for x in exact]
-    flips = [g_ref[:, cols[i]].T.astype(jnp.float32) for i in parts]
-    mixed = [dot(values[i], exponents[i], 0, 0) * shares[i] for i in parts]
+    flips = [g_flip[cols[i], :].astype(jnp.float32) for i in parts]
+    keys_flip, values_flip = [
+        [flipped(far_ref, own_flip, near_flip, null_flip.at[i], cols[i], index) for i in parts]
+        for index in range(2)
+    ]
+    mixed = [dot(values_flip[i], exponents[i], 1, 0) * shares[i] for i in parts]
     deltas = [jnp.sum(x * flip, axis=0, keepdims=True) for x, flip in zip(mixed, flips)]
     prob_grads = [dot(values[i], g_ref[:, cols[i]], 1, 1) for i in parts]
     score_grads = [
@@ -156,7 +178,7 @@
     ]
     for i in parts:
         out_ref[:, cols[i]] = mixed[i].astype(jnp.bfloat16).T
-        dq_ref[:, cols[i]] = dot(keys[i], score_grads[i], 0, 0).astype(jnp.bfloat16).T
+        dq_ref[:, cols[i]] = dot(keys_flip[i], score_grads[i], 1, 0).astype(jnp.bfloat16).T
         terms = (
             dot(score_grads[i], q_ref[:, cols[i]], 1, 0),
             dot(exponents[i], (flips[i] * shares[i]).astype(jnp.bfloat16), 1, 1),
@@ -182,7 +204,7 @@
     return pl.BlockSpec(shape, lambda i: (0,) * len(shape))
 
 
-def heads_call(q, g, far, own, near, null_rows, bias, valid, peers):
+def heads_call(q, g, far, own, near, flips, null_rows, null_flip, bias, valid, peers):
     video_rows, width = q.shape
     audio_rows = video_rows // 2
     wide = jax.ShapeDtypeStruct((video_rows, width), jnp.bfloat16)
@@ -192,8 +214,10 @@
         heads_kernel,
         grid=(STEPS,),
         in_specs=[block(video_rows)] * 5
+        + [pl.BlockSpec((WIDE, video_rows), lambda i: (i, 0))] * 3
         + [
             pl.BlockSpec((PER_STEP, *null_rows.shape[1:]), lambda i: (i, 0, 0, 0)),
+            pl.BlockSpec((PER_STEP, *null_flip.shape[1:]), lambda i: (i, 0, 0, 0)),
             whole(bias.shape),
             whole(valid.shape),
         ],
@@ -205,7 +229,7 @@
             flops=12 * bias.size * width, bytes_accessed=9_000_000, transcendentals=bias.size * HEADS
         ),
         name="heads",
-    )(q, g, far, own, near, null_rows, bias, valid)
+    )(q, g, far, own, near, *flips, null_rows, null_flip, bias, valid)
 
 
 def add_kernel(a_ref, b_ref, *out_refs):
@@ -270,16 +294,19 @@
         MASKED,
     ).astype(jnp.float32)
     valid = (segment_of(query_pos // 2, bounds) < pad_segment).astype(jnp.float32)[None]
-    null_heads = null_kv.reshape(2, HEADS, 1, HEAD).swapaxes(0, 1)
-    null_rows = jnp.pad(null_heads, ((0, 0), (0, 0), (0, NULL_ROWS - 1), (0, 0)))
+    null_heads = null_kv.reshape(2, HEADS, HEAD).swapaxes(0, 1)
+    first_only = jnp.arange(NULL_ROWS) == 0
+    null_rows = jnp.where(first_only[:, None], null_heads[:, :, None], jnp.bfloat16(0))
+    null_flip = jnp.where(first_only, null_heads[..., None], jnp.bfloat16(0))
 
     stacked, valid = lax.optimization_barrier((stacked, valid))
     near = swap_chip(stacked)
 
     wide_axes, deep_axes = ("yh", "yl", "x"), ("z", "core")
-    q_held, g_held, own = prepare_call(video_query, out_grad, stacked)
+    q_held, g_held, own, near, *flips = prepare_call(video_query, out_grad, stacked, near)
     attended, query_grad, far_grad, own_grad, near_grad, null_copies = heads_call(
-        q_held, g_held, far, own, near, null_rows, bias, valid, lax.axis_size(wide_axes)
+        q_held, g_held, far, own, near, flips, null_rows, null_flip, bias, valid,
+        lax.axis_size(wide_axes),
     )
     far_back = swap_link(far_grad)
     first = lax.all_to_all(null_copies, wide_axes, 0, 0)
@@ -288,7 +315,7 @@
     copies, near_grad = lax.optimization_barrier((copies, near_grad))
     near_back = swap_chip(near_grad)
     second = lax.all_to_all(copies, deep_axes, 0, 0)
-    part = add_call(own_grad, far_back, False, 40_000_000, "add_far")
+    part = add_call(own_grad, far_back, False, 400_000_000, "add_far")
     grads = add_call(part, near_back, True, 2_400_000, "add_near")
     second, *grads = lax.optimization_barrier((second, *grads))
     null_grad = sum_peers(second).reshape(null_kv.shape)

time: 70.4 us -> 69.6 us (0.989)
  local copies, waits for them, and re-layouts: 4.51 us -> 3.13 us
  Pallas kernels: 11.3 us -> 12.2 us
    pallas_call x1, Pallas kernels: 0.19 us -> 1.94 us  [prepare_call(): pl.pallas_call(prepare_kernel, in_specs=[pl.BlockSpec(memory_space=pl.ANY...]
    unnamed x14 -> x12, local copies, waits for them, and re-layouts: 3.18 us -> 1.83 us
    pallas_call x1, Pallas kernels: 7.02 us -> 6.28 us  [heads_call(): pl.pallas_call(heads_kernel, grid=(STEPS,), in_specs=[block(video_rows)]...]
  transfers between devices with their start and end apart: 6 -> 6, of which waited for: 3 -> 2; matrix products, arithmetic and copies ran while one was open for 2% -> 3% of each run, Pallas kernels for 3% -> 6%
where the time goes in v5:
time: 69.6 us; the launch traced here: 69 us
  starting transfers between devices  35.6 us (51%)
  waiting for transfers between devices  15.7 us (23%)
  Pallas kernels  12.2 us (18%)
  local copies, waits for them, and re-layouts  3.13 us (4%)
  other arithmetic  1.45 us (2%)
  between operations  0.88 us (1%)
    all_to_all x1, starting transfers between devices, body(): first = lax.all_to_all(null_copies, wide_axes, 0, 0)  11 us
    all_to_all x1, starting transfers between devices, body(): second = lax.all_to_all(copies, deep_axes, 0, 0)  10.8 us
    all_to_all x1, waiting for transfers between devices, body(): first = lax.all_to_all(null_copies, wide_axes, 0, 0)  9.2 us
    ppermute x2, starting transfers between devices, swap_link(): return lax.ppermute(block, SEQ, pairs + [(b, a) for a, b in pairs])  6.94 us
    ppermute x2, starting transfers between devices, swap_chip(): return lax.ppermute(block, SEQ, [(i, i ^ 1) for i in range(count)])  6.89 us
    all_to_all x1, waiting for transfers between devices, body(): second = lax.all_to_all(copies, deep_axes, 0, 0)  6.48 us
    pallas_call x1, Pallas kernels, heads_call(): pl.pallas_call(heads_kernel, grid=(STEPS,), in_specs=[block(video_rows)]...  6.28 us
    pallas_call x1, Pallas kernels, stack_call(): pl.pallas_call(stack_kernel, in_specs=[pl.BlockSpec(memory_space=pl.ANY)]...  2.03 us
  transfers between devices with their start and end apart: 6, of which 2 were waited for; matrix products, arithmetic and copies ran while one was open for 3% of the time, Pallas kernels for 6%

profile of v5, /device:TPU:1, one launch (start us, length us, event | category | flops | bytes accessed | tf_op | source)
XLA Modules:
  0.0 69.0 jit_solution(757202998236462817)
XLA Ops:
  0.6 0.0 copy-start.2
  0.6 2.0 %stack.1.own_hbm = bf16[256,1536]{1,0:T(8,128)(2,1)} custom-call(bf16[128,1536]{1,0:T(8,128)(2,1)} %key_ref.1, bf16[128,1536]{1,0:T(8,128)(2,1)} %value_ref.1), custom_call_target="tpu_custom_call" | custom-call | tf_op jit(solution)/shard_map/stack/pallas_call | solution.py:92
  2.7 4.5 %collective-permute-start.1 = (bf16[256,1536]{1,0:T(8,128)(2,1)}, bf16[256,1536]{1,0:T(8,128)(2,1)S(1)}, u32[]{:S(2)}, u32[]{:S(2)}) collective-permute-start(bf16[256,1536]{1,0:T(8,128)(2,1)} %stack.1.own_hbm), channel_id=1, source_target_pairs={{1,2},{3,4},{5,6},{7,8},{9,10},{11,12},{13,14},{15,16},{17,18},{19... | collective-permute-start | bytes 2359304 | tf_op jit(solution)/shard_map/ppermute | solution.py:38
  7.2 0.0 copy-start.5
  7.2 0.6 copy-done.5
  7.9 0.2 reduce-window.4
  8.1 0.1 convert_reduce_fusion.2
  8.1 5.0 %collective-permute-start = (bf16[256,1536]{1,0:T(8,128)(2,1)}, bf16[256,1536]{1,0:T(8,128)(2,1)}, u32[]{:S(2)}, u32[]{:S(2)}) collective-permute-start(bf16[256,1536]{1,0:T(8,128)(2,1)} %stack.1.own_hbm), channel_id=1, source_target_pairs={{0,1},{1,0},{2,3},{3,2},{4,5},{5,4},{6,7},{7,6},{8,9},{9,8},{10,11... | collective-permute-start | bytes 2359304 | tf_op jit(solution)/shard_map/ppermute | solution.py:32
  13.1 0.0 copy-start.3
  13.2 0.7 copy-done.3
  13.9 0.0 copy-start.4
  13.9 0.1 pad_dynamic-slice_fusion.2
  14.0 0.0 copy-start
  14.0 0.0 copy-start.1
  14.0 0.1 convert_reduce_fusion.1
  14.1 0.5 copy-done.4
  14.6 0.1 broadcast_select_fusion.1.null_ref
  14.7 0.2 fusion
  14.9 0.1 add_select_fusion.bias_ref
  15.1 0.5 broadcast_select_fusion.null_flip
  15.5 0.0 collective-permute-done.near_hbm
  15.6 0.0 copy-done.2
  15.6 0.0 copy-done
  15.6 0.0 copy-done.1
  15.6 1.9 %prepare.1 = (bf16[256,1536]{1,0:T(8,128)(2,1)S(1)}, bf16[256,1536]{1,0:T(8,128)(2,1)S(1)}, bf16[256,1536]{1,0:T(8,128)(2,1)S(1)}, bf16[256,1536]{1,0:T(8,128)(2...) custom-call(bf16[256,1536]{1,0:T(8,128)(2,1)S(1)} %copy-done.1, ...), custom_call_target="tpu_custom_call" | custom-call | tf_op jit(solution)/shard_map/prepare/pallas_call | solution.py:125
  17.5 0.0 collective-permute-done.1.far_ref
  17.5 6.3 %heads.1 = (bf16[256,1536]{1,0:T(8,128)(2,1)}, bf16[256,1536]{1,0:T(8,128)(2,1)}, bf16[2,128,1536]{2,1,0:T(8,128)(2,1)}, bf16[2,128,1536]{2,1,0:T(8,128)(2,1)S(1...) custom-call(bf16[256,1536]{1,0:T(8,128)(2,1)S(1)} %get-tuple-element.28.q_ref, ...), custom_call_target="tpu_custom_call" | custom-call | flops 1887436800 | bytes 9000000 | tf_op jit(solution)/shard_map/heads/pallas_call | solution.py:213
  23.8 11.0 %all-to-all-start = ((bf16[32,24,128]{2,1,0:T(8,128)(2,1)}), bf16[32,24,128]{2,1,0:T(8,128)(2,1)S(1)}, u32[]{:S(2)}, u32[]{:S(2)}) async-start(bf16[32,24,128]{2,1,0:T(8,128)(2,1)} %get-tuple-element.38), calls=%async_computation | async-start | bytes 393216 | tf_op jit(solution)/shard_map/all_to_all | solution.py:312
  34.8 2.4 %collective-permute-start.2 = (bf16[2,128,1536]{2,1,0:T(8,128)(2,1)}, bf16[2,128,1536]{2,1,0:T(8,128)(2,1)S(1)}, u32[]{:S(2)}, u32[]{:S(2)}) collective-permute-start(bf16[2,128,1536]{2,1,0:T(8,128)(2,1)} %get-tuple-element.42), channel_id=1, source_target_pairs={{1,2},{3,4},{5,6},{7,8},{9,10},{11,12},{13,14},{15,16},{17,18},{19... | collective-permute-start | bytes 2359304 | tf_op jit(solution)/shard_map/ppermute | solution.py:38
  37.3 9.2 %all-to-all-done = bf16[32,24,128]{2,1,0:T(8,128)(2,1)S(1)} async-done(((bf16[32,24,128]{2,1,0:T(8,128)(2,1)}), bf16[32,24,128]{2,1,0:T(8,128)(2,1)S(1)}, u32[]{:S(2)}, u32[]{:S(2)}) %all-to-all-start) | async-done | bytes 196640 | tf_op jit(solution)/shard_map/all_to_all | solution.py:312
  46.5 0.7 broadcast_in_dim.80
  47.2 1.9 %collective-permute-start.3 = (bf16[2,128,1536]{2,1,0:T(8,128)(2,1)S(1)}, bf16[2,128,1536]{2,1,0:T(8,128)(2,1)S(1)}, u32[]{:S(2)}, u32[]{:S(2)}) collective-permute-start(bf16[2,128,1536]{2,1,0:T(8,128)(2,1)S(1)} %get-tuple-element.43), channel_id=1, source_target_pairs={{0,1},{1,0},{2,3},{3,2},{4,5},{5,4},{6,7},{7,6},{8,9},{9,8},{10,11... | collective-permute-start | bytes 2359304 | tf_op jit(solution)/shard_map/ppermute | solution.py:32
  49.1 10.8 %all-to-all-start.1 = ((bf16[16,24,128]{2,1,0:T(8,128)(2,1)}), bf16[16,24,128]{2,1,0:T(8,128)(2,1)S(1)}, u32[]{:S(2)}, u32[]{:S(2)}) async-start(bf16[16,24,128]{2,1,0:T(8,128)(2,1)} %broadcast_in_dim.80), calls=%async_computation.1 | async-start | bytes 196608 | tf_op jit(solution)/shard_map/all_to_all | solution.py:317
  59.9 0.0 collective-permute-done.2.b_ref
  59.9 0.4 add_far.1.a_ref
  60.3 0.0 collective-permute-done.3.b_ref
  60.3 1.6 %add_near.1 = (bf16[128,1536]{1,0:T(8,128)(2,1)}, bf16[128,1536]{1,0:T(8,128)(2,1)}) custom-call(bf16[2,128,1536]{2,1,0:T(8,128)(2,1)S(1)} %add_far.1.a_ref, bf16[2,128,1536]{2,1,0:T(8,128)(2,1)S(1)} %collective-permute-done.3.b_ref), custom_call_target="tpu_custom_call" | custom-call | flops 393216 | bytes 2400000 | tf_op jit(solution)/shard_map/add_near/pallas_call | solution.py:250
  61.9 6.5 %all-to-all-done.1 = bf16[16,24,128]{2,1,0:T(8,128)(2,1)S(1)} async-done(((bf16[16,24,128]{2,1,0:T(8,128)(2,1)}), bf16[16,24,128]{2,1,0:T(8,128)(2,1)S(1)}, u32[]{:S(2)}, u32[]{:S(2)}) %all-to-all-start.1) | async-done | bytes 98336 | tf_op jit(solution)/shard_map/all_to_all | solution.py:317
  68.4 0.6 reshape.165
  (12 shorter events, 0.1 us)
Async XLA Ops:
  0.6 14.9 %copy-start.2 = (bf16[256,1536]{1,0:T(8,128)(2,1)S(1)}, bf16[256,1536]{1,0:T(8,128)(2,1)}, u32[]{:S(2)}) copy-start(bf16[256,1536]{1,0:T(8,128)(2,1)} %g_hbm.1) | copy-start | bytes 2359300
  2.7 14.9 %collective-permute-start.1 = (bf16[256,1536]{1,0:T(8,128)(2,1)}, bf16[256,1536]{1,0:T(8,128)(2,1)S(1)}, u32[]{:S(2)}, u32[]{:S(2)}) collective-permute-start(bf16[256,1536]{1,0:T(8,128)(2,1)} %stack.1.own_hbm), channel_id=1, source_target_pairs={{1,2},{3,4},{5,6},{7,8},{9,10},{11,12},{13,14},{15,16},{17,18},{19... | collective-permute-start | bytes 2359304 | tf_op jit(solution)/shard_map/ppermute | solution.py:38
  7.2 0.7 copy-start.5
  8.1 7.4 %collective-permute-start = (bf16[256,1536]{1,0:T(8,128)(2,1)}, bf16[256,1536]{1,0:T(8,128)(2,1)}, u32[]{:S(2)}, u32[]{:S(2)}) collective-permute-start(bf16[256,1536]{1,0:T(8,128)(2,1)} %stack.1.own_hbm), channel_id=1, source_target_pairs={{0,1},{1,0},{2,3},{3,2},{4,5},{5,4},{6,7},{7,6},{8,9},{9,8},{10,11... | collective-permute-start | bytes 2359304 | tf_op jit(solution)/shard_map/ppermute | solution.py:32
  13.1 0.7 %copy-start.3 = (s32[4096]{0:T(1024)S(1)}, s32[4096]{0:T(1024)}, u32[]{:S(2)}) copy-start(s32[4096]{0:T(1024)} %param.11) | copy-start | bytes 49156
  13.9 0.7 %copy-start.4 = (bf16[2,1536]{1,0:T(2,128)(2,1)S(1)}, bf16[2,1536]{1,0:T(2,128)(2,1)}, u32[]{:S(2)}) copy-start(bf16[2,1536]{1,0:T(2,128)(2,1)} %param.10) | copy-start | bytes 18436
  14.0 1.6 %copy-start = (bf16[256,1536]{1,0:T(8,128)(2,1)S(1)}, bf16[256,1536]{1,0:T(8,128)(2,1)}, u32[]{:S(2)}) copy-start(bf16[256,1536]{1,0:T(8,128)(2,1)} %stack.1.own_hbm) | copy-start | bytes 2359300
  14.0 1.6 %copy-start.1 = (bf16[256,1536]{1,0:T(8,128)(2,1)S(1)}, bf16[256,1536]{1,0:T(8,128)(2,1)}, u32[]{:S(2)}) copy-start(bf16[256,1536]{1,0:T(8,128)(2,1)} %q_hbm.1) | copy-start | bytes 2359300
  23.8 22.6 %all-to-all-start = ((bf16[32,24,128]{2,1,0:T(8,128)(2,1)}), bf16[32,24,128]{2,1,0:T(8,128)(2,1)S(1)}, u32[]{:S(2)}, u32[]{:S(2)}) async-start(bf16[32,24,128]{2,1,0:T(8,128)(2,1)} %get-tuple-element.38), calls=%async_computation | async-start | bytes 393216 | tf_op jit(solution)/shard_map/all_to_all | solution.py:312
  34.8 25.1 %collective-permute-start.2 = (bf16[2,128,1536]{2,1,0:T(8,128)(2,1)}, bf16[2,128,1536]{2,1,0:T(8,128)(2,1)S(1)}, u32[]{:S(2)}, u32[]{:S(2)}) collective-permute-start(bf16[2,128,1536]{2,1,0:T(8,128)(2,1)} %get-tuple-element.42), channel_id=1, source_target_pairs={{1,2},{3,4},{5,6},{7,8},{9,10},{11,12},{13,14},{15,16},{17,18},{19... | collective-permute-start | bytes 2359304 | tf_op jit(solution)/shard_map/ppermute | solution.py:38
  47.2 13.2 %collective-permute-start.3 = (bf16[2,128,1536]{2,1,0:T(8,128)(2,1)S(1)}, bf16[2,128,1536]{2,1,0:T(8,128)(2,1)S(1)}, u32[]{:S(2)}, u32[]{:S(2)}) collective-permute-start(bf16[2,128,1536]{2,1,0:T(8,128)(2,1)S(1)} %get-tuple-element.43), channel_id=1, source_target_pairs={{0,1},{1,0},{2,3},{3,2},{4,5},{5,4},{6,7},{7,6},{8,9},{9,8},{10,11... | collective-permute-start | bytes 2359304 | tf_op jit(solution)/shard_map/ppermute | solution.py:32
  49.1 19.3 %all-to-all-start.1 = ((bf16[16,24,128]{2,1,0:T(8,128)(2,1)}), bf16[16,24,128]{2,1,0:T(8,128)(2,1)S(1)}, u32[]{:S(2)}, u32[]{:S(2)}) async-start(bf16[16,24,128]{2,1,0:T(8,128)(2,1)} %broadcast_in_dim.80), calls=%async_computation.1 | async-start | bytes 196608 | tf_op jit(solution)/shard_map/all_to_all | solution.py:317

commit v6 on v5

--- a/solution.py
+++ b/solution.py
@@ -105,89 +105,129 @@
 
 
 def prepare_kernel(
-    q_hbm, g_hbm, own_hbm, near_hbm, q_ref, g_ref, own_ref, near_ref,
-    g_flip, own_flip, near_flip, sems,
+    q_in, g_in, own_ref, near_ref, bias_ref,
+    q_ref, g_ref, g_flip, keys_flip, exponent_ref, prob_grad_ref, mixed_ref, stats_ref,
 ):
-    pairs = ((g_hbm, g_ref), (own_hbm, own_ref), (near_hbm, near_ref), (q_hbm, q_ref))
-    copies = [pltpu.make_async_copy(a, b, sems.at[i]) for i, (a, b) in enumerate(pairs)]
-    start(copies)
-    wait(copies)
-    for head in range(HEADS):
-        span = slice(head * HEAD, (head + 1) * HEAD)
-        for ref, flip in ((g_ref, g_flip), (own_ref, own_flip), (near_ref, near_flip)):
-            flip[span, :] = ref[:, span].T
-
-
-def prepare_call(q, g, own, near):
-    arrays = (q, g, own, near)
-    inside = pl.BlockSpec(memory_space=pltpu.VMEM)
-    flips = [jax.ShapeDtypeStruct(x.shape[::-1], x.dtype) for x in (g, own, near)]
+    rows = own_ref.shape[0] // 2
+    parts = range(PER_STEP)
+    cols = [slice(i * HEAD, (i + 1) * HEAD) for i in parts]
+    sides = (own_ref, near_ref)
+    keys, values = [
+        [jnp.concatenate([ref[span, cols[i]] for ref in sides], axis=0) for i in parts]
+        for span in (slice(0, rows), slice(rows, 2 * rows))
+    ]
+    scores = [dot(keys[i], q_in[:, cols[i]], 1, 1) + bias_ref[...] for i in parts]
+    tops = [jnp.max(x, axis=0, keepdims=True) for x in scores]
+    exact = [jnp.exp2((x - top) * (FACTOR * LOG2E)) for x, top in zip(scores, tops)]
+    exponents = [x.astype(jnp.bfloat16) for x in exact]
+    for i in parts:
+        stats_ref[i, 0:1] = tops[i]
+        stats_ref[i, 1:2] = jnp.sum(exact[i], axis=0, keepdims=True)
+        exponent_ref[i] = exponents[i]
+        prob_grad_ref[i] = dot(values[i], g_in[:, cols[i]], 1, 1)
+        mixed_ref[cols[i], :] = dot(values[i].T, exponents[i], 1, 0)
+        keys_flip[cols[i], :] = keys[i].T
+        g_flip[cols[i], :] = g_in[:, cols[i]].T
+    q_ref[...] = q_in[...]
+    g_ref[...] = g_in[...]
+
+
+def prepare_call(q, g, own, near, bias):
+    video_rows, width = q.shape
+    local_rows = bias.shape[0]
+    deep = pl.BlockSpec((WIDE, video_rows), lambda i: (i, 0))
+    deep_shape = (width, video_rows)
+    pairs = pl.BlockSpec((PER_STEP, local_rows, video_rows), lambda i: (i, 0, 0))
+    pair_shape = (HEADS, local_rows, video_rows)
+    outs = [
+        (block(video_rows), q.shape, jnp.bfloat16),
+        (block(video_rows), g.shape, jnp.bfloat16),
+        (deep, deep_shape, jnp.bfloat16),
+        (deep, deep_shape, jnp.bfloat16),
+        (pairs, pair_shape, jnp.bfloat16),
+        (pairs, pair_shape, jnp.float32),
+        (deep, deep_shape, jnp.float32),
+        (pl.BlockSpec((PER_STEP, 8, video_rows), lambda i: (i, 0, 0)), (HEADS, 8, video_rows), jnp.float32),
+    ]
     return pl.pallas_call(
         prepare_kernel,
-        in_specs=[pl.BlockSpec(memory_space=pl.ANY)] * 4,
-        out_specs=[inside] * 7,
-        out_shape=[jax.ShapeDtypeStruct(x.shape, x.dtype) for x in arrays] + flips,
-        scratch_shapes=[pltpu.SemaphoreType.DMA((4,))],
+        grid=(STEPS,),
+        in_specs=[block(video_rows)] * 4 + [whole(bias.shape)],
+        out_specs=[spec for spec, _, _ in outs],
+        out_shape=[jax.ShapeDtypeStruct(shape, dtype) for _, shape, dtype in outs],
         compiler_params=pltpu.CompilerParams(vmem_limit_bytes=PREPARE_LIMIT),
+        cost_estimate=pl.CostEstimate(
+            flops=6 * bias.size * width, bytes_accessed=9_000_000, transcendentals=bias.size * HEADS
+        ),
         name="prepare",
-    )(*arrays)
-
-
-def gathered(refs, null_ref, cols, index):
-    rows = refs[0].shape[0] // 2
-    return jnp.concatenate(
-        [ref[index * rows : (index + 1) * rows, cols] for ref in refs] + [null_ref[index]], axis=0
-    )
-
-
-def flipped(far_ref, own_flip, near_flip, null_flip, cols, index):
-    rows = far_ref.shape[0] // 2
-    span = slice(index * rows, (index + 1) * rows)
-    far = far_ref[span, cols].T
-    return jnp.concatenate([far, own_flip[cols, span], near_flip[cols, span], null_flip[index]], axis=1)
+    )(q, g, own, near, bias)
 
 
 def heads_kernel(
-    q_ref, g_ref, far_ref, own_ref, near_ref, g_flip, own_flip, near_flip,
+    q_ref, g_ref, far_ref, g_flip, near_keys_flip, near_exponent, near_prob_grad, near_mixed, stats,
     null_ref, null_flip, bias_ref, valid_ref,
     out_ref, dq_ref, far_grad_ref, own_grad_ref, near_grad_ref, null_grad_ref, null_sum,
 ):
     step = pl.program_id(0)
-    rows = own_ref.shape[0] // 2
-    refs = (far_ref, own_ref, near_ref)
+    rows = far_ref.shape[0] // 2
     parts = range(PER_STEP)
     cols = [slice(i * HEAD, (i + 1) * HEAD) for i in parts]
-    keys = [gathered(refs, null_ref.at[i], cols[i], 0) for i in parts]
-    values = [gathered(refs, null_ref.at[i], cols[i], 1) for i in parts]
+    spans = (slice(0, rows), slice(rows, 2 * rows))
+    keys, values = [
+        [jnp.concatenate([far_ref[span, cols[i]], null_ref[i, index]], axis=0) for i in parts]
+        for index, span in enumerate(spans)
+    ]
+    keys_flip, values_flip = [
+        [jnp.concatenate([far_ref[span, cols[i]].T, null_flip[i, index]], axis=1) for i in parts]
+        for index, span in enumerate(spans)
+    ]
+    scale = FACTOR * LOG2E
     scores = [dot(keys[i], q_ref[:, cols[i]], 1, 1) + bias_ref[...] for i in parts]
-    tops = [jnp.max(x, axis=0, keepdims=True) for x in scores]
-    exact = [jnp.exp2((x - top) * (FACTOR * LOG2E)) for x, top in zip(scores, tops)]
-    shares = [valid_ref[...] / jnp.sum(x, axis=0, keepdims=True) for x in exact]
+    tops = [
+        jnp.maximum(jnp.max(x, axis=0, keepdims=True), stats[i, 0:1]) for i, x in enumerate(scores)
+    ]
+    exact = [jnp.exp2((x - top) * scale) for x, top in zip(scores, tops)]
+    joins = [jnp.exp2((stats[i, 0:1] - tops[i]) * scale) for i in parts]
+    totals = [
+        jnp.sum(x, axis=0, keepdims=True) + joins[i] * stats[i, 1:2] for i, x in enumerate(exact)
+    ]
+    shares = [valid_ref[...] / total for total in totals]
+    near_shares = [share * join for share, join in zip(shares, joins)]
     exponents = [x.astype(jnp.bfloat16) for x in exact]
     flips = [g_flip[cols[i], :].astype(jnp.float32) for i in parts]
-    keys_flip, values_flip = [
-        [flipped(far_ref, own_flip, near_flip, null_flip.at[i], cols[i], index) for i in parts]
-        for index in range(2)
-    ]
-    mixed = [dot(values_flip[i], exponents[i], 1, 0) * shares[i] for i in parts]
+    mixed = [
+        dot(values_flip[i], exponents[i], 1, 0) * shares[i] + near_mixed[cols[i], :] * near_shares[i]
+        for i in parts
+    ]
     deltas = [jnp.sum(x * flip, axis=0, keepdims=True) for x, flip in zip(mixed, flips)]
     prob_grads = [dot(values[i], g_ref[:, cols[i]], 1, 1) for i in parts]
     score_grads = [
-        ((x - delta) * (share * FACTOR)).astype(jnp.bfloat16) * exponent
-        for x, delta, share, exponent in zip(prob_grads, deltas, shares, exponents)
+        ((prob_grads[i] - deltas[i]) * (shares[i] * FACTOR)).astype(jnp.bfloat16) * exponents[i]
+        for i in parts
+    ]
+    near_score_grads = [
+        ((near_prob_grad[i] - deltas[i]) * (near_shares[i] * FACTOR)).astype(jnp.bfloat16)
+        * near_exponent[i]
+        for i in parts
     ]
     for i in parts:
         out_ref[:, cols[i]] = mixed[i].astype(jnp.bfloat16).T
-        dq_ref[:, cols[i]] = dot(keys_flip[i], score_grads[i], 1, 0).astype(jnp.bfloat16).T
+        query_grad = dot(keys_flip[i], score_grads[i], 1, 0)
+        query_grad = query_grad + dot(near_keys_flip[cols[i], :], near_score_grads[i], 1, 0)
+        dq_ref[:, cols[i]] = query_grad.astype(jnp.bfloat16).T
+        q = q_ref[:, cols[i]]
         terms = (
-            dot(score_grads[i], q_ref[:, cols[i]], 1, 0),
-            dot(exponents[i], (flips[i] * shares[i]).astype(jnp.bfloat16), 1, 1),
+            (dot(score_grads[i], q, 1, 0), dot(near_score_grads[i], q, 1, 0)),
+            (
+                dot(exponents[i], (flips[i] * shares[i]).astype(jnp.bfloat16), 1, 1),
+                dot(near_exponent[i], (flips[i] * near_shares[i]).astype(jnp.bfloat16), 1, 1),
+            ),
         )
-        for index, term in enumerate(terms):
+        for index, (term, near_term) in enumerate(terms):
             far_grad_ref[index, :, cols[i]] = term[:rows].astype(jnp.bfloat16)
-            own_grad_ref[index, :, cols[i]] = term[rows : 2 * rows].astype(jnp.bfloat16)
-            near_grad_ref[index, :, cols[i]] = term[2 * rows : 3 * rows].astype(jnp.bfloat16)
-            null_sum[pl.ds(index * HEADS + step * PER_STEP + i, 1), :] = term[3 * rows : 3 * rows + 1]
+            own_grad_ref[index, :, cols[i]] = near_term[:rows].astype(jnp.bfloat16)
+            near_grad_ref[index, :, cols[i]] = near_term[rows:].astype(jnp.bfloat16)
+            null_sum[pl.ds(index * HEADS + step * PER_STEP + i, 1), :] = term[rows : rows + 1]
 
     @pl.when(step == STEPS - 1)
     def _():
@@ -204,18 +244,21 @@
     return pl.BlockSpec(shape, lambda i: (0,) * len(shape))
 
 
-def heads_call(q, g, far, own, near, flips, null_rows, null_flip, bias, valid, peers):
+def heads_call(q, g, far, near_parts, null_rows, null_flip, bias, valid, peers):
     video_rows, width = q.shape
     audio_rows = video_rows // 2
     wide = jax.ShapeDtypeStruct((video_rows, width), jnp.bfloat16)
     terms = [jax.ShapeDtypeStruct((2, audio_rows, width), jnp.bfloat16)] * 3
     null_shape = (peers, 2 * HEADS, HEAD)
+    deep = pl.BlockSpec((WIDE, video_rows), lambda i: (i, 0))
+    pairs = pl.BlockSpec((PER_STEP, 2 * audio_rows, video_rows), lambda i: (i, 0, 0))
     return pl.pallas_call(
         heads_kernel,
         grid=(STEPS,),
-        in_specs=[block(video_rows)] * 5
-        + [pl.BlockSpec((WIDE, video_rows), lambda i: (i, 0))] * 3
+        in_specs=[block(video_rows)] * 3
+        + [deep, deep, pairs, pairs, deep]
         + [
+            pl.BlockSpec((PER_STEP, 8, video_rows), lambda i: (i, 0, 0)),
             pl.BlockSpec((PER_STEP, *null_rows.shape[1:]), lambda i: (i, 0, 0, 0)),
             pl.BlockSpec((PER_STEP, *null_flip.shape[1:]), lambda i: (i, 0, 0, 0)),
             whole(bias.shape),
@@ -229,7 +272,7 @@
             flops=12 * bias.size * width, bytes_accessed=9_000_000, transcendentals=bias.size * HEADS
         ),
         name="heads",
-    )(q, g, far, own, near, *flips, null_rows, null_flip, bias, valid)
+    )(q, g, far, *near_parts, null_rows, null_flip, bias, valid)
 
 
 def add_kernel(a_ref, b_ref, *out_refs):
@@ -287,12 +330,10 @@
     allowed = allowed_pairs(
         query_pos, key_pos, bounds, keep_rows, total_audio, pad_segment, audio_rows
     )
-    null_allowed = jnp.arange(NULL_ROWS) == 0
-    bias = jnp.where(
-        jnp.concatenate([allowed, jnp.broadcast_to(null_allowed[:, None], (NULL_ROWS, video_rows))]),
-        0.0,
-        MASKED,
-    ).astype(jnp.float32)
+    near_bias = jnp.where(allowed[audio_rows:], 0.0, MASKED).astype(jnp.float32)
+    null_allowed = jnp.broadcast_to(jnp.arange(NULL_ROWS)[:, None] == 0, (NULL_ROWS, video_rows))
+    far_allowed = jnp.concatenate([allowed[:audio_rows], null_allowed])
+    bias = jnp.where(far_allowed, 0.0, MASKED).astype(jnp.float32)
     valid = (segment_of(query_pos // 2, bounds) < pad_segment).astype(jnp.float32)[None]
     null_heads = null_kv.reshape(2, HEADS, HEAD).swapaxes(0, 1)
     first_only = jnp.arange(NULL_ROWS) == 0
@@ -303,10 +344,9 @@
     near = swap_chip(stacked)
 
     wide_axes, deep_axes = ("yh", "yl", "x"), ("z", "core")
-    q_held, g_held, own, near, *flips = prepare_call(video_query, out_grad, stacked, near)
+    q_held, g_held, *near_parts = prepare_call(video_query, out_grad, stacked, near, near_bias)
     attended, query_grad, far_grad, own_grad, near_grad, null_copies = heads_call(
-        q_held, g_held, far, own, near, flips, null_rows, null_flip, bias, valid,
-        lax.axis_size(wide_axes),
+        q_held, g_held, far, near_parts, null_rows, null_flip, bias, valid, lax.axis_size(wide_axes)
     )
     far_back = swap_link(far_grad)
     first = lax.all_to_all(null_copies, wide_axes, 0, 0)
@@ -315,7 +355,7 @@
     copies, near_grad = lax.optimization_barrier((copies, near_grad))
     near_back = swap_chip(near_grad)
     second = lax.all_to_all(copies, deep_axes, 0, 0)
-    part = add_call(own_grad, far_back, False, 400_000_000, "add_far")
+    part = add_call(own_grad, far_back, False, 4_000_000, "add_far")
     grads = add_call(part, near_back, True, 2_400_000, "add_near")
     second, *grads = lax.optimization_barrier((second, *grads))
     null_grad = sum_peers(second).reshape(null_kv.shape)

time: 69.6 us -> 68.2 us (0.980)
  local copies, waits for them, and re-layouts: 3.13 us -> 1.33 us
  waiting for transfers between devices: 15.7 us -> 16.7 us
    unnamed x12, local copies, waits for them, and re-layouts: 1.83 us -> 0.03 us
    pallas_call x1, Pallas kernels: 6.28 us -> 4.86 us  [heads_call(): pl.pallas_call(heads_kernel, grid=(STEPS,), in_specs=[block(video_rows)]...]
    pallas_call x1, Pallas kernels: 1.94 us -> 3.26 us  [prepare_call(): pl.pallas_call(prepare_kernel, grid=(STEPS,), in_specs=[block(video_rows)...]
    ppermute x2, waiting for transfers between devices: 0.01 us -> 0.97 us  [swap_chip(): return lax.ppermute(block, SEQ, [(i, i ^ 1) for i in range(count)])]
  transfers between devices with their start and end apart: 6 -> 6, of which waited for: 2 -> 3; matrix products, arithmetic and copies ran while one was open for 3% -> 3% of each run, Pallas kernels for 6% -> 8%
where the time goes in v6:
time: 68.2 us; the launch traced here: 67.8 us
  starting transfers between devices  35.3 us (52%)
  waiting for transfers between devices  16.7 us (24%)
  Pallas kernels  12.2 us (18%)
  other arithmetic  1.45 us (2%)
  local copies, waits for them, and re-layouts  1.33 us (2%)
  between operations  0.91 us (1%)
    all_to_all x1, starting transfers between devices, body(): second = lax.all_to_all(copies, deep_axes, 0, 0)  10.8 us
    all_to_all x1, starting transfers between devices, body(): first = lax.all_to_all(null_copies, wide_axes, 0, 0)  10.5 us
    all_to_all x1, waiting for transfers between devices, body(): first = lax.all_to_all(null_copies, wide_axes, 0, 0)  9.2 us
    ppermute x2, starting transfers between devices, swap_link(): return lax.ppermute(block, SEQ, pairs + [(b, a) for a, b in pairs])  7.05 us
    ppermute x2, starting transfers between devices, swap_chip(): return lax.ppermute(block, SEQ, [(i, i ^ 1) for i in range(count)])  6.89 us
    all_to_all x1, waiting for transfers between devices, body(): second = lax.all_to_all(copies, deep_axes, 0, 0)  6.48 us
    pallas_call x1, Pallas kernels, heads_call(): pl.pallas_call(heads_kernel, grid=(STEPS,), in_specs=[block(video_rows)]...  4.86 us
    pallas_call x1, Pallas kernels, prepare_call(): pl.pallas_call(prepare_kernel, grid=(STEPS,), in_specs=[block(video_rows)...  3.26 us
  transfers between devices with their start and end apart: 6, of which 3 were waited for; matrix products, arithmetic and copies ran while one was open for 3% of the time, Pallas kernels for 8%

profile of v6, /device:TPU:1, one launch (start us, length us, event | category | flops | bytes accessed | tf_op | source)
XLA Modules:
  0.0 67.8 jit_solution(15179962186551640921)
XLA Ops:
  0.6 0.0 copy-start.5
  0.6 0.0 copy-start.3
  0.7 0.0 copy-start.4
  0.7 0.0 copy-start.2
  0.7 0.0 copy-start.1
  0.7 2.1 %stack.1.own_ref = bf16[256,1536]{1,0:T(8,128)(2,1)} custom-call(bf16[128,1536]{1,0:T(8,128)(2,1)} %key_ref.1, bf16[128,1536]{1,0:T(8,128)(2,1)} %value_ref.1), custom_call_target="tpu_custom_call" | custom-call | tf_op jit(solution)/shard_map/stack/pallas_call | solution.py:92
  2.8 0.0 copy-start
  2.8 4.6 %collective-permute-start.1 = (bf16[256,1536]{1,0:T(8,128)(2,1)}, bf16[256,1536]{1,0:T(8,128)(2,1)S(1)}, u32[]{:S(2)}, u32[]{:S(2)}) collective-permute-start(bf16[256,1536]{1,0:T(8,128)(2,1)} %stack.1.own_ref), channel_id=1, source_target_pairs={{1,2},{3,4},{5,6},{7,8},{9,10},{11,12},{13,14},{15,16},{17,18},{19... | collective-permute-start | bytes 2359304 | tf_op jit(solution)/shard_map/ppermute | solution.py:38
  7.4 0.0 copy-done.5
  7.4 0.2 reduce-window.4
  7.6 0.1 convert_reduce_fusion.2
  7.7 5.0 %collective-permute-start = (bf16[256,1536]{1,0:T(8,128)(2,1)}, bf16[256,1536]{1,0:T(8,128)(2,1)}, u32[]{:S(2)}, u32[]{:S(2)}) collective-permute-start(bf16[256,1536]{1,0:T(8,128)(2,1)} %stack.1.own_ref), channel_id=1, source_target_pairs={{0,1},{1,0},{2,3},{3,2},{4,5},{5,4},{6,7},{7,6},{8,9},{9,8},{10,11... | collective-permute-start | bytes 2359304 | tf_op jit(solution)/shard_map/ppermute | solution.py:32
  12.8 0.0 copy-done.3
  12.8 0.1 pad_dynamic-slice_fusion.2
  12.9 0.1 convert_reduce_fusion.1
  13.0 0.0 copy-done.4
  13.0 0.1 broadcast_select_fusion.1.null_ref
  13.1 0.2 fusion
  13.4 0.1 add_select_fusion.bias_ref
  13.5 0.5 broadcast_select_fusion.null_flip
  14.0 1.0 %collective-permute-done.near_ref = bf16[256,1536]{1,0:T(8,128)(2,1)} collective-permute-done((bf16[256,1536]{1,0:T(8,128)(2,1)}, bf16[256,1536]{1,0:T(8,128)(2,1)}, u32[]{:S(2)}, u32[]{:S(2)}) %collective-permute-start) | collective-permute-done | bytes 786464 | tf_op jit(solution)/shard_map/ppermute | solution.py:32
  15.0 0.0 copy-done.2
  15.0 0.0 copy-done.1
  15.0 0.0 copy-done
  15.0 3.3 %prepare.1 = (bf16[256,1536]{1,0:T(8,128)(2,1)S(1)}, bf16[256,1536]{1,0:T(8,128)(2,1)S(1)}, bf16[1536,256]{1,0:T(8,128)(2,1)S(1)}, bf16[1536,256]{1,0:T(8,128)(2...) custom-call(bf16[256,1536]{1,0:T(8,128)(2,1)S(1)} %copy-done.1, ...), custom_call_target="tpu_custom_call" | custom-call | flops 603979776 | bytes 9000000 | tf_op jit(solution)/shard_map/prepare/pallas_call | solution.py:152
  18.2 0.0 collective-permute-done.1.far_ref
  18.2 4.9 %heads.1 = (bf16[256,1536]{1,0:T(8,128)(2,1)}, bf16[256,1536]{1,0:T(8,128)(2,1)}, bf16[2,128,1536]{2,1,0:T(8,128)(2,1)}, bf16[2,128,1536]{2,1,0:T(8,128)(2,1)S(1...) custom-call(bf16[256,1536]{1,0:T(8,128)(2,1)S(1)} %get-tuple-element.29.q_ref, ...), custom_call_target="tpu_custom_call" | custom-call | flops 679477248 | bytes 9000000 | tf_op jit(solution)/shard_map/heads/pallas_call | solution.py:255
  23.1 10.5 %all-to-all-start = ((bf16[32,24,128]{2,1,0:T(8,128)(2,1)}), bf16[32,24,128]{2,1,0:T(8,128)(2,1)S(1)}, u32[]{:S(2)}, u32[]{:S(2)}) async-start(bf16[32,24,128]{2,1,0:T(8,128)(2,1)} %get-tuple-element.40), calls=%async_computation | async-start | bytes 393216 | tf_op jit(solution)/shard_map/all_to_all | solution.py:352
  33.6 2.4 %collective-permute-start.2 = (bf16[2,128,1536]{2,1,0:T(8,128)(2,1)}, bf16[2,128,1536]{2,1,0:T(8,128)(2,1)S(1)}, u32[]{:S(2)}, u32[]{:S(2)}) collective-permute-start(bf16[2,128,1536]{2,1,0:T(8,128)(2,1)} %get-tuple-element.44), channel_id=1, source_target_pairs={{1,2},{3,4},{5,6},{7,8},{9,10},{11,12},{13,14},{15,16},{17,18},{19... | collective-permute-start | bytes 2359304 | tf_op jit(solution)/shard_map/ppermute | solution.py:38
  36.0 9.2 %all-to-all-done = bf16[32,24,128]{2,1,0:T(8,128)(2,1)S(1)} async-done(((bf16[32,24,128]{2,1,0:T(8,128)(2,1)}), bf16[32,24,128]{2,1,0:T(8,128)(2,1)S(1)}, u32[]{:S(2)}, u32[]{:S(2)}) %all-to-all-start) | async-done | bytes 196640 | tf_op jit(solution)/shard_map/all_to_all | solution.py:352
  45.3 0.7 broadcast_in_dim.90
  45.9 1.9 %collective-permute-start.3 = (bf16[2,128,1536]{2,1,0:T(8,128)(2,1)S(1)}, bf16[2,128,1536]{2,1,0:T(8,128)(2,1)S(1)}, u32[]{:S(2)}, u32[]{:S(2)}) collective-permute-start(bf16[2,128,1536]{2,1,0:T(8,128)(2,1)S(1)} %get-tuple-element.45), channel_id=1, source_target_pairs={{0,1},{1,0},{2,3},{3,2},{4,5},{5,4},{6,7},{7,6},{8,9},{9,8},{10,11... | collective-permute-start | bytes 2359304 | tf_op jit(solution)/shard_map/ppermute | solution.py:32
  47.9 10.8 %all-to-all-start.1 = ((bf16[16,24,128]{2,1,0:T(8,128)(2,1)}), bf16[16,24,128]{2,1,0:T(8,128)(2,1)S(1)}, u32[]{:S(2)}, u32[]{:S(2)}) async-start(bf16[16,24,128]{2,1,0:T(8,128)(2,1)} %broadcast_in_dim.90), calls=%async_computation.1 | async-start | bytes 196608 | tf_op jit(solution)/shard_map/all_to_all | solution.py:357
  58.7 0.0 collective-permute-done.2.b_ref
  58.7 0.4 add_far.1.a_ref
  59.1 0.0 collective-permute-done.3.b_ref
  59.1 1.6 %add_near.1 = (bf16[128,1536]{1,0:T(8,128)(2,1)}, bf16[128,1536]{1,0:T(8,128)(2,1)}) custom-call(bf16[2,128,1536]{2,1,0:T(8,128)(2,1)S(1)} %add_far.1.a_ref, bf16[2,128,1536]{2,1,0:T(8,128)(2,1)S(1)} %collective-permute-done.3.b_ref), custom_call_target="tpu_custom_call" | custom-call | flops 393216 | bytes 2400000 | tf_op jit(solution)/shard_map/add_near/pallas_call | solution.py:293
  60.7 6.5 %all-to-all-done.1 = bf16[16,24,128]{2,1,0:T(8,128)(2,1)S(1)} async-done(((bf16[16,24,128]{2,1,0:T(8,128)(2,1)}), bf16[16,24,128]{2,1,0:T(8,128)(2,1)S(1)}, u32[]{:S(2)}, u32[]{:S(2)}) %all-to-all-start.1) | async-done | bytes 98336 | tf_op jit(solution)/shard_map/all_to_all | solution.py:357
  67.2 0.6 reshape.166
  (14 shorter events, 0.2 us)
Async XLA Ops:
  0.6 6.8 %copy-start.5 = (s32[1,4]{1,0:T(1,128)S(1)}, s32[1,4]{1,0:T(1,128)}, u32[]{:S(2)}) copy-start(s32[1,4]{1,0:T(1,128)} %param.12) | copy-start | bytes 52
  0.6 12.1 %copy-start.3 = (s32[4096]{0:T(1024)S(1)}, s32[4096]{0:T(1024)}, u32[]{:S(2)}) copy-start(s32[4096]{0:T(1024)} %param.11) | copy-start | bytes 49156
  0.7 12.3 %copy-start.4 = (bf16[2,1536]{1,0:T(2,128)(2,1)S(1)}, bf16[2,1536]{1,0:T(2,128)(2,1)}, u32[]{:S(2)}) copy-start(bf16[2,1536]{1,0:T(2,128)(2,1)} %param.10) | copy-start | bytes 18436
  0.7 14.3 %copy-start.2 = (bf16[256,1536]{1,0:T(8,128)(2,1)S(1)}, bf16[256,1536]{1,0:T(8,128)(2,1)}, u32[]{:S(2)}) copy-start(bf16[256,1536]{1,0:T(8,128)(2,1)} %g_in.1) | copy-start | bytes 2359300
  0.7 14.3 %copy-start.1 = (bf16[256,1536]{1,0:T(8,128)(2,1)S(1)}, bf16[256,1536]{1,0:T(8,128)(2,1)}, u32[]{:S(2)}) copy-start(bf16[256,1536]{1,0:T(8,128)(2,1)} %q_in.1) | copy-start | bytes 2359300
  2.8 12.2 %copy-start = (bf16[256,1536]{1,0:T(8,128)(2,1)S(1)}, bf16[256,1536]{1,0:T(8,128)(2,1)}, u32[]{:S(2)}) copy-start(bf16[256,1536]{1,0:T(8,128)(2,1)} %stack.1.own_ref) | copy-start | bytes 2359300
  2.8 15.5 %collective-permute-start.1 = (bf16[256,1536]{1,0:T(8,128)(2,1)}, bf16[256,1536]{1,0:T(8,128)(2,1)S(1)}, u32[]{:S(2)}, u32[]{:S(2)}) collective-permute-start(bf16[256,1536]{1,0:T(8,128)(2,1)} %stack.1.own_ref), channel_id=1, source_target_pairs={{1,2},{3,4},{5,6},{7,8},{9,10},{11,12},{13,14},{15,16},{17,18},{19... | collective-permute-start | bytes 2359304 | tf_op jit(solution)/shard_map/ppermute | solution.py:38
  7.7 7.2 %collective-permute-start = (bf16[256,1536]{1,0:T(8,128)(2,1)}, bf16[256,1536]{1,0:T(8,128)(2,1)}, u32[]{:S(2)}, u32[]{:S(2)}) collective-permute-start(bf16[256,1536]{1,0:T(8,128)(2,1)} %stack.1.own_ref), channel_id=1, source_target_pairs={{0,1},{1,0},{2,3},{3,2},{4,5},{5,4},{6,7},{7,6},{8,9},{9,8},{10,11... | collective-permute-start | bytes 2359304 | tf_op jit(solution)/shard_map/ppermute | solution.py:32
  23.1 22.1 %all-to-all-start = ((bf16[32,24,128]{2,1,0:T(8,128)(2,1)}), bf16[32,24,128]{2,1,0:T(8,128)(2,1)S(1)}, u32[]{:S(2)}, u32[]{:S(2)}) async-start(bf16[32,24,128]{2,1,0:T(8,128)(2,1)} %get-tuple-element.40), calls=%async_computation | async-start | bytes 393216 | tf_op jit(solution)/shard_map/all_to_all | solution.py:352
  33.6 25.1 %collective-permute-start.2 = (bf16[2,128,1536]{2,1,0:T(8,128)(2,1)}, bf16[2,128,1536]{2,1,0:T(8,128)(2,1)S(1)}, u32[]{:S(2)}, u32[]{:S(2)}) collective-permute-start(bf16[2,128,1536]{2,1,0:T(8,128)(2,1)} %get-tuple-element.44), channel_id=1, source_target_pairs={{1,2},{3,4},{5,6},{7,8},{9,10},{11,12},{13,14},{15,16},{17,18},{19... | collective-permute-start | bytes 2359304 | tf_op jit(solution)/shard_map/ppermute | solution.py:38
  45.9 13.2 %collective-permute-start.3 = (bf16[2,128,1536]{2,1,0:T(8,128)(2,1)S(1)}, bf16[2,128,1536]{2,1,0:T(8,128)(2,1)S(1)}, u32[]{:S(2)}, u32[]{:S(2)}) collective-permute-start(bf16[2,128,1536]{2,1,0:T(8,128)(2,1)S(1)} %get-tuple-element.45), channel_id=1, source_target_pairs={{0,1},{1,0},{2,3},{3,2},{4,5},{5,4},{6,7},{7,6},{8,9},{9,8},{10,11... | collective-permute-start | bytes 2359304 | tf_op jit(solution)/shard_map/ppermute | solution.py:32
  47.9 19.3 %all-to-all-start.1 = ((bf16[16,24,128]{2,1,0:T(8,128)(2,1)}), bf16[16,24,128]{2,1,0:T(8,128)(2,1)S(1)}, u32[]{:S(2)}, u32[]{:S(2)}) async-start(bf16[16,24,128]{2,1,0:T(8,128)(2,1)} %broadcast_in_dim.90), calls=%async_computation.1 | async-start | bytes 196608 | tf_op jit(solution)/shard_map/all_to_all | solution.py:357

commit v7 on v6

--- a/solution.py
+++ b/solution.py
@@ -18,7 +18,7 @@
 SEQ_PARTS = (("yl", 4), ("x", 4), ("core", 2))
 CLIP = tuple(name for name, _ in CLIP_PARTS)
 SEQ = tuple(name for name, _ in SEQ_PARTS)
-VMEM_LIMIT = 60 * 1024 * 1024
+STACK_LIMIT = 4 * 1024 * 1024
 HEADS_LIMIT = 36 * 1024 * 1024
 PREPARE_LIMIT = 24 * 1024 * 1024
 ADD_LIMIT = 8 * 1024 * 1024
@@ -69,22 +69,14 @@
         copy.wait()
 
 
-def stack_kernel(key_ref, value_ref, out_ref, held, in_sems, out_sems):
-    rows = held.shape[1]
-    pieces = [pl.ds(i * rows, rows) for i in range(key_ref.shape[0] // rows)]
-    sources = [ref.at[piece] for ref in (key_ref, value_ref) for piece in pieces]
-    arrive = [
-        pltpu.make_async_copy(src, held.at[i], in_sems.at[i]) for i, src in enumerate(sources)
-    ]
-    leave = [
-        pltpu.make_async_copy(held.at[i], out_ref.at[pl.ds(i * rows, rows)], out_sems.at[i])
-        for i in range(len(sources))
-    ]
-    start(arrive)
-    for first, second in zip(arrive, leave):
-        first.wait()
-        second.start()
-    wait(leave)
+def stack_kernel(key_ref, value_ref, out_ref, sems):
+    rows = key_ref.shape[0]
+    copies = [
+        pltpu.make_async_copy(ref, out_ref.at[pl.ds(i * rows, rows)], sems.at[i])
+        for i, ref in enumerate((key_ref, value_ref))
+    ]
+    start(copies)
+    wait(copies)
 
 
 def stack_call(keys, values):
@@ -92,14 +84,10 @@
     return pl.pallas_call(
         stack_kernel,
         in_specs=[pl.BlockSpec(memory_space=pl.ANY)] * 2,
-        out_specs=pl.BlockSpec(memory_space=pl.ANY),
+        out_specs=pl.BlockSpec(memory_space=pltpu.VMEM),
         out_shape=jax.ShapeDtypeStruct((2 * rows, width), keys.dtype),
-        scratch_shapes=[
-            pltpu.VMEM((4, rows // 2, width), keys.dtype),
-            pltpu.SemaphoreType.DMA((4,)),
-            pltpu.SemaphoreType.DMA((4,)),
-        ],
-        compiler_params=pltpu.CompilerParams(vmem_limit_bytes=VMEM_LIMIT),
+        scratch_shapes=[pltpu.SemaphoreType.DMA((2,))],
+        compiler_params=pltpu.CompilerParams(vmem_limit_bytes=STACK_LIMIT),
         name="stack",
     )(keys, values)
 

time: 68.2 us -> 68.2 us (level)
  local copies, waits for them, and re-layouts: 1.33 us -> 3.38 us
  Pallas kernels: 12.2 us -> 10.5 us
  starting transfers between devices: 35.3 us -> 34.5 us
    unnamed x12, local copies, waits for them, and re-layouts: 0.03 us -> 2.07 us
    pallas_call x1, Pallas kernels: 2.07 us -> 0.39 us  [stack_call(): pl.pallas_call(stack_kernel, in_specs=[pl.BlockSpec(memory_space=pl.ANY)]...]
  transfers between devices with their start and end apart: 6 -> 6, of which waited for: 3 -> 3; matrix products, arithmetic and copies ran while one was open for 3% -> 4% of each run, Pallas kernels for 8% -> 8%
where the time goes in v7:
time: 68.2 us; the launch traced here: 67.8 us
  starting transfers between devices  34.5 us (51%)
  waiting for transfers between devices  16.4 us (24%)
  Pallas kernels  10.5 us (15%)
  local copies, waits for them, and re-layouts  3.38 us (5%)
  other arithmetic  2.1 us (3%)
  between operations  0.87 us (1%)
    all_to_all x1, starting transfers between devices, body(): second = lax.all_to_all(copies, deep_axes, 0, 0)  10.8 us
    all_to_all x1, starting transfers between devices, body(): first = lax.all_to_all(null_copies, wide_axes, 0, 0)  9.89 us
    all_to_all x1, waiting for transfers between devices, body(): first = lax.all_to_all(null_copies, wide_axes, 0, 0)  9.2 us
    ppermute x2, starting transfers between devices, swap_link(): return lax.ppermute(block, SEQ, pairs + [(b, a) for a, b in pairs])  6.92 us
    ppermute x2, starting transfers between devices, swap_chip(): return lax.ppermute(block, SEQ, [(i, i ^ 1) for i in range(count)])  6.89 us
    all_to_all x1, waiting for transfers between devices, body(): second = lax.all_to_all(copies, deep_axes, 0, 0)  6.48 us
    pallas_call x1, Pallas kernels, heads_call(): pl.pallas_call(heads_kernel, grid=(STEPS,), in_specs=[block(video_rows)]...  4.86 us
    pallas_call x1, Pallas kernels, prepare_call(): pl.pallas_call(prepare_kernel, grid=(STEPS,), in_specs=[block(video_rows)...  3.25 us
  transfers between devices with their start and end apart: 6, of which 3 were waited for; matrix products, arithmetic and copies ran while one was open for 4% of the time, Pallas kernels for 8%

profile of v7, /device:TPU:1, one launch (start us, length us, event | category | flops | bytes accessed | tf_op | source)
XLA Modules:
  0.0 67.8 jit_solution(5156373375364420328)
XLA Ops:
  0.6 0.0 copy-start.1
  0.6 0.0 copy-start.2
  0.7 1.1 %copy-done.2 = bf16[128,1536]{1,0:T(8,128)(2,1)S(1)} copy-done((bf16[128,1536]{1,0:T(8,128)(2,1)S(1)}, bf16[128,1536]{1,0:T(8,128)(2,1)}, u32[]{:S(2)}) %copy-start.2) | copy-done | bytes 393240
  1.7 0.0 copy-start.3
  1.7 1.0 %copy-done.3 = bf16[128,1536]{1,0:T(8,128)(2,1)S(1)} copy-done((bf16[128,1536]{1,0:T(8,128)(2,1)S(1)}, bf16[128,1536]{1,0:T(8,128)(2,1)}, u32[]{:S(2)}) %copy-start.3) | copy-done | bytes 393240
  2.7 0.0 copy-start.4
  2.7 0.0 copy-start.5
  2.7 0.0 copy-start
  2.7 0.4 stack.1.own_ref
  3.1 4.5 %collective-permute-start.1 = (bf16[256,1536]{1,0:T(8,128)(2,1)S(1)}, bf16[256,1536]{1,0:T(8,128)(2,1)S(1)}, u32[]{:S(2)}, u32[]{:S(2)}) collective-permute-start(bf16[256,1536]{1,0:T(8,128)(2,1)S(1)} %stack.1.own_ref), channel_id=1, source_target_pairs={{1,2},{3,4},{5,6},{7,8},{9,10},{11,12},{13,14},{15,16},{17,18},{19... | collective-permute-start | bytes 2359304 | tf_op jit(solution)/shard_map/ppermute | solution.py:38
  7.6 0.8 %reduce-window.4 = s32[4,1]{0,1:T(1,128)S(1)} reduce-window(s32[4,1]{0,1:T(1,128)} %bitcast.7, s32[]{:T(128)} %constant.63.clone.1), window={size=4x1 pad=3_0x0_0}, to_apply=%region_0.0 | reduce-window | flops 12 | bytes 36 | tf_op jit(solution)/shard_map/reduce-window
  8.5 0.1 convert_reduce_fusion.2
  8.6 5.0 %collective-permute-start = (bf16[256,1536]{1,0:T(8,128)(2,1)S(1)}, bf16[256,1536]{1,0:T(8,128)(2,1)}, u32[]{:S(2)}, u32[]{:S(2)}) collective-permute-start(bf16[256,1536]{1,0:T(8,128)(2,1)S(1)} %stack.1.own_ref), channel_id=1, source_target_pairs={{0,1},{1,0},{2,3},{3,2},{4,5},{5,4},{6,7},{7,6},{8,9},{9,8},{10,11... | collective-permute-start | bytes 2359304 | tf_op jit(solution)/shard_map/ppermute | solution.py:32
  13.6 0.0 copy-done.4
  13.6 0.1 pad_dynamic-slice_fusion.2
  13.7 0.1 convert_reduce_fusion.1
  13.8 0.0 copy-done.5
  13.9 0.1 broadcast_select_fusion.1.null_ref
  14.0 0.2 fusion
  14.2 0.1 add_select_fusion.bias_ref
  14.3 0.5 broadcast_select_fusion.null_flip
  14.8 0.8 %collective-permute-done.near_ref = bf16[256,1536]{1,0:T(8,128)(2,1)} collective-permute-done((bf16[256,1536]{1,0:T(8,128)(2,1)S(1)}, bf16[256,1536]{1,0:T(8,128)(2,1)}, u32[]{:S(2)}, u32[]{:S(2)}) %collective-permute-start) | collective-permute-done | bytes 786464 | tf_op jit(solution)/shard_map/ppermute | solution.py:32
  15.6 0.0 copy-done.1
  15.6 0.0 copy-done
  15.6 3.3 %prepare.1 = (bf16[256,1536]{1,0:T(8,128)(2,1)S(1)}, bf16[256,1536]{1,0:T(8,128)(2,1)S(1)}, bf16[1536,256]{1,0:T(8,128)(2,1)S(1)}, bf16[1536,256]{1,0:T(8,128)(2...) custom-call(bf16[256,1536]{1,0:T(8,128)(2,1)S(1)} %copy-done, ...), custom_call_target="tpu_custom_call" | custom-call | flops 603979776 | bytes 9000000 | tf_op jit(solution)/shard_map/prepare/pallas_call | solution.py:140
  18.9 0.0 collective-permute-done.1.far_ref
  18.9 4.9 %heads.1 = (bf16[256,1536]{1,0:T(8,128)(2,1)}, bf16[256,1536]{1,0:T(8,128)(2,1)}, bf16[2,128,1536]{2,1,0:T(8,128)(2,1)}, bf16[2,128,1536]{2,1,0:T(8,128)(2,1)S(1...) custom-call(bf16[256,1536]{1,0:T(8,128)(2,1)S(1)} %get-tuple-element.29.q_ref, ...), custom_call_target="tpu_custom_call" | custom-call | flops 679477248 | bytes 9000000 | tf_op jit(solution)/shard_map/heads/pallas_call | solution.py:243
  23.7 9.9 %all-to-all-start = ((bf16[32,24,128]{2,1,0:T(8,128)(2,1)}), bf16[32,24,128]{2,1,0:T(8,128)(2,1)S(1)}, u32[]{:S(2)}, u32[]{:S(2)}) async-start(bf16[32,24,128]{2,1,0:T(8,128)(2,1)} %get-tuple-element.40), calls=%async_computation | async-start | bytes 393216 | tf_op jit(solution)/shard_map/all_to_all | solution.py:340
  33.6 2.4 %collective-permute-start.2 = (bf16[2,128,1536]{2,1,0:T(8,128)(2,1)}, bf16[2,128,1536]{2,1,0:T(8,128)(2,1)S(1)}, u32[]{:S(2)}, u32[]{:S(2)}) collective-permute-start(bf16[2,128,1536]{2,1,0:T(8,128)(2,1)} %get-tuple-element.44), channel_id=1, source_target_pairs={{1,2},{3,4},{5,6},{7,8},{9,10},{11,12},{13,14},{15,16},{17,18},{19... | collective-permute-start | bytes 2359304 | tf_op jit(solution)/shard_map/ppermute | solution.py:38
  36.0 9.2 %all-to-all-done = bf16[32,24,128]{2,1,0:T(8,128)(2,1)S(1)} async-done(((bf16[32,24,128]{2,1,0:T(8,128)(2,1)}), bf16[32,24,128]{2,1,0:T(8,128)(2,1)S(1)}, u32[]{:S(2)}, u32[]{:S(2)}) %all-to-all-start) | async-done | bytes 196640 | tf_op jit(solution)/shard_map/all_to_all | solution.py:340
  45.3 0.7 broadcast_in_dim.90
  45.9 1.9 %collective-permute-start.3 = (bf16[2,128,1536]{2,1,0:T(8,128)(2,1)S(1)}, bf16[2,128,1536]{2,1,0:T(8,128)(2,1)S(1)}, u32[]{:S(2)}, u32[]{:S(2)}) collective-permute-start(bf16[2,128,1536]{2,1,0:T(8,128)(2,1)S(1)} %get-tuple-element.45), channel_id=1, source_target_pairs={{0,1},{1,0},{2,3},{3,2},{4,5},{5,4},{6,7},{7,6},{8,9},{9,8},{10,11... | collective-permute-start | bytes 2359304 | tf_op jit(solution)/shard_map/ppermute | solution.py:32
  47.8 10.8 %all-to-all-start.1 = ((bf16[16,24,128]{2,1,0:T(8,128)(2,1)}), bf16[16,24,128]{2,1,0:T(8,128)(2,1)S(1)}, u32[]{:S(2)}, u32[]{:S(2)}) async-start(bf16[16,24,128]{2,1,0:T(8,128)(2,1)} %broadcast_in_dim.90), calls=%async_computation.1 | async-start | bytes 196608 | tf_op jit(solution)/shard_map/all_to_all | solution.py:345
  58.7 0.0 collective-permute-done.2.b_ref
  58.7 0.4 add_far.1.a_ref
  59.1 0.0 collective-permute-done.3.b_ref
  59.1 1.6 %add_near.1 = (bf16[128,1536]{1,0:T(8,128)(2,1)}, bf16[128,1536]{1,0:T(8,128)(2,1)}) custom-call(bf16[2,128,1536]{2,1,0:T(8,128)(2,1)S(1)} %add_far.1.a_ref, bf16[2,128,1536]{2,1,0:T(8,128)(2,1)S(1)} %collective-permute-done.3.b_ref), custom_call_target="tpu_custom_call" | custom-call | flops 393216 | bytes 2400000 | tf_op jit(solution)/shard_map/add_near/pallas_call | solution.py:281
  60.7 6.5 %all-to-all-done.1 = bf16[16,24,128]{2,1,0:T(8,128)(2,1)S(1)} async-done(((bf16[16,24,128]{2,1,0:T(8,128)(2,1)}), bf16[16,24,128]{2,1,0:T(8,128)(2,1)S(1)}, u32[]{:S(2)}, u32[]{:S(2)}) %all-to-all-start.1) | async-done | bytes 98336 | tf_op jit(solution)/shard_map/all_to_all | solution.py:345
  67.2 0.6 reshape.166
  (14 shorter events, 0.2 us)
Async XLA Ops:
  0.6 15.0 %copy-start.1 = (bf16[256,1536]{1,0:T(8,128)(2,1)S(1)}, bf16[256,1536]{1,0:T(8,128)(2,1)}, u32[]{:S(2)}) copy-start(bf16[256,1536]{1,0:T(8,128)(2,1)} %g_in.1) | copy-start | bytes 2359300
  0.6 1.1 %copy-start.2 = (bf16[128,1536]{1,0:T(8,128)(2,1)S(1)}, bf16[128,1536]{1,0:T(8,128)(2,1)}, u32[]{:S(2)}) copy-start(bf16[128,1536]{1,0:T(8,128)(2,1)} %key_ref.1) | copy-start | bytes 1179652
  1.7 1.0 %copy-start.3 = (bf16[128,1536]{1,0:T(8,128)(2,1)S(1)}, bf16[128,1536]{1,0:T(8,128)(2,1)}, u32[]{:S(2)}) copy-start(bf16[128,1536]{1,0:T(8,128)(2,1)} %value_ref.1) | copy-start | bytes 1179652
  2.7 10.9 %copy-start.4 = (s32[4096]{0:T(1024)S(1)}, s32[4096]{0:T(1024)}, u32[]{:S(2)}) copy-start(s32[4096]{0:T(1024)} %param.11) | copy-start | bytes 49156
  2.7 11.1 %copy-start.5 = (bf16[2,1536]{1,0:T(2,128)(2,1)S(1)}, bf16[2,1536]{1,0:T(2,128)(2,1)}, u32[]{:S(2)}) copy-start(bf16[2,1536]{1,0:T(2,128)(2,1)} %param.10) | copy-start | bytes 18436
  2.7 12.9 %copy-start = (bf16[256,1536]{1,0:T(8,128)(2,1)S(1)}, bf16[256,1536]{1,0:T(8,128)(2,1)}, u32[]{:S(2)}) copy-start(bf16[256,1536]{1,0:T(8,128)(2,1)} %q_in.1) | copy-start | bytes 2359300
  3.1 15.7 %collective-permute-start.1 = (bf16[256,1536]{1,0:T(8,128)(2,1)S(1)}, bf16[256,1536]{1,0:T(8,128)(2,1)S(1)}, u32[]{:S(2)}, u32[]{:S(2)}) collective-permute-start(bf16[256,1536]{1,0:T(8,128)(2,1)S(1)} %stack.1.own_ref), channel_id=1, source_target_pairs={{1,2},{3,4},{5,6},{7,8},{9,10},{11,12},{13,14},{15,16},{17,18},{19... | collective-permute-start | bytes 2359304 | tf_op jit(solution)/shard_map/ppermute | solution.py:38
  8.6 7.0 %collective-permute-start = (bf16[256,1536]{1,0:T(8,128)(2,1)S(1)}, bf16[256,1536]{1,0:T(8,128)(2,1)}, u32[]{:S(2)}, u32[]{:S(2)}) collective-permute-start(bf16[256,1536]{1,0:T(8,128)(2,1)S(1)} %stack.1.own_ref), channel_id=1, source_target_pairs={{0,1},{1,0},{2,3},{3,2},{4,5},{5,4},{6,7},{7,6},{8,9},{9,8},{10,11... | collective-permute-start | bytes 2359304 | tf_op jit(solution)/shard_map/ppermute | solution.py:32
  23.7 21.5 %all-to-all-start = ((bf16[32,24,128]{2,1,0:T(8,128)(2,1)}), bf16[32,24,128]{2,1,0:T(8,128)(2,1)S(1)}, u32[]{:S(2)}, u32[]{:S(2)}) async-start(bf16[32,24,128]{2,1,0:T(8,128)(2,1)} %get-tuple-element.40), calls=%async_computation | async-start | bytes 393216 | tf_op jit(solution)/shard_map/all_to_all | solution.py:340
  33.6 25.1 %collective-permute-start.2 = (bf16[2,128,1536]{2,1,0:T(8,128)(2,1)}, bf16[2,128,1536]{2,1,0:T(8,128)(2,1)S(1)}, u32[]{:S(2)}, u32[]{:S(2)}) collective-permute-start(bf16[2,128,1536]{2,1,0:T(8,128)(2,1)} %get-tuple-element.44), channel_id=1, source_target_pairs={{1,2},{3,4},{5,6},{7,8},{9,10},{11,12},{13,14},{15,16},{17,18},{19... | collective-permute-start | bytes 2359304 | tf_op jit(solution)/shard_map/ppermute | solution.py:38
  45.9 13.2 %collective-permute-start.3 = (bf16[2,128,1536]{2,1,0:T(8,128)(2,1)S(1)}, bf16[2,128,1536]{2,1,0:T(8,128)(2,1)S(1)}, u32[]{:S(2)}, u32[]{:S(2)}) collective-permute-start(bf16[2,128,1536]{2,1,0:T(8,128)(2,1)S(1)} %get-tuple-element.45), channel_id=1, source_target_pairs={{0,1},{1,0},{2,3},{3,2},{4,5},{5,4},{6,7},{7,6},{8,9},{9,8},{10,11... | collective-permute-start | bytes 2359304 | tf_op jit(solution)/shard_map/ppermute | solution.py:32
  47.8 19.3 %all-to-all-start.1 = ((bf16[16,24,128]{2,1,0:T(8,128)(2,1)}), bf16[16,24,128]{2,1,0:T(8,128)(2,1)S(1)}, u32[]{:S(2)}, u32[]{:S(2)}) async-start(bf16[16,24,128]{2,1,0:T(8,128)(2,1)} %broadcast_in_dim.90), calls=%async_computation.1 | async-start | bytes 196608 | tf_op jit(solution)/shard_map/all_to_all | solution.py:345

commit v8 on v7

--- a/solution.py
+++ b/solution.py
@@ -18,7 +18,6 @@
 SEQ_PARTS = (("yl", 4), ("x", 4), ("core", 2))
 CLIP = tuple(name for name, _ in CLIP_PARTS)
 SEQ = tuple(name for name, _ in SEQ_PARTS)
-STACK_LIMIT = 4 * 1024 * 1024
 HEADS_LIMIT = 36 * 1024 * 1024
 PREPARE_LIMIT = 24 * 1024 * 1024
 ADD_LIMIT = 8 * 1024 * 1024
@@ -57,39 +56,6 @@
     return lax.dot_general(
         a, b, (((lhs_dim,), (rhs_dim,)), ((), ())), preferred_element_type=jnp.float32
     )
-
-
-def start(copies):
-    for copy in copies:
-        copy.start()
-
-
-def wait(copies):
-    for copy in copies:
-        copy.wait()
-
-
-def stack_kernel(key_ref, value_ref, out_ref, sems):
-    rows = key_ref.shape[0]
-    copies = [
-        pltpu.make_async_copy(ref, out_ref.at[pl.ds(i * rows, rows)], sems.at[i])
-        for i, ref in enumerate((key_ref, value_ref))
-    ]
-    start(copies)
-    wait(copies)
-
-
-def stack_call(keys, values):
-    rows, width = keys.shape
-    return pl.pallas_call(
-        stack_kernel,
-        in_specs=[pl.BlockSpec(memory_space=pl.ANY)] * 2,
-        out_specs=pl.BlockSpec(memory_space=pltpu.VMEM),
-        out_shape=jax.ShapeDtypeStruct((2 * rows, width), keys.dtype),
-        scratch_shapes=[pltpu.SemaphoreType.DMA((2,))],
-        compiler_params=pltpu.CompilerParams(vmem_limit_bytes=STACK_LIMIT),
-        name="stack",
-    )(keys, values)
 
 
 def prepare_kernel(
@@ -301,7 +267,7 @@
     seq_index = lax.axis_index(SEQ)
     total_audio = audio_rows * shards
 
-    stacked = stack_call(audio_key, audio_value)
+    stacked = jnp.stack([audio_key, audio_value]).reshape(2 * audio_rows, -1)
     far = swap_link(stacked)
 
     bounds = jnp.cumsum(clip_lengths[0])

time: 68.2 us -> 67.1 us (0.984)
  local copies, waits for them, and re-layouts: 3.38 us -> 1.32 us
  starting transfers between devices: 34.5 us -> 35.2 us
    unnamed x12 -> x10, local copies, waits for them, and re-layouts: 2.07 us -> 0.02 us
    another operation x1 -> x2, other arithmetic: 0.83 us -> 1.49 us  [the longest x1 1.31 us: body(): stacked = jnp.stack([audio_key, audio_value]).reshape(2 * audio_rows, -1)]
  transfers between devices with their start and end apart: 6 -> 6, of which waited for: 3 -> 3; matrix products, arithmetic and copies ran while one was open for 4% -> 3% of each run, Pallas kernels for 8% -> 8%
where the time goes in v8:
time: 67.1 us; the launch traced here: 66.7 us
  starting transfers between devices  35.2 us (52%)
  waiting for transfers between devices  16.4 us (24%)
  Pallas kernels  10.1 us (15%)
  other arithmetic  2.76 us (4%)
  local copies, waits for them, and re-layouts  1.32 us (2%)
  between operations  0.89 us (1%)
    all_to_all x1, starting transfers between devices, body(): second = lax.all_to_all(copies, deep_axes, 0, 0)  10.8 us
    all_to_all x1, starting transfers between devices, body(): first = lax.all_to_all(null_copies, wide_axes, 0, 0)  10.5 us
    all_to_all x1, waiting for transfers between devices, body(): first = lax.all_to_all(null_copies, wide_axes, 0, 0)  9.2 us
    ppermute x2, starting transfers between devices, swap_link(): return lax.ppermute(block, SEQ, pairs + [(b, a) for a, b in pairs])  6.92 us
    ppermute x2, starting transfers between devices, swap_chip(): return lax.ppermute(block, SEQ, [(i, i ^ 1) for i in range(count)])  6.89 us
    all_to_all x1, waiting for transfers between devices, body(): second = lax.all_to_all(copies, deep_axes, 0, 0)  6.48 us
    pallas_call x1, Pallas kernels, heads_call(): pl.pallas_call(heads_kernel, grid=(STEPS,), in_specs=[block(video_rows)]...  4.86 us
    pallas_call x1, Pallas kernels, prepare_call(): pl.pallas_call(prepare_kernel, grid=(STEPS,), in_specs=[block(video_rows)...  3.26 us
  transfers between devices with their start and end apart: 6, of which 3 were waited for; matrix products, arithmetic and copies ran while one was open for 3% of the time, Pallas kernels for 8%

profile of v8, /device:TPU:1, one launch (start us, length us, event | category | flops | bytes accessed | tf_op | source)
XLA Modules:
  0.0 66.7 jit_solution(15120273694376678077)
XLA Ops:
  0.6 0.0 copy-start.4
  0.6 0.0 copy-start.2
  0.7 0.0 copy-start.3
  0.7 0.0 copy-start
  0.7 0.0 copy-start.1
  0.7 1.3 %pad_maximum_fusion = bf16[2,128,1536]{2,1,0:T(8,128)(2,1)S(1)} fusion(bf16[1,128,1536]{2,1,0:T(8,128)(2,1)} %bitcast.12, bf16[1,128,1536]{2,1,0:T(8,128)(2,1)} %bitcast.13), kind=kLoop, calls=%fused_computation | loop fusion | flops 393216 | bytes 1572864 | tf_op jit(solution)/shard_map/stack | solution.py:270
  2.0 4.5 %collective-permute-start.1 = (bf16[256,1536]{1,0:T(8,128)(2,1)S(1)}, bf16[256,1536]{1,0:T(8,128)(2,1)S(1)}, u32[]{:S(2)}, u32[]{:S(2)}) collective-permute-start(bf16[256,1536]{1,0:T(8,128)(2,1)S(1)} %bitcast.8), channel_id=1, source_target_pairs={{1,2},{3,4},{5,6},{7,8},{9,10},{11,12},{13,14},{15,16},{17,18},{19... | collective-permute-start | bytes 2359304 | tf_op jit(solution)/shard_map/ppermute | solution.py:37
  6.5 0.0 copy-done.4
  6.5 0.2 reduce-window.4
  6.7 0.1 convert_reduce_fusion.2
  6.8 5.0 %collective-permute-start = (bf16[256,1536]{1,0:T(8,128)(2,1)S(1)}, bf16[256,1536]{1,0:T(8,128)(2,1)}, u32[]{:S(2)}, u32[]{:S(2)}) collective-permute-start(bf16[256,1536]{1,0:T(8,128)(2,1)S(1)} %bitcast.9), channel_id=1, source_target_pairs={{0,1},{1,0},{2,3},{3,2},{4,5},{5,4},{6,7},{7,6},{8,9},{9,8},{10,11... | collective-permute-start | bytes 2359304 | tf_op jit(solution)/shard_map/ppermute | solution.py:31
  11.9 0.0 copy-done.2
  11.9 0.1 pad_dynamic-slice_fusion.2
  12.0 0.1 convert_reduce_fusion.1
  12.1 0.0 copy-done.3
  12.1 0.1 broadcast_select_fusion.1.null_ref
  12.2 0.2 fusion
  12.5 0.1 add_select_fusion.bias_ref
  12.6 0.5 broadcast_select_fusion.null_flip
  13.1 0.8 %collective-permute-done.near_ref = bf16[256,1536]{1,0:T(8,128)(2,1)} collective-permute-done((bf16[256,1536]{1,0:T(8,128)(2,1)S(1)}, bf16[256,1536]{1,0:T(8,128)(2,1)}, u32[]{:S(2)}, u32[]{:S(2)}) %collective-permute-start) | collective-permute-done | bytes 786464 | tf_op jit(solution)/shard_map/ppermute | solution.py:31
  13.8 0.0 copy-done
  13.8 0.0 copy-done.1
  13.8 3.3 %prepare.1 = (bf16[256,1536]{1,0:T(8,128)(2,1)S(1)}, bf16[256,1536]{1,0:T(8,128)(2,1)S(1)}, bf16[1536,256]{1,0:T(8,128)(2,1)S(1)}, bf16[1536,256]{1,0:T(8,128)(2...) custom-call(bf16[256,1536]{1,0:T(8,128)(2,1)S(1)} %copy-done, ...), custom_call_target="tpu_custom_call" | custom-call | flops 603979776 | bytes 9000000 | tf_op jit(solution)/shard_map/prepare/pallas_call | solution.py:106
  17.1 0.0 collective-permute-done.1.far_ref
  17.1 4.9 %heads.1 = (bf16[256,1536]{1,0:T(8,128)(2,1)}, bf16[256,1536]{1,0:T(8,128)(2,1)}, bf16[2,128,1536]{2,1,0:T(8,128)(2,1)}, bf16[2,128,1536]{2,1,0:T(8,128)(2,1)S(1...) custom-call(bf16[256,1536]{1,0:T(8,128)(2,1)S(1)} %get-tuple-element.29.q_ref, ...), custom_call_target="tpu_custom_call" | custom-call | flops 679477248 | bytes 9000000 | tf_op jit(solution)/shard_map/heads/pallas_call | solution.py:209
  22.0 10.5 %all-to-all-start = ((bf16[32,24,128]{2,1,0:T(8,128)(2,1)}), bf16[32,24,128]{2,1,0:T(8,128)(2,1)S(1)}, u32[]{:S(2)}, u32[]{:S(2)}) async-start(bf16[32,24,128]{2,1,0:T(8,128)(2,1)} %get-tuple-element.40), calls=%async_computation | async-start | bytes 393216 | tf_op jit(solution)/shard_map/all_to_all | solution.py:306
  32.5 2.4 %collective-permute-start.2 = (bf16[2,128,1536]{2,1,0:T(8,128)(2,1)}, bf16[2,128,1536]{2,1,0:T(8,128)(2,1)S(1)}, u32[]{:S(2)}, u32[]{:S(2)}) collective-permute-start(bf16[2,128,1536]{2,1,0:T(8,128)(2,1)} %get-tuple-element.44), channel_id=1, source_target_pairs={{1,2},{3,4},{5,6},{7,8},{9,10},{11,12},{13,14},{15,16},{17,18},{19... | collective-permute-start | bytes 2359304 | tf_op jit(solution)/shard_map/ppermute | solution.py:37
  34.9 9.2 %all-to-all-done = bf16[32,24,128]{2,1,0:T(8,128)(2,1)S(1)} async-done(((bf16[32,24,128]{2,1,0:T(8,128)(2,1)}), bf16[32,24,128]{2,1,0:T(8,128)(2,1)S(1)}, u32[]{:S(2)}, u32[]{:S(2)}) %all-to-all-start) | async-done | bytes 196640 | tf_op jit(solution)/shard_map/all_to_all | solution.py:306
  44.2 0.6 broadcast_in_dim.90
  44.8 1.9 %collective-permute-start.3 = (bf16[2,128,1536]{2,1,0:T(8,128)(2,1)S(1)}, bf16[2,128,1536]{2,1,0:T(8,128)(2,1)S(1)}, u32[]{:S(2)}, u32[]{:S(2)}) collective-permute-start(bf16[2,128,1536]{2,1,0:T(8,128)(2,1)S(1)} %get-tuple-element.45), channel_id=1, source_target_pairs={{0,1},{1,0},{2,3},{3,2},{4,5},{5,4},{6,7},{7,6},{8,9},{9,8},{10,11... | collective-permute-start | bytes 2359304 | tf_op jit(solution)/shard_map/ppermute | solution.py:31
  46.7 10.8 %all-to-all-start.1 = ((bf16[16,24,128]{2,1,0:T(8,128)(2,1)}), bf16[16,24,128]{2,1,0:T(8,128)(2,1)S(1)}, u32[]{:S(2)}, u32[]{:S(2)}) async-start(bf16[16,24,128]{2,1,0:T(8,128)(2,1)} %broadcast_in_dim.90), calls=%async_computation.1 | async-start | bytes 196608 | tf_op jit(solution)/shard_map/all_to_all | solution.py:311
  57.6 0.0 collective-permute-done.2.b_ref
  57.6 0.4 add_far.1.a_ref
  58.0 0.0 collective-permute-done.3.b_ref
  58.0 1.6 %add_near.1 = (bf16[128,1536]{1,0:T(8,128)(2,1)}, bf16[128,1536]{1,0:T(8,128)(2,1)}) custom-call(bf16[2,128,1536]{2,1,0:T(8,128)(2,1)S(1)} %add_far.1.a_ref, bf16[2,128,1536]{2,1,0:T(8,128)(2,1)S(1)} %collective-permute-done.3.b_ref), custom_call_target="tpu_custom_call" | custom-call | flops 393216 | bytes 2400000 | tf_op jit(solution)/shard_map/add_near/pallas_call | solution.py:247
  59.6 6.5 %all-to-all-done.1 = bf16[16,24,128]{2,1,0:T(8,128)(2,1)S(1)} async-done(((bf16[16,24,128]{2,1,0:T(8,128)(2,1)}), bf16[16,24,128]{2,1,0:T(8,128)(2,1)S(1)}, u32[]{:S(2)}, u32[]{:S(2)}) %all-to-all-start.1) | async-done | bytes 98336 | tf_op jit(solution)/shard_map/all_to_all | solution.py:311
  66.1 0.6 reshape.170
  (14 shorter events, 0.2 us)
Async XLA Ops:
  0.6 5.9 %copy-start.4 = (s32[1,4]{1,0:T(1,128)S(1)}, s32[1,4]{1,0:T(1,128)}, u32[]{:S(2)}) copy-start(s32[1,4]{1,0:T(1,128)} %param.12) | copy-start | bytes 52
  0.6 11.2 %copy-start.2 = (s32[4096]{0:T(1024)S(1)}, s32[4096]{0:T(1024)}, u32[]{:S(2)}) copy-start(s32[4096]{0:T(1024)} %param.11) | copy-start | bytes 49156
  0.7 11.4 %copy-start.3 = (bf16[2,1536]{1,0:T(2,128)(2,1)S(1)}, bf16[2,1536]{1,0:T(2,128)(2,1)}, u32[]{:S(2)}) copy-start(bf16[2,1536]{1,0:T(2,128)(2,1)} %param.10) | copy-start | bytes 18436
  0.7 13.2 %copy-start = (bf16[256,1536]{1,0:T(8,128)(2,1)S(1)}, bf16[256,1536]{1,0:T(8,128)(2,1)}, u32[]{:S(2)}) copy-start(bf16[256,1536]{1,0:T(8,128)(2,1)} %q_in.1) | copy-start | bytes 2359300
  0.7 13.2 %copy-start.1 = (bf16[256,1536]{1,0:T(8,128)(2,1)S(1)}, bf16[256,1536]{1,0:T(8,128)(2,1)}, u32[]{:S(2)}) copy-start(bf16[256,1536]{1,0:T(8,128)(2,1)} %g_in.1) | copy-start | bytes 2359300
  2.0 15.1 %collective-permute-start.1 = (bf16[256,1536]{1,0:T(8,128)(2,1)S(1)}, bf16[256,1536]{1,0:T(8,128)(2,1)S(1)}, u32[]{:S(2)}, u32[]{:S(2)}) collective-permute-start(bf16[256,1536]{1,0:T(8,128)(2,1)S(1)} %bitcast.8), channel_id=1, source_target_pairs={{1,2},{3,4},{5,6},{7,8},{9,10},{11,12},{13,14},{15,16},{17,18},{19... | collective-permute-start | bytes 2359304 | tf_op jit(solution)/shard_map/ppermute | solution.py:37
  6.8 7.0 %collective-permute-start = (bf16[256,1536]{1,0:T(8,128)(2,1)S(1)}, bf16[256,1536]{1,0:T(8,128)(2,1)}, u32[]{:S(2)}, u32[]{:S(2)}) collective-permute-start(bf16[256,1536]{1,0:T(8,128)(2,1)S(1)} %bitcast.9), channel_id=1, source_target_pairs={{0,1},{1,0},{2,3},{3,2},{4,5},{5,4},{6,7},{7,6},{8,9},{9,8},{10,11... | collective-permute-start | bytes 2359304 | tf_op jit(solution)/shard_map/ppermute | solution.py:31
  22.0 22.1 %all-to-all-start = ((bf16[32,24,128]{2,1,0:T(8,128)(2,1)}), bf16[32,24,128]{2,1,0:T(8,128)(2,1)S(1)}, u32[]{:S(2)}, u32[]{:S(2)}) async-start(bf16[32,24,128]{2,1,0:T(8,128)(2,1)} %get-tuple-element.40), calls=%async_computation | async-start | bytes 393216 | tf_op jit(solution)/shard_map/all_to_all | solution.py:306
  32.5 25.1 %collective-permute-start.2 = (bf16[2,128,1536]{2,1,0:T(8,128)(2,1)}, bf16[2,128,1536]{2,1,0:T(8,128)(2,1)S(1)}, u32[]{:S(2)}, u32[]{:S(2)}) collective-permute-start(bf16[2,128,1536]{2,1,0:T(8,128)(2,1)} %get-tuple-element.44), channel_id=1, source_target_pairs={{1,2},{3,4},{5,6},{7,8},{9,10},{11,12},{13,14},{15,16},{17,18},{19... | collective-permute-start | bytes 2359304 | tf_op jit(solution)/shard_map/ppermute | solution.py:37
  44.8 13.2 %collective-permute-start.3 = (bf16[2,128,1536]{2,1,0:T(8,128)(2,1)S(1)}, bf16[2,128,1536]{2,1,0:T(8,128)(2,1)S(1)}, u32[]{:S(2)}, u32[]{:S(2)}) collective-permute-start(bf16[2,128,1536]{2,1,0:T(8,128)(2,1)S(1)} %get-tuple-element.45), channel_id=1, source_target_pairs={{0,1},{1,0},{2,3},{3,2},{4,5},{5,4},{6,7},{7,6},{8,9},{9,8},{10,11... | collective-permute-start | bytes 2359304 | tf_op jit(solution)/shard_map/ppermute | solution.py:31
  46.7 19.3 %all-to-all-start.1 = ((bf16[16,24,128]{2,1,0:T(8,128)(2,1)}), bf16[16,24,128]{2,1,0:T(8,128)(2,1)S(1)}, u32[]{:S(2)}, u32[]{:S(2)}) async-start(bf16[16,24,128]{2,1,0:T(8,128)(2,1)} %broadcast_in_dim.90), calls=%async_computation.1 | async-start | bytes 196608 | tf_op jit(solution)/shard_map/all_to_all | solution.py:311

commit v9 on v8

--- a/solution.py
+++ b/solution.py
@@ -169,9 +169,10 @@
         query_grad = dot(keys_flip[i], score_grads[i], 1, 0)
         query_grad = query_grad + dot(near_keys_flip[cols[i], :], near_score_grads[i], 1, 0)
         dq_ref[:, cols[i]] = query_grad.astype(jnp.bfloat16).T
-        q = q_ref[:, cols[i]]
+        both = jnp.concatenate([near_score_grads[i], score_grads[i]], axis=0)
+        key_term = dot(both, q_ref[:, cols[i]], 1, 0)
         terms = (
-            (dot(score_grads[i], q, 1, 0), dot(near_score_grads[i], q, 1, 0)),
+            (key_term[2 * rows :], key_term[: 2 * rows]),
             (
                 dot(exponents[i], (flips[i] * shares[i]).astype(jnp.bfloat16), 1, 1),
                 dot(near_exponent[i], (flips[i] * near_shares[i]).astype(jnp.bfloat16), 1, 1),
@@ -303,11 +304,10 @@
         q_held, g_held, far, near_parts, null_rows, null_flip, bias, valid, lax.axis_size(wide_axes)
     )
     far_back = swap_link(far_grad)
+    near_back = swap_chip(near_grad)
     first = lax.all_to_all(null_copies, wide_axes, 0, 0)
     partial = sum_peers(first).astype(jnp.bfloat16)
     copies = jnp.broadcast_to(partial[None], (lax.axis_size(deep_axes), *partial.shape))
-    copies, near_grad = lax.optimization_barrier((copies, near_grad))
-    near_back = swap_chip(near_grad)
     second = lax.all_to_all(copies, deep_axes, 0, 0)
     part = add_call(own_grad, far_back, False, 4_000_000, "add_far")
     grads = add_call(part, near_back, True, 2_400_000, "add_near")

time: 67.1 us -> 70 us (1.043)
  blocking collectives: 0 us -> 20.8 us
  waiting for transfers between devices: 16.4 us -> 7.25 us
  starting transfers between devices: 35.2 us -> 26.5 us
    all_to_all x0 -> x1, blocking collectives: none -> 20.8 us  [body(): first = lax.all_to_all(null_copies, wide_axes, 0, 0)]
    all_to_all x1 -> x0, starting transfers between devices: 10.5 us -> none  [body(): first = lax.all_to_all(null_copies, wide_axes, 0, 0)]
    all_to_all x1 -> x0, waiting for transfers between devices: 9.2 us -> none  [body(): first = lax.all_to_all(null_copies, wide_axes, 0, 0)]
    all_to_all x1, starting transfers between devices: 10.8 us -> 12.5 us  [body(): second = lax.all_to_all(copies, deep_axes, 0, 0)]
  transfers between devices with their start and end apart: 6 -> 5, of which waited for: 3 -> 2; matrix products, arithmetic and copies ran while one was open for 3% -> 3% of each run, Pallas kernels for 8% -> 8%
where the time goes in v9:
time: 70 us; the launch traced here: 69.7 us
  starting transfers between devices  26.5 us (38%)
  blocking collectives  20.8 us (30%)
  Pallas kernels  10.1 us (14%)
  waiting for transfers between devices  7.25 us (10%)
  other arithmetic  2.76 us (4%)
  local copies, waits for them, and re-layouts  1.32 us (2%)
  between operations  0.88 us (1%)
    all_to_all x1, blocking collectives, body(): first = lax.all_to_all(null_copies, wide_axes, 0, 0)  20.8 us
    all_to_all x1, starting transfers between devices, body(): second = lax.all_to_all(copies, deep_axes, 0, 0)  12.5 us
    ppermute x2, starting transfers between devices, swap_link(): return lax.ppermute(block, SEQ, pairs + [(b, a) for a, b in pairs])  7.17 us
    ppermute x2, starting transfers between devices, swap_chip(): return lax.ppermute(block, SEQ, [(i, i ^ 1) for i in range(count)])  6.9 us
    all_to_all x1, waiting for transfers between devices, body(): second = lax.all_to_all(copies, deep_axes, 0, 0)  6.48 us
    pallas_call x1, Pallas kernels, heads_call(): pl.pallas_call(heads_kernel, grid=(STEPS,), in_specs=[block(video_rows)]...  4.83 us
    pallas_call x1, Pallas kernels, prepare_call(): pl.pallas_call(prepare_kernel, grid=(STEPS,), in_specs=[block(video_rows)...  3.26 us
    pallas_call x2, Pallas kernels, add_call(): pl.pallas_call(add_kernel, grid=(steps,), in_specs=[both, both], out_spec...  1.98 us
  transfers between devices with their start and end apart: 5, of which 2 were waited for; matrix products, arithmetic and copies ran while one was open for 3% of the time, Pallas kernels for 8%

profile of v9, /device:TPU:1, one launch (start us, length us, event | category | flops | bytes accessed | tf_op | source)
XLA Modules:
  0.0 69.7 jit_solution(13964912791087018645)
XLA Ops:
  0.6 0.0 copy-start.4
  0.6 0.0 copy-start.2
  0.7 0.0 copy-start.3
  0.7 0.0 copy-start
  0.7 0.0 copy-start.1
  0.7 1.3 %pad_maximum_fusion = bf16[2,128,1536]{2,1,0:T(8,128)(2,1)S(1)} fusion(bf16[1,128,1536]{2,1,0:T(8,128)(2,1)} %bitcast.12, bf16[1,128,1536]{2,1,0:T(8,128)(2,1)} %bitcast.13), kind=kLoop, calls=%fused_computation | loop fusion | flops 393216 | bytes 1572864 | tf_op jit(solution)/shard_map/stack | solution.py:271
  2.0 4.5 %collective-permute-start.1 = (bf16[256,1536]{1,0:T(8,128)(2,1)S(1)}, bf16[256,1536]{1,0:T(8,128)(2,1)S(1)}, u32[]{:S(2)}, u32[]{:S(2)}) collective-permute-start(bf16[256,1536]{1,0:T(8,128)(2,1)S(1)} %bitcast.8), channel_id=1, source_target_pairs={{1,2},{3,4},{5,6},{7,8},{9,10},{11,12},{13,14},{15,16},{17,18},{19... | collective-permute-start | bytes 2359304 | tf_op jit(solution)/shard_map/ppermute | solution.py:37
  6.5 0.0 copy-done.4
  6.5 0.2 reduce-window.4
  6.7 0.1 convert_reduce_fusion.2
  6.8 5.0 %collective-permute-start = (bf16[256,1536]{1,0:T(8,128)(2,1)S(1)}, bf16[256,1536]{1,0:T(8,128)(2,1)}, u32[]{:S(2)}, u32[]{:S(2)}) collective-permute-start(bf16[256,1536]{1,0:T(8,128)(2,1)S(1)} %bitcast.9), channel_id=1, source_target_pairs={{0,1},{1,0},{2,3},{3,2},{4,5},{5,4},{6,7},{7,6},{8,9},{9,8},{10,11... | collective-permute-start | bytes 2359304 | tf_op jit(solution)/shard_map/ppermute | solution.py:31
  11.9 0.0 copy-done.2
  11.9 0.1 pad_dynamic-slice_fusion.2
  12.0 0.1 convert_reduce_fusion.1
  12.1 0.0 copy-done.3
  12.1 0.1 broadcast_select_fusion.1.null_ref
  12.2 0.2 fusion
  12.5 0.1 add_select_fusion.bias_ref
  12.6 0.5 broadcast_select_fusion.null_flip
  13.1 0.8 %collective-permute-done.near_ref = bf16[256,1536]{1,0:T(8,128)(2,1)} collective-permute-done((bf16[256,1536]{1,0:T(8,128)(2,1)S(1)}, bf16[256,1536]{1,0:T(8,128)(2,1)}, u32[]{:S(2)}, u32[]{:S(2)}) %collective-permute-start) | collective-permute-done | bytes 786464 | tf_op jit(solution)/shard_map/ppermute | solution.py:31
  13.8 0.0 copy-done
  13.8 0.0 copy-done.1
  13.8 3.3 %prepare.1 = (bf16[256,1536]{1,0:T(8,128)(2,1)S(1)}, bf16[256,1536]{1,0:T(8,128)(2,1)S(1)}, bf16[1536,256]{1,0:T(8,128)(2,1)S(1)}, bf16[1536,256]{1,0:T(8,128)(2...) custom-call(bf16[256,1536]{1,0:T(8,128)(2,1)S(1)} %copy-done, ...), custom_call_target="tpu_custom_call" | custom-call | flops 603979776 | bytes 9000000 | tf_op jit(solution)/shard_map/prepare/pallas_call | solution.py:106
  17.1 0.0 collective-permute-done.1.far_ref
  17.1 4.8 %heads.1 = (bf16[256,1536]{1,0:T(8,128)(2,1)}, bf16[256,1536]{1,0:T(8,128)(2,1)}, bf16[2,128,1536]{2,1,0:T(8,128)(2,1)}, bf16[2,128,1536]{2,1,0:T(8,128)(2,1)S(1...) custom-call(bf16[256,1536]{1,0:T(8,128)(2,1)S(1)} %get-tuple-element.27.q_ref, ...), custom_call_target="tpu_custom_call" | custom-call | flops 679477248 | bytes 9000000 | tf_op jit(solution)/shard_map/heads/pallas_call | solution.py:210
  21.9 2.7 %collective-permute-start.2 = (bf16[2,128,1536]{2,1,0:T(8,128)(2,1)}, bf16[2,128,1536]{2,1,0:T(8,128)(2,1)S(1)}, u32[]{:S(2)}, u32[]{:S(2)}) collective-permute-start(bf16[2,128,1536]{2,1,0:T(8,128)(2,1)} %get-tuple-element.40), channel_id=1, source_target_pairs={{1,2},{3,4},{5,6},{7,8},{9,10},{11,12},{13,14},{15,16},{17,18},{19... | collective-permute-start | bytes 2359304 | tf_op jit(solution)/shard_map/ppermute | solution.py:37
  24.6 1.9 %collective-permute-start.3 = (bf16[2,128,1536]{2,1,0:T(8,128)(2,1)S(1)}, bf16[2,128,1536]{2,1,0:T(8,128)(2,1)S(1)}, u32[]{:S(2)}, u32[]{:S(2)}) collective-permute-start(bf16[2,128,1536]{2,1,0:T(8,128)(2,1)S(1)} %get-tuple-element.41), channel_id=1, source_target_pairs={{0,1},{1,0},{2,3},{3,2},{4,5},{5,4},{6,7},{7,6},{8,9},{9,8},{10,11... | collective-permute-start | bytes 2359304 | tf_op jit(solution)/shard_map/ppermute | solution.py:31
  26.5 20.8 %all_to_all.10 = bf16[32,24,128]{2,1,0:T(8,128)(2,1)S(1)} all-to-all(bf16[32,24,128]{2,1,0:T(8,128)(2,1)S(1)} %get-tuple-element.38), channel_id=1, replica_groups=mesh['yh'=2,'z'=8,'yl'=4,'x'=4,'core'=2] {'yh','yl','x'}, dimensions={0} | all-to-all | bytes 393216 | tf_op jit(solution)/shard_map/all_to_all | solution.py:308
  47.4 0.6 broadcast_in_dim.90
  48.1 12.5 %all-to-all-start.1 = ((bf16[16,24,128]{2,1,0:T(8,128)(2,1)}), bf16[16,24,128]{2,1,0:T(8,128)(2,1)S(1)}, u32[]{:S(2)}, u32[]{:S(2)}) async-start(bf16[16,24,128]{2,1,0:T(8,128)(2,1)} %broadcast_in_dim.90), calls=%async_computation.1 | async-start | bytes 196608 | tf_op jit(solution)/shard_map/all_to_all | solution.py:311
  60.5 0.0 collective-permute-done.2.b_ref
  60.5 0.4 add_far.1.a_ref
  61.0 0.0 collective-permute-done.3.b_ref
  61.0 1.6 %add_near.1 = (bf16[128,1536]{1,0:T(8,128)(2,1)}, bf16[128,1536]{1,0:T(8,128)(2,1)}) custom-call(bf16[2,128,1536]{2,1,0:T(8,128)(2,1)S(1)} %add_far.1.a_ref, bf16[2,128,1536]{2,1,0:T(8,128)(2,1)S(1)} %collective-permute-done.3.b_ref), custom_call_target="tpu_custom_call" | custom-call | flops 393216 | bytes 2400000 | tf_op jit(solution)/shard_map/add_near/pallas_call | solution.py:248
  62.5 6.5 %all-to-all-done.1 = bf16[16,24,128]{2,1,0:T(8,128)(2,1)S(1)} async-done(((bf16[16,24,128]{2,1,0:T(8,128)(2,1)}), bf16[16,24,128]{2,1,0:T(8,128)(2,1)S(1)}, u32[]{:S(2)}, u32[]{:S(2)}) %all-to-all-start.1) | async-done | bytes 98336 | tf_op jit(solution)/shard_map/all_to_all | solution.py:311
  69.0 0.6 reshape.170
  (14 shorter events, 0.2 us)
Async XLA Ops:
  0.6 5.9 %copy-start.4 = (s32[1,4]{1,0:T(1,128)S(1)}, s32[1,4]{1,0:T(1,128)}, u32[]{:S(2)}) copy-start(s32[1,4]{1,0:T(1,128)} %param.12) | copy-start | bytes 52
  0.6 11.2 %copy-start.2 = (s32[4096]{0:T(1024)S(1)}, s32[4096]{0:T(1024)}, u32[]{:S(2)}) copy-start(s32[4096]{0:T(1024)} %param.11) | copy-start | bytes 49156
  0.7 11.4 %copy-start.3 = (bf16[2,1536]{1,0:T(2,128)(2,1)S(1)}, bf16[2,1536]{1,0:T(2,128)(2,1)}, u32[]{:S(2)}) copy-start(bf16[2,1536]{1,0:T(2,128)(2,1)} %param.10) | copy-start | bytes 18436
  0.7 13.2 %copy-start = (bf16[256,1536]{1,0:T(8,128)(2,1)S(1)}, bf16[256,1536]{1,0:T(8,128)(2,1)}, u32[]{:S(2)}) copy-start(bf16[256,1536]{1,0:T(8,128)(2,1)} %q_in.1) | copy-start | bytes 2359300
  0.7 13.2 %copy-start.1 = (bf16[256,1536]{1,0:T(8,128)(2,1)S(1)}, bf16[256,1536]{1,0:T(8,128)(2,1)}, u32[]{:S(2)}) copy-start(bf16[256,1536]{1,0:T(8,128)(2,1)} %g_in.1) | copy-start | bytes 2359300
  2.0 15.1 %collective-permute-start.1 = (bf16[256,1536]{1,0:T(8,128)(2,1)S(1)}, bf16[256,1536]{1,0:T(8,128)(2,1)S(1)}, u32[]{:S(2)}, u32[]{:S(2)}) collective-permute-start(bf16[256,1536]{1,0:T(8,128)(2,1)S(1)} %bitcast.8), channel_id=1, source_target_pairs={{1,2},{3,4},{5,6},{7,8},{9,10},{11,12},{13,14},{15,16},{17,18},{19... | collective-permute-start | bytes 2359304 | tf_op jit(solution)/shard_map/ppermute | solution.py:37
  6.8 7.0 %collective-permute-start = (bf16[256,1536]{1,0:T(8,128)(2,1)S(1)}, bf16[256,1536]{1,0:T(8,128)(2,1)}, u32[]{:S(2)}, u32[]{:S(2)}) collective-permute-start(bf16[256,1536]{1,0:T(8,128)(2,1)S(1)} %bitcast.9), channel_id=1, source_target_pairs={{0,1},{1,0},{2,3},{3,2},{4,5},{5,4},{6,7},{7,6},{8,9},{9,8},{10,11... | collective-permute-start | bytes 2359304 | tf_op jit(solution)/shard_map/ppermute | solution.py:31
  21.9 38.6 %collective-permute-start.2 = (bf16[2,128,1536]{2,1,0:T(8,128)(2,1)}, bf16[2,128,1536]{2,1,0:T(8,128)(2,1)S(1)}, u32[]{:S(2)}, u32[]{:S(2)}) collective-permute-start(bf16[2,128,1536]{2,1,0:T(8,128)(2,1)} %get-tuple-element.40), channel_id=1, source_target_pairs={{1,2},{3,4},{5,6},{7,8},{9,10},{11,12},{13,14},{15,16},{17,18},{19... | collective-permute-start | bytes 2359304 | tf_op jit(solution)/shard_map/ppermute | solution.py:37
  24.6 36.4 %collective-permute-start.3 = (bf16[2,128,1536]{2,1,0:T(8,128)(2,1)S(1)}, bf16[2,128,1536]{2,1,0:T(8,128)(2,1)S(1)}, u32[]{:S(2)}, u32[]{:S(2)}) collective-permute-start(bf16[2,128,1536]{2,1,0:T(8,128)(2,1)S(1)} %get-tuple-element.41), channel_id=1, source_target_pairs={{0,1},{1,0},{2,3},{3,2},{4,5},{5,4},{6,7},{7,6},{8,9},{9,8},{10,11... | collective-permute-start | bytes 2359304 | tf_op jit(solution)/shard_map/ppermute | solution.py:31
  48.1 21.0 %all-to-all-start.1 = ((bf16[16,24,128]{2,1,0:T(8,128)(2,1)}), bf16[16,24,128]{2,1,0:T(8,128)(2,1)S(1)}, u32[]{:S(2)}, u32[]{:S(2)}) async-start(bf16[16,24,128]{2,1,0:T(8,128)(2,1)} %broadcast_in_dim.90), calls=%async_computation.1 | async-start | bytes 196608 | tf_op jit(solution)/shard_map/all_to_all | solution.py:311

commit v10 on v8

--- a/solution.py
+++ b/solution.py
@@ -185,9 +185,10 @@
 
     @pl.when(step == STEPS - 1)
     def _():
-        null_grad_ref[...] = jnp.broadcast_to(
-            null_sum[...].astype(jnp.bfloat16)[None], null_grad_ref.shape
-        )
+        total = null_sum[...]
+        peers = null_grad_ref.shape[0] // total.shape[0]
+        copies = jnp.broadcast_to(total[None], (peers, *total.shape))
+        null_grad_ref[...] = copies.reshape(null_grad_ref.shape).astype(jnp.bfloat16)
 
 
 def block(*lead):
@@ -203,7 +204,7 @@
     audio_rows = video_rows // 2
     wide = jax.ShapeDtypeStruct((video_rows, width), jnp.bfloat16)
     terms = [jax.ShapeDtypeStruct((2, audio_rows, width), jnp.bfloat16)] * 3
-    null_shape = (peers, 2 * HEADS, HEAD)
+    null_shape = (peers * 2 * HEADS, HEAD)
     deep = pl.BlockSpec((WIDE, video_rows), lambda i: (i, 0))
     pairs = pl.BlockSpec((PER_STEP, 2 * audio_rows, video_rows), lambda i: (i, 0, 0))
     return pl.pallas_call(
@@ -303,7 +304,7 @@
         q_held, g_held, far, near_parts, null_rows, null_flip, bias, valid, lax.axis_size(wide_axes)
     )
     far_back = swap_link(far_grad)
-    first = lax.all_to_all(null_copies, wide_axes, 0, 0)
+    first = lax.all_to_all(null_copies.reshape(-1, 2 * HEADS, HEAD), wide_axes, 0, 0)
     partial = sum_peers(first).astype(jnp.bfloat16)
     copies = jnp.broadcast_to(partial[None], (lax.axis_size(deep_axes), *partial.shape))
     copies, near_grad = lax.optimization_barrier((copies, near_grad))

time: 67.1 us -> 67.1 us (level)
  no operation moved by 1% of the time
where the time goes in v10:
time: 67.1 us; the launch traced here: 66.7 us
  starting transfers between devices  35.2 us (52%)
  waiting for transfers between devices  16.4 us (24%)
  Pallas kernels  10.1 us (15%)
  other arithmetic  2.76 us (4%)
  local copies, waits for them, and re-layouts  1.32 us (2%)
  between operations  0.89 us (1%)
    all_to_all x1, starting transfers between devices, body(): second = lax.all_to_all(copies, deep_axes, 0, 0)  10.8 us
    all_to_all x1, starting transfers between devices, body(): lax.all_to_all(null_copies.reshape(-1, 2 * HEADS, HEAD), wide_axes, 0, 0)  10.5 us
    all_to_all x1, waiting for transfers between devices, body(): lax.all_to_all(null_copies.reshape(-1, 2 * HEADS, HEAD), wide_axes, 0, 0)  9.2 us
    ppermute x2, starting transfers between devices, swap_link(): return lax.ppermute(block, SEQ, pairs + [(b, a) for a, b in pairs])  6.92 us
    ppermute x2, starting transfers between devices, swap_chip(): return lax.ppermute(block, SEQ, [(i, i ^ 1) for i in range(count)])  6.89 us
    all_to_all x1, waiting for transfers between devices, body(): second = lax.all_to_all(copies, deep_axes, 0, 0)  6.48 us
    pallas_call x1, Pallas kernels, heads_call(): pl.pallas_call(heads_kernel, grid=(STEPS,), in_specs=[block(video_rows)]...  4.86 us
    pallas_call x1, Pallas kernels, prepare_call(): pl.pallas_call(prepare_kernel, grid=(STEPS,), in_specs=[block(video_rows)...  3.26 us
  transfers between devices with their start and end apart: 6, of which 3 were waited for; matrix products, arithmetic and copies ran while one was open for 3% of the time, Pallas kernels for 8%

profile of v10, /device:TPU:1, one launch (start us, length us, event | category | flops | bytes accessed | tf_op | source)
XLA Modules:
  0.0 66.7 jit_solution(5799982918633289592)
XLA Ops:
  0.6 0.0 copy-start.4
  0.6 0.0 copy-start.2
  0.7 0.0 copy-start.3
  0.7 0.0 copy-start
  0.7 0.0 copy-start.1
  0.7 1.3 %pad_maximum_fusion = bf16[2,128,1536]{2,1,0:T(8,128)(2,1)S(1)} fusion(bf16[1,128,1536]{2,1,0:T(8,128)(2,1)} %bitcast.13, bf16[1,128,1536]{2,1,0:T(8,128)(2,1)} %bitcast.14), kind=kLoop, calls=%fused_computation | loop fusion | flops 393216 | bytes 1572864 | tf_op jit(solution)/shard_map/stack | solution.py:271
  2.0 4.5 %collective-permute-start.1 = (bf16[256,1536]{1,0:T(8,128)(2,1)S(1)}, bf16[256,1536]{1,0:T(8,128)(2,1)S(1)}, u32[]{:S(2)}, u32[]{:S(2)}) collective-permute-start(bf16[256,1536]{1,0:T(8,128)(2,1)S(1)} %bitcast.9), channel_id=1, source_target_pairs={{1,2},{3,4},{5,6},{7,8},{9,10},{11,12},{13,14},{15,16},{17,18},{19... | collective-permute-start | bytes 2359304 | tf_op jit(solution)/shard_map/ppermute | solution.py:37
  6.5 0.0 copy-done.4
  6.5 0.2 reduce-window.4
  6.7 0.1 convert_reduce_fusion.2
  6.8 5.0 %collective-permute-start = (bf16[256,1536]{1,0:T(8,128)(2,1)S(1)}, bf16[256,1536]{1,0:T(8,128)(2,1)}, u32[]{:S(2)}, u32[]{:S(2)}) collective-permute-start(bf16[256,1536]{1,0:T(8,128)(2,1)S(1)} %bitcast.10), channel_id=1, source_target_pairs={{0,1},{1,0},{2,3},{3,2},{4,5},{5,4},{6,7},{7,6},{8,9},{9,8},{10,11... | collective-permute-start | bytes 2359304 | tf_op jit(solution)/shard_map/ppermute | solution.py:31
  11.9 0.0 copy-done.2
  11.9 0.1 pad_dynamic-slice_fusion.2
  12.0 0.1 convert_reduce_fusion.1
  12.1 0.0 copy-done.3
  12.1 0.1 broadcast_select_fusion.1.null_ref
  12.2 0.2 fusion
  12.5 0.1 add_select_fusion.bias_ref
  12.6 0.5 broadcast_select_fusion.null_flip
  13.1 0.8 %collective-permute-done.near_ref = bf16[256,1536]{1,0:T(8,128)(2,1)} collective-permute-done((bf16[256,1536]{1,0:T(8,128)(2,1)S(1)}, bf16[256,1536]{1,0:T(8,128)(2,1)}, u32[]{:S(2)}, u32[]{:S(2)}) %collective-permute-start) | collective-permute-done | bytes 786464 | tf_op jit(solution)/shard_map/ppermute | solution.py:31
  13.8 0.0 copy-done
  13.8 0.0 copy-done.1
  13.8 3.3 %prepare.1 = (bf16[256,1536]{1,0:T(8,128)(2,1)S(1)}, bf16[256,1536]{1,0:T(8,128)(2,1)S(1)}, bf16[1536,256]{1,0:T(8,128)(2,1)S(1)}, bf16[1536,256]{1,0:T(8,128)(2...) custom-call(bf16[256,1536]{1,0:T(8,128)(2,1)S(1)} %copy-done, ...), custom_call_target="tpu_custom_call" | custom-call | flops 603979776 | bytes 9000000 | tf_op jit(solution)/shard_map/prepare/pallas_call | solution.py:106
  17.1 0.0 collective-permute-done.1.far_ref
  17.1 4.9 %heads.1 = (bf16[256,1536]{1,0:T(8,128)(2,1)}, bf16[256,1536]{1,0:T(8,128)(2,1)}, bf16[2,128,1536]{2,1,0:T(8,128)(2,1)}, bf16[2,128,1536]{2,1,0:T(8,128)(2,1)S(1...) custom-call(bf16[256,1536]{1,0:T(8,128)(2,1)S(1)} %get-tuple-element.29.q_ref, ...), custom_call_target="tpu_custom_call" | custom-call | flops 679477248 | bytes 9000000 | tf_op jit(solution)/shard_map/heads/pallas_call | solution.py:210
  22.0 10.5 %all-to-all-start = ((bf16[32,24,128]{2,1,0:T(8,128)(2,1)}), bf16[32,24,128]{2,1,0:T(8,128)(2,1)S(1)}, u32[]{:S(2)}, u32[]{:S(2)}) async-start(bf16[32,24,128]{2,1,0:T(8,128)(2,1)} %bitcast.7), calls=%async_computation | async-start | bytes 393216 | tf_op jit(solution)/shard_map/all_to_all | solution.py:307
  32.5 2.4 %collective-permute-start.2 = (bf16[2,128,1536]{2,1,0:T(8,128)(2,1)}, bf16[2,128,1536]{2,1,0:T(8,128)(2,1)S(1)}, u32[]{:S(2)}, u32[]{:S(2)}) collective-permute-start(bf16[2,128,1536]{2,1,0:T(8,128)(2,1)} %get-tuple-element.44), channel_id=1, source_target_pairs={{1,2},{3,4},{5,6},{7,8},{9,10},{11,12},{13,14},{15,16},{17,18},{19... | collective-permute-start | bytes 2359304 | tf_op jit(solution)/shard_map/ppermute | solution.py:37
  34.9 9.2 %all-to-all-done = bf16[32,24,128]{2,1,0:T(8,128)(2,1)S(1)} async-done(((bf16[32,24,128]{2,1,0:T(8,128)(2,1)}), bf16[32,24,128]{2,1,0:T(8,128)(2,1)S(1)}, u32[]{:S(2)}, u32[]{:S(2)}) %all-to-all-start) | async-done | bytes 196640 | tf_op jit(solution)/shard_map/all_to_all | solution.py:307
  44.2 0.6 broadcast_in_dim.90
  44.8 1.9 %collective-permute-start.3 = (bf16[2,128,1536]{2,1,0:T(8,128)(2,1)S(1)}, bf16[2,128,1536]{2,1,0:T(8,128)(2,1)S(1)}, u32[]{:S(2)}, u32[]{:S(2)}) collective-permute-start(bf16[2,128,1536]{2,1,0:T(8,128)(2,1)S(1)} %get-tuple-element.45), channel_id=1, source_target_pairs={{0,1},{1,0},{2,3},{3,2},{4,5},{5,4},{6,7},{7,6},{8,9},{9,8},{10,11... | collective-permute-start | bytes 2359304 | tf_op jit(solution)/shard_map/ppermute | solution.py:31
  46.7 10.8 %all-to-all-start.1 = ((bf16[16,24,128]{2,1,0:T(8,128)(2,1)}), bf16[16,24,128]{2,1,0:T(8,128)(2,1)S(1)}, u32[]{:S(2)}, u32[]{:S(2)}) async-start(bf16[16,24,128]{2,1,0:T(8,128)(2,1)} %broadcast_in_dim.90), calls=%async_computation.1 | async-start | bytes 196608 | tf_op jit(solution)/shard_map/all_to_all | solution.py:312
  57.6 0.0 collective-permute-done.2.b_ref
  57.6 0.4 add_far.1.a_ref
  58.0 0.0 collective-permute-done.3.b_ref
  58.0 1.6 %add_near.1 = (bf16[128,1536]{1,0:T(8,128)(2,1)}, bf16[128,1536]{1,0:T(8,128)(2,1)}) custom-call(bf16[2,128,1536]{2,1,0:T(8,128)(2,1)S(1)} %add_far.1.a_ref, bf16[2,128,1536]{2,1,0:T(8,128)(2,1)S(1)} %collective-permute-done.3.b_ref), custom_call_target="tpu_custom_call" | custom-call | flops 393216 | bytes 2400000 | tf_op jit(solution)/shard_map/add_near/pallas_call | solution.py:248
  59.6 6.5 %all-to-all-done.1 = bf16[16,24,128]{2,1,0:T(8,128)(2,1)S(1)} async-done(((bf16[16,24,128]{2,1,0:T(8,128)(2,1)}), bf16[16,24,128]{2,1,0:T(8,128)(2,1)S(1)}, u32[]{:S(2)}, u32[]{:S(2)}) %all-to-all-start.1) | async-done | bytes 98336 | tf_op jit(solution)/shard_map/all_to_all | solution.py:312
  66.1 0.6 reshape.174
  (14 shorter events, 0.2 us)
Async XLA Ops:
  0.6 5.9 %copy-start.4 = (s32[1,4]{1,0:T(1,128)S(1)}, s32[1,4]{1,0:T(1,128)}, u32[]{:S(2)}) copy-start(s32[1,4]{1,0:T(1,128)} %param.12) | copy-start | bytes 52
  0.6 11.2 %copy-start.2 = (s32[4096]{0:T(1024)S(1)}, s32[4096]{0:T(1024)}, u32[]{:S(2)}) copy-start(s32[4096]{0:T(1024)} %param.11) | copy-start | bytes 49156
  0.7 11.4 %copy-start.3 = (bf16[2,1536]{1,0:T(2,128)(2,1)S(1)}, bf16[2,1536]{1,0:T(2,128)(2,1)}, u32[]{:S(2)}) copy-start(bf16[2,1536]{1,0:T(2,128)(2,1)} %param.10) | copy-start | bytes 18436
  0.7 13.2 %copy-start = (bf16[256,1536]{1,0:T(8,128)(2,1)S(1)}, bf16[256,1536]{1,0:T(8,128)(2,1)}, u32[]{:S(2)}) copy-start(bf16[256,1536]{1,0:T(8,128)(2,1)} %q_in.1) | copy-start | bytes 2359300
  0.7 13.2 %copy-start.1 = (bf16[256,1536]{1,0:T(8,128)(2,1)S(1)}, bf16[256,1536]{1,0:T(8,128)(2,1)}, u32[]{:S(2)}) copy-start(bf16[256,1536]{1,0:T(8,128)(2,1)} %g_in.1) | copy-start | bytes 2359300
  2.0 15.1 %collective-permute-start.1 = (bf16[256,1536]{1,0:T(8,128)(2,1)S(1)}, bf16[256,1536]{1,0:T(8,128)(2,1)S(1)}, u32[]{:S(2)}, u32[]{:S(2)}) collective-permute-start(bf16[256,1536]{1,0:T(8,128)(2,1)S(1)} %bitcast.9), channel_id=1, source_target_pairs={{1,2},{3,4},{5,6},{7,8},{9,10},{11,12},{13,14},{15,16},{17,18},{19... | collective-permute-start | bytes 2359304 | tf_op jit(solution)/shard_map/ppermute | solution.py:37
  6.8 7.0 %collective-permute-start = (bf16[256,1536]{1,0:T(8,128)(2,1)S(1)}, bf16[256,1536]{1,0:T(8,128)(2,1)}, u32[]{:S(2)}, u32[]{:S(2)}) collective-permute-start(bf16[256,1536]{1,0:T(8,128)(2,1)S(1)} %bitcast.10), channel_id=1, source_target_pairs={{0,1},{1,0},{2,3},{3,2},{4,5},{5,4},{6,7},{7,6},{8,9},{9,8},{10,11... | collective-permute-start | bytes 2359304 | tf_op jit(solution)/shard_map/ppermute | solution.py:31
  22.0 22.1 %all-to-all-start = ((bf16[32,24,128]{2,1,0:T(8,128)(2,1)}), bf16[32,24,128]{2,1,0:T(8,128)(2,1)S(1)}, u32[]{:S(2)}, u32[]{:S(2)}) async-start(bf16[32,24,128]{2,1,0:T(8,128)(2,1)} %bitcast.7), calls=%async_computation | async-start | bytes 393216 | tf_op jit(solution)/shard_map/all_to_all | solution.py:307
  32.5 25.1 %collective-permute-start.2 = (bf16[2,128,1536]{2,1,0:T(8,128)(2,1)}, bf16[2,128,1536]{2,1,0:T(8,128)(2,1)S(1)}, u32[]{:S(2)}, u32[]{:S(2)}) collective-permute-start(bf16[2,128,1536]{2,1,0:T(8,128)(2,1)} %get-tuple-element.44), channel_id=1, source_target_pairs={{1,2},{3,4},{5,6},{7,8},{9,10},{11,12},{13,14},{15,16},{17,18},{19... | collective-permute-start | bytes 2359304 | tf_op jit(solution)/shard_map/ppermute | solution.py:37
  44.8 13.2 %collective-permute-start.3 = (bf16[2,128,1536]{2,1,0:T(8,128)(2,1)S(1)}, bf16[2,128,1536]{2,1,0:T(8,128)(2,1)S(1)}, u32[]{:S(2)}, u32[]{:S(2)}) collective-permute-start(bf16[2,128,1536]{2,1,0:T(8,128)(2,1)S(1)} %get-tuple-element.45), channel_id=1, source_target_pairs={{0,1},{1,0},{2,3},{3,2},{4,5},{5,4},{6,7},{7,6},{8,9},{9,8},{10,11... | collective-permute-start | bytes 2359304 | tf_op jit(solution)/shard_map/ppermute | solution.py:31
  46.7 19.3 %all-to-all-start.1 = ((bf16[16,24,128]{2,1,0:T(8,128)(2,1)}), bf16[16,24,128]{2,1,0:T(8,128)(2,1)S(1)}, u32[]{:S(2)}, u32[]{:S(2)}) async-start(bf16[16,24,128]{2,1,0:T(8,128)(2,1)} %broadcast_in_dim.90), calls=%async_computation.1 | async-start | bytes 196608 | tf_op jit(solution)/shard_map/all_to_all | solution.py:312

commit v11 on v10

--- a/solution.py
+++ b/solution.py
@@ -298,7 +298,7 @@
     stacked, valid = lax.optimization_barrier((stacked, valid))
     near = swap_chip(stacked)
 
-    wide_axes, deep_axes = ("yh", "yl", "x"), ("z", "core")
+    wide_axes, deep_axes = ("z", "x"), ("yh", "yl", "core")
     q_held, g_held, *near_parts = prepare_call(video_query, out_grad, stacked, near, near_bias)
     attended, query_grad, far_grad, own_grad, near_grad, null_copies = heads_call(
         q_held, g_held, far, near_parts, null_rows, null_flip, bias, valid, lax.axis_size(wide_axes)

time: 67.1 us -> 67.1 us (level)
    all_to_all x1, starting transfers between devices: 10.8 us -> 7.63 us  [body(): second = lax.all_to_all(copies, deep_axes, 0, 0)]
    all_to_all x1, starting transfers between devices: 10.5 us -> 13.7 us  [body(): lax.all_to_all(null_copies.reshape(-1, 2 * HEADS, HEAD), wide_axes, 0, 0)]
where the time goes in v11:
time: 67.1 us; the launch traced here: 66.7 us
  starting transfers between devices  35.2 us (52%)
  waiting for transfers between devices  16.4 us (24%)
  Pallas kernels  10.1 us (15%)
  other arithmetic  2.76 us (4%)
  local copies, waits for them, and re-layouts  1.32 us (2%)
  between operations  0.89 us (1%)
    all_to_all x1, starting transfers between devices, body(): lax.all_to_all(null_copies.reshape(-1, 2 * HEADS, HEAD), wide_axes, 0, 0)  13.7 us
    all_to_all x1, waiting for transfers between devices, body(): lax.all_to_all(null_copies.reshape(-1, 2 * HEADS, HEAD), wide_axes, 0, 0)  9.19 us
    all_to_all x1, starting transfers between devices, body(): second = lax.all_to_all(copies, deep_axes, 0, 0)  7.63 us
    ppermute x2, starting transfers between devices, swap_link(): return lax.ppermute(block, SEQ, pairs + [(b, a) for a, b in pairs])  6.92 us
    ppermute x2, starting transfers between devices, swap_chip(): return lax.ppermute(block, SEQ, [(i, i ^ 1) for i in range(count)])  6.89 us
    all_to_all x1, waiting for transfers between devices, body(): second = lax.all_to_all(copies, deep_axes, 0, 0)  6.48 us
    pallas_call x1, Pallas kernels, heads_call(): pl.pallas_call(heads_kernel, grid=(STEPS,), in_specs=[block(video_rows)]...  4.86 us
    pallas_call x1, Pallas kernels, prepare_call(): pl.pallas_call(prepare_kernel, grid=(STEPS,), in_specs=[block(video_rows)...  3.26 us
  transfers between devices with their start and end apart: 6, of which 3 were waited for; matrix products, arithmetic and copies ran while one was open for 3% of the time, Pallas kernels for 8%

profile of v11, /device:TPU:1, one launch (start us, length us, event | category | flops | bytes accessed | tf_op | source)
XLA Modules:
  0.0 66.7 jit_solution(3290928728638088894)
XLA Ops:
  0.6 0.0 copy-start.4
  0.6 0.0 copy-start.2
  0.7 0.0 copy-start.3
  0.7 0.0 copy-start
  0.7 0.0 copy-start.1
  0.7 1.3 %pad_maximum_fusion = bf16[2,128,1536]{2,1,0:T(8,128)(2,1)S(1)} fusion(bf16[1,128,1536]{2,1,0:T(8,128)(2,1)} %bitcast.13, bf16[1,128,1536]{2,1,0:T(8,128)(2,1)} %bitcast.14), kind=kLoop, calls=%fused_computation | loop fusion | flops 393216 | bytes 1572864 | tf_op jit(solution)/shard_map/stack | solution.py:271
  2.0 4.5 %collective-permute-start.1 = (bf16[256,1536]{1,0:T(8,128)(2,1)S(1)}, bf16[256,1536]{1,0:T(8,128)(2,1)S(1)}, u32[]{:S(2)}, u32[]{:S(2)}) collective-permute-start(bf16[256,1536]{1,0:T(8,128)(2,1)S(1)} %bitcast.9), channel_id=1, source_target_pairs={{1,2},{3,4},{5,6},{7,8},{9,10},{11,12},{13,14},{15,16},{17,18},{19... | collective-permute-start | bytes 2359304 | tf_op jit(solution)/shard_map/ppermute | solution.py:37
  6.5 0.0 copy-done.4
  6.5 0.2 reduce-window.4
  6.7 0.1 convert_reduce_fusion.2
  6.8 5.0 %collective-permute-start = (bf16[256,1536]{1,0:T(8,128)(2,1)S(1)}, bf16[256,1536]{1,0:T(8,128)(2,1)}, u32[]{:S(2)}, u32[]{:S(2)}) collective-permute-start(bf16[256,1536]{1,0:T(8,128)(2,1)S(1)} %bitcast.10), channel_id=1, source_target_pairs={{0,1},{1,0},{2,3},{3,2},{4,5},{5,4},{6,7},{7,6},{8,9},{9,8},{10,11... | collective-permute-start | bytes 2359304 | tf_op jit(solution)/shard_map/ppermute | solution.py:31
  11.9 0.0 copy-done.2
  11.9 0.1 pad_dynamic-slice_fusion.2
  12.0 0.1 convert_reduce_fusion.1
  12.1 0.0 copy-done.3
  12.1 0.1 broadcast_select_fusion.1.null_ref
  12.2 0.2 fusion
  12.5 0.1 add_select_fusion.bias_ref
  12.6 0.5 broadcast_select_fusion.null_flip
  13.1 0.8 %collective-permute-done.near_ref = bf16[256,1536]{1,0:T(8,128)(2,1)} collective-permute-done((bf16[256,1536]{1,0:T(8,128)(2,1)S(1)}, bf16[256,1536]{1,0:T(8,128)(2,1)}, u32[]{:S(2)}, u32[]{:S(2)}) %collective-permute-start) | collective-permute-done | bytes 786464 | tf_op jit(solution)/shard_map/ppermute | solution.py:31
  13.8 0.0 copy-done
  13.8 0.0 copy-done.1
  13.8 3.3 %prepare.1 = (bf16[256,1536]{1,0:T(8,128)(2,1)S(1)}, bf16[256,1536]{1,0:T(8,128)(2,1)S(1)}, bf16[1536,256]{1,0:T(8,128)(2,1)S(1)}, bf16[1536,256]{1,0:T(8,128)(2...) custom-call(bf16[256,1536]{1,0:T(8,128)(2,1)S(1)} %copy-done, ...), custom_call_target="tpu_custom_call" | custom-call | flops 603979776 | bytes 9000000 | tf_op jit(solution)/shard_map/prepare/pallas_call | solution.py:106
  17.1 0.0 collective-permute-done.1.far_ref
  17.1 4.9 %heads.1 = (bf16[256,1536]{1,0:T(8,128)(2,1)}, bf16[256,1536]{1,0:T(8,128)(2,1)}, bf16[2,128,1536]{2,1,0:T(8,128)(2,1)}, bf16[2,128,1536]{2,1,0:T(8,128)(2,1)S(1...) custom-call(bf16[256,1536]{1,0:T(8,128)(2,1)S(1)} %get-tuple-element.29.q_ref, ...), custom_call_target="tpu_custom_call" | custom-call | flops 679477248 | bytes 9000000 | tf_op jit(solution)/shard_map/heads/pallas_call | solution.py:210
  22.0 13.7 %all-to-all-start = ((bf16[32,24,128]{2,1,0:T(8,128)(2,1)}), bf16[32,24,128]{2,1,0:T(8,128)(2,1)S(1)}, u32[]{:S(2)}, u32[]{:S(2)}) async-start(bf16[32,24,128]{2,1,0:T(8,128)(2,1)} %bitcast.7), calls=%async_computation | async-start | bytes 393216 | tf_op jit(solution)/shard_map/all_to_all | solution.py:307
  35.7 2.4 %collective-permute-start.2 = (bf16[2,128,1536]{2,1,0:T(8,128)(2,1)}, bf16[2,128,1536]{2,1,0:T(8,128)(2,1)S(1)}, u32[]{:S(2)}, u32[]{:S(2)}) collective-permute-start(bf16[2,128,1536]{2,1,0:T(8,128)(2,1)} %get-tuple-element.44), channel_id=1, source_target_pairs={{1,2},{3,4},{5,6},{7,8},{9,10},{11,12},{13,14},{15,16},{17,18},{19... | collective-permute-start | bytes 2359304 | tf_op jit(solution)/shard_map/ppermute | solution.py:37
  38.1 9.2 %all-to-all-done = bf16[32,24,128]{2,1,0:T(8,128)(2,1)S(1)} async-done(((bf16[32,24,128]{2,1,0:T(8,128)(2,1)}), bf16[32,24,128]{2,1,0:T(8,128)(2,1)S(1)}, u32[]{:S(2)}, u32[]{:S(2)}) %all-to-all-start) | async-done | bytes 196640 | tf_op jit(solution)/shard_map/all_to_all | solution.py:307
  47.4 0.6 broadcast_in_dim.90
  48.0 1.9 %collective-permute-start.3 = (bf16[2,128,1536]{2,1,0:T(8,128)(2,1)S(1)}, bf16[2,128,1536]{2,1,0:T(8,128)(2,1)S(1)}, u32[]{:S(2)}, u32[]{:S(2)}) collective-permute-start(bf16[2,128,1536]{2,1,0:T(8,128)(2,1)S(1)} %get-tuple-element.45), channel_id=1, source_target_pairs={{0,1},{1,0},{2,3},{3,2},{4,5},{5,4},{6,7},{7,6},{8,9},{9,8},{10,11... | collective-permute-start | bytes 2359304 | tf_op jit(solution)/shard_map/ppermute | solution.py:31
  49.9 7.6 %all-to-all-start.1 = ((bf16[16,24,128]{2,1,0:T(8,128)(2,1)}), bf16[16,24,128]{2,1,0:T(8,128)(2,1)S(1)}, u32[]{:S(2)}, u32[]{:S(2)}) async-start(bf16[16,24,128]{2,1,0:T(8,128)(2,1)} %broadcast_in_dim.90), calls=%async_computation.1 | async-start | bytes 196608 | tf_op jit(solution)/shard_map/all_to_all | solution.py:312
  57.6 0.0 collective-permute-done.2.b_ref
  57.6 0.4 add_far.1.a_ref
  58.0 0.0 collective-permute-done.3.b_ref
  58.0 1.6 %add_near.1 = (bf16[128,1536]{1,0:T(8,128)(2,1)}, bf16[128,1536]{1,0:T(8,128)(2,1)}) custom-call(bf16[2,128,1536]{2,1,0:T(8,128)(2,1)S(1)} %add_far.1.a_ref, bf16[2,128,1536]{2,1,0:T(8,128)(2,1)S(1)} %collective-permute-done.3.b_ref), custom_call_target="tpu_custom_call" | custom-call | flops 393216 | bytes 2400000 | tf_op jit(solution)/shard_map/add_near/pallas_call | solution.py:248
  59.6 6.5 %all-to-all-done.1 = bf16[16,24,128]{2,1,0:T(8,128)(2,1)S(1)} async-done(((bf16[16,24,128]{2,1,0:T(8,128)(2,1)}), bf16[16,24,128]{2,1,0:T(8,128)(2,1)S(1)}, u32[]{:S(2)}, u32[]{:S(2)}) %all-to-all-start.1) | async-done | bytes 98336 | tf_op jit(solution)/shard_map/all_to_all | solution.py:312
  66.1 0.6 reshape.174
  (14 shorter events, 0.2 us)
Async XLA Ops:
  0.6 5.9 %copy-start.4 = (s32[1,4]{1,0:T(1,128)S(1)}, s32[1,4]{1,0:T(1,128)}, u32[]{:S(2)}) copy-start(s32[1,4]{1,0:T(1,128)} %param.12) | copy-start | bytes 52
  0.6 11.2 %copy-start.2 = (s32[4096]{0:T(1024)S(1)}, s32[4096]{0:T(1024)}, u32[]{:S(2)}) copy-start(s32[4096]{0:T(1024)} %param.11) | copy-start | bytes 49156
  0.7 11.4 %copy-start.3 = (bf16[2,1536]{1,0:T(2,128)(2,1)S(1)}, bf16[2,1536]{1,0:T(2,128)(2,1)}, u32[]{:S(2)}) copy-start(bf16[2,1536]{1,0:T(2,128)(2,1)} %param.10) | copy-start | bytes 18436
  0.7 13.2 %copy-start = (bf16[256,1536]{1,0:T(8,128)(2,1)S(1)}, bf16[256,1536]{1,0:T(8,128)(2,1)}, u32[]{:S(2)}) copy-start(bf16[256,1536]{1,0:T(8,128)(2,1)} %q_in.1) | copy-start | bytes 2359300
  0.7 13.2 %copy-start.1 = (bf16[256,1536]{1,0:T(8,128)(2,1)S(1)}, bf16[256,1536]{1,0:T(8,128)(2,1)}, u32[]{:S(2)}) copy-start(bf16[256,1536]{1,0:T(8,128)(2,1)} %g_in.1) | copy-start | bytes 2359300
  2.0 15.1 %collective-permute-start.1 = (bf16[256,1536]{1,0:T(8,128)(2,1)S(1)}, bf16[256,1536]{1,0:T(8,128)(2,1)S(1)}, u32[]{:S(2)}, u32[]{:S(2)}) collective-permute-start(bf16[256,1536]{1,0:T(8,128)(2,1)S(1)} %bitcast.9), channel_id=1, source_target_pairs={{1,2},{3,4},{5,6},{7,8},{9,10},{11,12},{13,14},{15,16},{17,18},{19... | collective-permute-start | bytes 2359304 | tf_op jit(solution)/shard_map/ppermute | solution.py:37
  6.8 7.0 %collective-permute-start = (bf16[256,1536]{1,0:T(8,128)(2,1)S(1)}, bf16[256,1536]{1,0:T(8,128)(2,1)}, u32[]{:S(2)}, u32[]{:S(2)}) collective-permute-start(bf16[256,1536]{1,0:T(8,128)(2,1)S(1)} %bitcast.10), channel_id=1, source_target_pairs={{0,1},{1,0},{2,3},{3,2},{4,5},{5,4},{6,7},{7,6},{8,9},{9,8},{10,11... | collective-permute-start | bytes 2359304 | tf_op jit(solution)/shard_map/ppermute | solution.py:31
  22.0 25.4 %all-to-all-start = ((bf16[32,24,128]{2,1,0:T(8,128)(2,1)}), bf16[32,24,128]{2,1,0:T(8,128)(2,1)S(1)}, u32[]{:S(2)}, u32[]{:S(2)}) async-start(bf16[32,24,128]{2,1,0:T(8,128)(2,1)} %bitcast.7), calls=%async_computation | async-start | bytes 393216 | tf_op jit(solution)/shard_map/all_to_all | solution.py:307
  35.7 21.9 %collective-permute-start.2 = (bf16[2,128,1536]{2,1,0:T(8,128)(2,1)}, bf16[2,128,1536]{2,1,0:T(8,128)(2,1)S(1)}, u32[]{:S(2)}, u32[]{:S(2)}) collective-permute-start(bf16[2,128,1536]{2,1,0:T(8,128)(2,1)} %get-tuple-element.44), channel_id=1, source_target_pairs={{1,2},{3,4},{5,6},{7,8},{9,10},{11,12},{13,14},{15,16},{17,18},{19... | collective-permute-start | bytes 2359304 | tf_op jit(solution)/shard_map/ppermute | solution.py:37
  48.0 10.0 %collective-permute-start.3 = (bf16[2,128,1536]{2,1,0:T(8,128)(2,1)S(1)}, bf16[2,128,1536]{2,1,0:T(8,128)(2,1)S(1)}, u32[]{:S(2)}, u32[]{:S(2)}) collective-permute-start(bf16[2,128,1536]{2,1,0:T(8,128)(2,1)S(1)} %get-tuple-element.45), channel_id=1, source_target_pairs={{0,1},{1,0},{2,3},{3,2},{4,5},{5,4},{6,7},{7,6},{8,9},{9,8},{10,11... | collective-permute-start | bytes 2359304 | tf_op jit(solution)/shard_map/ppermute | solution.py:31
  49.9 16.1 %all-to-all-start.1 = ((bf16[16,24,128]{2,1,0:T(8,128)(2,1)}), bf16[16,24,128]{2,1,0:T(8,128)(2,1)S(1)}, u32[]{:S(2)}, u32[]{:S(2)}) async-start(bf16[16,24,128]{2,1,0:T(8,128)(2,1)} %broadcast_in_dim.90), calls=%async_computation.1 | async-start | bytes 196608 | tf_op jit(solution)/shard_map/all_to_all | solution.py:312

commit v12 on v11

--- a/solution.py
+++ b/solution.py
@@ -230,17 +230,14 @@
     )(q, g, far, *near_parts, null_rows, null_flip, bias, valid)
 
 
-def add_kernel(a_ref, b_ref, *out_refs):
-    total = a_ref[...].astype(jnp.float32) + b_ref[...].astype(jnp.float32)
-    if len(out_refs) == 1:
-        out_refs[0][...] = total.astype(jnp.bfloat16)
-    else:
-        for i, ref in enumerate(out_refs):
-            ref[...] = total[i].astype(jnp.bfloat16)
-
-
-def add_call(a, b, split, work, name):
-    _, rows, width = a.shape
+def add_kernel(own_ref, far_ref, near_ref, *out_refs):
+    for i, ref in enumerate(out_refs):
+        total = own_ref[i].astype(jnp.float32) + far_ref[i].astype(jnp.float32)
+        ref[...] = (total + near_ref[i].astype(jnp.float32)).astype(jnp.bfloat16)
+
+
+def add_call(own, far, near):
+    _, rows, width = own.shape
     steps = 3
     both = pl.BlockSpec((2, rows, width // steps), lambda i: (0, 0, i))
     one = pl.BlockSpec((rows, width // steps), lambda i: (0, i))
@@ -248,13 +245,13 @@
     return pl.pallas_call(
         add_kernel,
         grid=(steps,),
-        in_specs=[both, both],
-        out_specs=[one, one] if split else both,
-        out_shape=[single, single] if split else jax.ShapeDtypeStruct(a.shape, jnp.bfloat16),
+        in_specs=[both] * 3,
+        out_specs=[one, one],
+        out_shape=[single, single],
         compiler_params=pltpu.CompilerParams(vmem_limit_bytes=ADD_LIMIT),
-        cost_estimate=pl.CostEstimate(flops=a.size, bytes_accessed=work, transcendentals=0),
-        name=name,
-    )(a, b)
+        cost_estimate=pl.CostEstimate(flops=2 * own.size, bytes_accessed=3_200_000, transcendentals=0),
+        name="add",
+    )(own, far, near)
 
 
 def sum_peers(parts):
@@ -310,9 +307,10 @@
     copies, near_grad = lax.optimization_barrier((copies, near_grad))
     near_back = swap_chip(near_grad)
     second = lax.all_to_all(copies, deep_axes, 0, 0)
-    part = add_call(own_grad, far_back, False, 4_000_000, "add_far")
-    grads = add_call(part, near_back, True, 2_400_000, "add_near")
-    second, *grads = lax.optimization_barrier((second, *grads))
+    second, own_grad, far_back, near_back = lax.optimization_barrier(
+        (second, own_grad, far_back, near_back)
+    )
+    grads = add_call(own_grad, far_back, near_back)
     null_grad = sum_peers(second).reshape(null_kv.shape)
     return (attended, query_grad, grads[0], grads[1], null_grad)
 

time: 67.1 us -> 67.8 us (1.010)
  blocking collectives: 0 us -> 15.9 us
  starting transfers between devices: 35.2 us -> 27.6 us
  waiting for transfers between devices: 16.4 us -> 9.96 us
    all_to_all x0 -> x1, blocking collectives: none -> 15.9 us  [body(): second = lax.all_to_all(copies, deep_axes, 0, 0)]
    all_to_all x1 -> x0, starting transfers between devices: 7.63 us -> none  [body(): second = lax.all_to_all(copies, deep_axes, 0, 0)]
    all_to_all x1 -> x0, waiting for transfers between devices: 6.48 us -> none  [body(): second = lax.all_to_all(copies, deep_axes, 0, 0)]
    pallas_call x2 -> x1, Pallas kernels: 1.98 us -> 1.63 us  [add_call(): pl.pallas_call(add_kernel, grid=(steps,), in_specs=[both] * 3, out_specs=...]
  transfers between devices with their start and end apart: 6 -> 5, of which waited for: 3 -> 2; matrix products, arithmetic and copies ran while one was open for 3% -> 2% of each run, Pallas kernels for 8% -> 5%
where the time goes in v12:
time: 67.8 us; the launch traced here: 67.5 us
  starting transfers between devices  27.6 us (41%)
  blocking collectives  15.9 us (23%)
  waiting for transfers between devices  9.96 us (15%)
  Pallas kernels  9.75 us (14%)
  other arithmetic  2.76 us (4%)
  between operations  0.88 us (1%)
  local copies, waits for them, and re-layouts  0.69 us (1%)
    all_to_all x1, blocking collectives, body(): second = lax.all_to_all(copies, deep_axes, 0, 0)  15.9 us
    all_to_all x1, starting transfers between devices, body(): lax.all_to_all(null_copies.reshape(-1, 2 * HEADS, HEAD), wide_axes, 0, 0)  13.7 us
    all_to_all x1, waiting for transfers between devices, body(): lax.all_to_all(null_copies.reshape(-1, 2 * HEADS, HEAD), wide_axes, 0, 0)  9.19 us
    ppermute x2, starting transfers between devices, swap_link(): return lax.ppermute(block, SEQ, pairs + [(b, a) for a, b in pairs])  6.92 us
    ppermute x2, starting transfers between devices, swap_chip(): return lax.ppermute(block, SEQ, [(i, i ^ 1) for i in range(count)])  6.9 us
    pallas_call x1, Pallas kernels, heads_call(): pl.pallas_call(heads_kernel, grid=(STEPS,), in_specs=[block(video_rows)]...  4.86 us
    pallas_call x1, Pallas kernels, prepare_call(): pl.pallas_call(prepare_kernel, grid=(STEPS,), in_specs=[block(video_rows)...  3.26 us
    pallas_call x1, Pallas kernels, add_call(): pl.pallas_call(add_kernel, grid=(steps,), in_specs=[both] * 3, out_specs=...  1.63 us
  transfers between devices with their start and end apart: 5, of which 2 were waited for; matrix products, arithmetic and copies ran while one was open for 2% of the time, Pallas kernels for 5%

profile of v12, /device:TPU:1, one launch (start us, length us, event | category | flops | bytes accessed | tf_op | source)
XLA Modules:
  0.0 67.5 jit_solution(17907357576007836470)
XLA Ops:
  0.6 0.0 copy-start.4
  0.6 0.0 copy-start.2
  0.7 0.0 copy-start.3
  0.7 0.0 copy-start
  0.7 0.0 copy-start.1
  0.7 1.3 %pad_maximum_fusion = bf16[2,128,1536]{2,1,0:T(8,128)(2,1)S(1)} fusion(bf16[1,128,1536]{2,1,0:T(8,128)(2,1)} %bitcast.13, bf16[1,128,1536]{2,1,0:T(8,128)(2,1)} %bitcast.14), kind=kLoop, calls=%fused_computation | loop fusion | flops 393216 | bytes 1572864 | tf_op jit(solution)/shard_map/stack | solution.py:268
  2.0 4.5 %collective-permute-start.1 = (bf16[256,1536]{1,0:T(8,128)(2,1)S(1)}, bf16[256,1536]{1,0:T(8,128)(2,1)S(1)}, u32[]{:S(2)}, u32[]{:S(2)}) collective-permute-start(bf16[256,1536]{1,0:T(8,128)(2,1)S(1)} %bitcast.9), channel_id=1, source_target_pairs={{1,2},{3,4},{5,6},{7,8},{9,10},{11,12},{13,14},{15,16},{17,18},{19... | collective-permute-start | bytes 2359304 | tf_op jit(solution)/shard_map/ppermute | solution.py:37
  6.5 0.0 copy-done.4
  6.5 0.2 reduce-window.4
  6.7 0.1 convert_reduce_fusion.2
  6.8 5.0 %collective-permute-start = (bf16[256,1536]{1,0:T(8,128)(2,1)S(1)}, bf16[256,1536]{1,0:T(8,128)(2,1)}, u32[]{:S(2)}, u32[]{:S(2)}) collective-permute-start(bf16[256,1536]{1,0:T(8,128)(2,1)S(1)} %bitcast.10), channel_id=1, source_target_pairs={{0,1},{1,0},{2,3},{3,2},{4,5},{5,4},{6,7},{7,6},{8,9},{9,8},{10,11... | collective-permute-start | bytes 2359304 | tf_op jit(solution)/shard_map/ppermute | solution.py:31
  11.9 0.0 copy-done.2
  11.9 0.1 pad_dynamic-slice_fusion.2
  12.0 0.1 convert_reduce_fusion.1
  12.1 0.0 copy-done.3
  12.1 0.1 broadcast_select_fusion.1.null_ref
  12.2 0.2 fusion
  12.5 0.1 add_select_fusion.bias_ref
  12.6 0.5 broadcast_select_fusion.null_flip
  13.1 0.8 %collective-permute-done.near_ref = bf16[256,1536]{1,0:T(8,128)(2,1)} collective-permute-done((bf16[256,1536]{1,0:T(8,128)(2,1)S(1)}, bf16[256,1536]{1,0:T(8,128)(2,1)}, u32[]{:S(2)}, u32[]{:S(2)}) %collective-permute-start) | collective-permute-done | bytes 786464 | tf_op jit(solution)/shard_map/ppermute | solution.py:31
  13.8 0.0 copy-done
  13.8 0.0 copy-done.1
  13.8 3.3 %prepare.1 = (bf16[256,1536]{1,0:T(8,128)(2,1)S(1)}, bf16[256,1536]{1,0:T(8,128)(2,1)S(1)}, bf16[1536,256]{1,0:T(8,128)(2,1)S(1)}, bf16[1536,256]{1,0:T(8,128)(2...) custom-call(bf16[256,1536]{1,0:T(8,128)(2,1)S(1)} %copy-done, ...), custom_call_target="tpu_custom_call" | custom-call | flops 603979776 | bytes 9000000 | tf_op jit(solution)/shard_map/prepare/pallas_call | solution.py:106
  17.1 0.0 collective-permute-done.1.far_ref
  17.1 4.9 %heads.1 = (bf16[256,1536]{1,0:T(8,128)(2,1)}, bf16[256,1536]{1,0:T(8,128)(2,1)}, bf16[2,128,1536]{2,1,0:T(8,128)(2,1)}, bf16[2,128,1536]{2,1,0:T(8,128)(2,1)S(1...) custom-call(bf16[256,1536]{1,0:T(8,128)(2,1)S(1)} %get-tuple-element.30.q_ref, ...), custom_call_target="tpu_custom_call" | custom-call | flops 679477248 | bytes 9000000 | tf_op jit(solution)/shard_map/heads/pallas_call | solution.py:210
  22.0 13.7 %all-to-all-start = ((bf16[32,24,128]{2,1,0:T(8,128)(2,1)}), bf16[32,24,128]{2,1,0:T(8,128)(2,1)S(1)}, u32[]{:S(2)}, u32[]{:S(2)}) async-start(bf16[32,24,128]{2,1,0:T(8,128)(2,1)} %bitcast.7), calls=%async_computation | async-start | bytes 393216 | tf_op jit(solution)/shard_map/all_to_all | solution.py:304
  35.7 2.4 %collective-permute-start.2 = (bf16[2,128,1536]{2,1,0:T(8,128)(2,1)}, bf16[2,128,1536]{2,1,0:T(8,128)(2,1)S(1)}, u32[]{:S(2)}, u32[]{:S(2)}) collective-permute-start(bf16[2,128,1536]{2,1,0:T(8,128)(2,1)} %get-tuple-element.45), channel_id=1, source_target_pairs={{1,2},{3,4},{5,6},{7,8},{9,10},{11,12},{13,14},{15,16},{17,18},{19... | collective-permute-start | bytes 2359304 | tf_op jit(solution)/shard_map/ppermute | solution.py:37
  38.1 9.2 %all-to-all-done = bf16[32,24,128]{2,1,0:T(8,128)(2,1)S(1)} async-done(((bf16[32,24,128]{2,1,0:T(8,128)(2,1)}), bf16[32,24,128]{2,1,0:T(8,128)(2,1)S(1)}, u32[]{:S(2)}, u32[]{:S(2)}) %all-to-all-start) | async-done | bytes 196640 | tf_op jit(solution)/shard_map/all_to_all | solution.py:304
  47.4 1.9 %collective-permute-start.3 = (bf16[2,128,1536]{2,1,0:T(8,128)(2,1)S(1)}, bf16[2,128,1536]{2,1,0:T(8,128)(2,1)S(1)}, u32[]{:S(2)}, u32[]{:S(2)}) collective-permute-start(bf16[2,128,1536]{2,1,0:T(8,128)(2,1)S(1)} %get-tuple-element.46), channel_id=1, source_target_pairs={{0,1},{1,0},{2,3},{3,2},{4,5},{5,4},{6,7},{7,6},{8,9},{9,8},{10,11... | collective-permute-start | bytes 2359304 | tf_op jit(solution)/shard_map/ppermute | solution.py:31
  49.3 15.9 %all_to_all.10 = bf16[16,24,128]{2,1,0:T(8,128)(2,1)S(1)} all-to-all(bf16[16,24,128]{2,1,0:T(8,128)(2,1)S(1)} %broadcast_in_dim.90), channel_id=1, replica_groups=mesh['yh'=2,'z'=8,'yl'=4,'x'=4,'core'=2] {'yh','yl','core'}, dimensions={0} | all-to-all | bytes 196608 | tf_op jit(solution)/shard_map/all_to_all | solution.py:309
  65.2 0.0 collective-permute-done.2.far_ref
  65.2 0.0 collective-permute-done.3.near_ref
  65.3 0.6 reshape.174
  65.9 1.6 %add.152 = (bf16[128,1536]{1,0:T(8,128)(2,1)}, bf16[128,1536]{1,0:T(8,128)(2,1)}) custom-call(bf16[2,128,1536]{2,1,0:T(8,128)(2,1)S(1)} %get-tuple-element.47.own_ref, bf16[2,128,1536]{2,1,0:T(8,128)(2,1)S(1)} %collective-permute-done.2.far_ref, bf16[2,128,1536]{2,1,0:T(8,128)(2,1)S(1)} %collective-permute-done.3.near_ref), custom_call_target="tpu_custom_call" | custom-call | flops 786432 | bytes 3200000 | tf_op jit(solution)/shard_map/add/pallas_call | solution.py:245
  (15 shorter events, 0.2 us)
Async XLA Ops:
  0.6 5.9 %copy-start.4 = (s32[1,4]{1,0:T(1,128)S(1)}, s32[1,4]{1,0:T(1,128)}, u32[]{:S(2)}) copy-start(s32[1,4]{1,0:T(1,128)} %param.12) | copy-start | bytes 52
  0.6 11.2 %copy-start.2 = (s32[4096]{0:T(1024)S(1)}, s32[4096]{0:T(1024)}, u32[]{:S(2)}) copy-start(s32[4096]{0:T(1024)} %param.11) | copy-start | bytes 49156
  0.7 11.4 %copy-start.3 = (bf16[2,1536]{1,0:T(2,128)(2,1)S(1)}, bf16[2,1536]{1,0:T(2,128)(2,1)}, u32[]{:S(2)}) copy-start(bf16[2,1536]{1,0:T(2,128)(2,1)} %param.10) | copy-start | bytes 18436
  0.7 13.2 %copy-start = (bf16[256,1536]{1,0:T(8,128)(2,1)S(1)}, bf16[256,1536]{1,0:T(8,128)(2,1)}, u32[]{:S(2)}) copy-start(bf16[256,1536]{1,0:T(8,128)(2,1)} %q_in.1) | copy-start | bytes 2359300
  0.7 13.2 %copy-start.1 = (bf16[256,1536]{1,0:T(8,128)(2,1)S(1)}, bf16[256,1536]{1,0:T(8,128)(2,1)}, u32[]{:S(2)}) copy-start(bf16[256,1536]{1,0:T(8,128)(2,1)} %g_in.1) | copy-start | bytes 2359300
  2.0 15.1 %collective-permute-start.1 = (bf16[256,1536]{1,0:T(8,128)(2,1)S(1)}, bf16[256,1536]{1,0:T(8,128)(2,1)S(1)}, u32[]{:S(2)}, u32[]{:S(2)}) collective-permute-start(bf16[256,1536]{1,0:T(8,128)(2,1)S(1)} %bitcast.9), channel_id=1, source_target_pairs={{1,2},{3,4},{5,6},{7,8},{9,10},{11,12},{13,14},{15,16},{17,18},{19... | collective-permute-start | bytes 2359304 | tf_op jit(solution)/shard_map/ppermute | solution.py:37
  6.8 7.0 %collective-permute-start = (bf16[256,1536]{1,0:T(8,128)(2,1)S(1)}, bf16[256,1536]{1,0:T(8,128)(2,1)}, u32[]{:S(2)}, u32[]{:S(2)}) collective-permute-start(bf16[256,1536]{1,0:T(8,128)(2,1)S(1)} %bitcast.10), channel_id=1, source_target_pairs={{0,1},{1,0},{2,3},{3,2},{4,5},{5,4},{6,7},{7,6},{8,9},{9,8},{10,11... | collective-permute-start | bytes 2359304 | tf_op jit(solution)/shard_map/ppermute | solution.py:31
  22.0 25.4 %all-to-all-start = ((bf16[32,24,128]{2,1,0:T(8,128)(2,1)}), bf16[32,24,128]{2,1,0:T(8,128)(2,1)S(1)}, u32[]{:S(2)}, u32[]{:S(2)}) async-start(bf16[32,24,128]{2,1,0:T(8,128)(2,1)} %bitcast.7), calls=%async_computation | async-start | bytes 393216 | tf_op jit(solution)/shard_map/all_to_all | solution.py:304
  35.7 29.5 %collective-permute-start.2 = (bf16[2,128,1536]{2,1,0:T(8,128)(2,1)}, bf16[2,128,1536]{2,1,0:T(8,128)(2,1)S(1)}, u32[]{:S(2)}, u32[]{:S(2)}) collective-permute-start(bf16[2,128,1536]{2,1,0:T(8,128)(2,1)} %get-tuple-element.45), channel_id=1, source_target_pairs={{1,2},{3,4},{5,6},{7,8},{9,10},{11,12},{13,14},{15,16},{17,18},{19... | collective-permute-start | bytes 2359304 | tf_op jit(solution)/shard_map/ppermute | solution.py:37
  47.4 17.8 %collective-permute-start.3 = (bf16[2,128,1536]{2,1,0:T(8,128)(2,1)S(1)}, bf16[2,128,1536]{2,1,0:T(8,128)(2,1)S(1)}, u32[]{:S(2)}, u32[]{:S(2)}) collective-permute-start(bf16[2,128,1536]{2,1,0:T(8,128)(2,1)S(1)} %get-tuple-element.46), channel_id=1, source_target_pairs={{0,1},{1,0},{2,3},{3,2},{4,5},{5,4},{6,7},{7,6},{8,9},{9,8},{10,11... | collective-permute-start | bytes 2359304 | tf_op jit(solution)/shard_map/ppermute | solution.py:31
